TPU v7x, 256 devices: a whole 4x4x8 slice. The times are simulated.
256 devices in a mesh: row: 16 (over z, y_lo), col: 16 (over x, y_hi, core).
Axes of the slice: x: 4, y: 4 (y_hi: 2, y_lo: 2; y = y_hi * 2 + y_lo), z: 8, core: 2. Of those that a mesh axis runs over, the one named last changes fastest.
Arguments:
- tensor: bfloat16 [2048, 64, 2048], P('row', None, 'col'), may hold values from -6 to 6
- loss_kind: int32 [2048, 64, 2048], P('row', None, 'col'), may hold values from 0 to 1, as said below
- factor_one: float32 [2048, 512], P(('row', 'col')), may hold values from -2 to 2
- factor_two: float32 [2048, 512], P(('col', 'row')), may hold values from -2 to 2
- factor_three: float32 [64, 512], replicated, may hold values from -2 to 2
- first_one: float32 [2048, 512], P(('row', 'col')), may hold values from -0.03 to 0.03
- second_one: float32 [2048, 512], P(('row', 'col')), may hold values from 0.0005 to 0.05
- first_two: float32 [2048, 512], P(('col', 'row')), may hold values from -0.03 to 0.03
- second_two: float32 [2048, 512], P(('col', 'row')), may hold values from 0.0005 to 0.05
- first_three: float32 [64, 512], replicated, may hold values from -0.03 to 0.03
- second_three: float32 [64, 512], replicated, may hold values from 0.0005 to 0.05
Outputs:
- new_one: float32 [2048, 512], P(('row', 'col'))
- new_two: float32 [2048, 512], P(('col', 'row'))
- new_three: float32 [64, 512], replicated
Inputs may be any that keep to these rules, and one draw needn't show every extreme that they name: loss_kind takes one value on each block of 128 first-mode by 128 second-mode indices (with all 64 third-mode ones), aligned to multiples of 128 and 128, and is 1 on exactly half of these blocks.
All inputs are finite; a program needn't handle non-finite values.
Results may differ from a plain program's by a relative error of at most 0.003.
Values may be sent and summed in bfloat16 or wider, within the bound.
No kernel may reach another device: no remote copies, remote signals or barrier semaphores. Data moves between devices by JAX's collectives and lax.ppermute only.
A program may use at most 128 MiB of HBM per device.

v0:
```python
import math

import jax
import jax.numpy as jnp
from jax import lax
from jax.sharding import PartitionSpec as P

ITERS = 2
STEP = 10


learn_rate = 0.05
beta_one = 0.8
beta_two = 0.95
adam_eps = 1e-08


def loss_slope(rebuilt, values, kinds):
    excess = rebuilt - values
    huber_part = jnp.clip(excess, -1.0, 1.0)
    target = jnp.where(values > 0, 1.0, 0.0).astype(rebuilt.dtype)
    logit_part = jax.nn.sigmoid(rebuilt) - target
    return jnp.where(kinds == 1, logit_part, huber_part)


def adam_step(param, first, second, grad, counter):
    first = beta_one * first + (1.0 - beta_one) * grad
    second = beta_two * second + (1.0 - beta_two) * grad * grad
    corr_one = 1.0 - beta_one**counter
    corr_two = 1.0 - beta_two**counter
    param = param - learn_rate * (first / corr_one) / (jnp.sqrt(second / corr_two) + adam_eps)
    return (param, first, second)


def tile_grads(tensor, loss_kind, half_one, half_two, half_three, scales):
    tile_rows, tile_depth, tile_cols = tensor.shape
    rank_width = half_one.shape[1]
    one_f = half_one.astype(jnp.float32)
    three_f = half_three.astype(jnp.float32)
    scaled_rows = (
        (one_f[:, None, :] * three_f[None, :, :])
        .astype(jnp.bfloat16)
        .reshape(tile_rows * tile_depth, rank_width)
    )
    rebuilt = lax.dot_general(
        scaled_rows, half_two, (((1,), (1,)), ((), ())), preferred_element_type=jnp.float32
    )
    values = tensor.reshape(tile_rows * tile_depth, tile_cols).astype(jnp.float32)
    deriv_bf = loss_slope(
        rebuilt, values, loss_kind.reshape(tile_rows * tile_depth, tile_cols)
    ).astype(jnp.bfloat16)
    projected = jnp.dot(deriv_bf, half_two, preferred_element_type=jnp.float32).reshape(
        tile_rows, tile_depth, rank_width
    )
    grad_one = jnp.sum(projected * three_f[None, :, :], axis=1) * scales[0]
    grad_three = jnp.sum(projected * one_f[:, None, :], axis=0) * scales[2]
    grad_two = (
        lax.dot_general(
            deriv_bf, scaled_rows, (((0,), (0,)), ((), ())), preferred_element_type=jnp.float32
        )
        * scales[1]
    )
    return (grad_one, grad_two, grad_three)


def third_sum(grad_three):
    return lax.psum(grad_three, ("row", "col"))


def shards(
    tensor,
    loss_kind,
    factor_one,
    factor_two,
    factor_three,
    first_one,
    second_one,
    first_two,
    second_two,
    first_three,
    second_three,
):
    tile_rows, tile_depth, tile_cols = tensor.shape
    full_rows = tile_rows * lax.axis_size("row")
    full_cols = tile_cols * lax.axis_size("col")
    scales = (
        1.0 / math.sqrt(full_cols * tile_depth),
        1.0 / math.sqrt(full_rows * tile_depth),
        1.0 / math.sqrt(full_rows * full_cols),
    )
    start_one, start_two, start_three = (factor_one, factor_two, factor_three)
    for iteration in range(ITERS):
        half_one = lax.all_gather(factor_one.astype(jnp.bfloat16), "col", axis=0, tiled=True)
        half_two = lax.all_gather(factor_two.astype(jnp.bfloat16), "row", axis=0, tiled=True)
        grad_one, grad_two, grad_three = tile_grads(
            tensor, loss_kind, half_one, half_two, factor_three.astype(jnp.bfloat16), scales
        )
        grad_one = lax.psum_scatter(grad_one, "col", scatter_dimension=0, tiled=True)
        grad_two = lax.psum_scatter(grad_two, "row", scatter_dimension=0, tiled=True)
        grad_three = third_sum(grad_three)
        counter = STEP + iteration + 1
        factor_one, first_one, second_one = adam_step(
            factor_one, first_one, second_one, grad_one, counter
        )
        factor_two, first_two, second_two = adam_step(
            factor_two, first_two, second_two, grad_two, counter
        )
        factor_three, first_three, second_three = adam_step(
            factor_three, first_three, second_three, grad_three, counter
        )
    spread = learn_rate * ITERS
    return (
        (start_one - factor_one) / spread,
        (start_two - factor_two) / spread,
        (start_three - factor_three) / spread,
    )


def solution(mesh):
    in_specs = (
        P("row", None, "col"),
        P("row", None, "col"),
        P(("row", "col"), None),
        P(("col", "row"), None),
        P(),
        P(("row", "col"), None),
        P(("row", "col"), None),
        P(("col", "row"), None),
        P(("col", "row"), None),
        P(),
        P(),
    )
    out_specs = (P(("row", "col"), None), P(("col", "row"), None), P())
    return jax.shard_map(shards, mesh=mesh, in_specs=in_specs, out_specs=out_specs, check_vma=False)
```

profile of v0, /device:TPU:1, one launch (start us, length us, event | category | flops | bytes accessed | tf_op | source)
XLA Modules:
  0.0 668.1 jit_solution(16243532245586999918)
XLA Ops:
  9.5 30.8 %all_gather.13 = bf16[128,512]{1,0:T(8,128)(2,1)S(1)} all-gather(bf16[8,512]{1,0:T(8,128)(2,1)S(1)} %convert_element_type.63), channel_id=1, replica_groups=mesh['row'=16,'col'=16] {'row'}, dimensions={0}, use_global_device_ids=true | all-gather | bytes 139264 | tf_op jit(solution)/shard_map/all_gather | solution.py:94
  40.3 31.9 %all_gather.12 = bf16[128,512]{1,0:T(8,128)(2,1)S(1)} all-gather(bf16[8,512]{1,0:T(8,128)(2,1)S(1)} %convert_element_type.57), channel_id=1, replica_groups=mesh['row'=16,'col'=16] {'col'}, dimensions={0}, use_global_device_ids=true | all-gather | bytes 139264 | tf_op jit(solution)/shard_map/all_gather | solution.py:93
  72.2 0.9 convert_convert_fusion
  73.2 2.8 broadcast_compare_fusion
  76.0 3.3 multiply_convert_fusion.1
  79.3 2.4 fusion.1
  81.7 0.8 copy-done
  82.5 8.1 %multiply_reduce_fusion.3 = (f32[128,512]{1,0:T(8,128)S(1)}, f32[8192,512]{1,0:T(8,128)}) fusion(f32[64,512]{1,0:T(8,128)S(1)} %convert_convert_fusion, bf16[8192,128]{1,0:T(8,128)(2,1)S(1)} %fusion.1, bf16[128,512]{1,0:T(8,128)(2,1)S(1)} %all_gather.13), kind=kOutput, calls=%fused_computation.4 | convolution fusion | flops 1082064896 | bytes 19398656 | tf_op jit(solution)/shard_map/dot_general | solution.py:52
  90.6 8.4 %multiply_reduce_fusion.2 = f32[64,512]{1,0:T(8,128)S(1)} fusion(f32[128,64,512]{2,1,0:T(8,128)} %bitcast.30, f32[128,512]{1,0:T(8,128)S(1)} %convert_element_type.58), kind=kLoop, calls=%fused_computation.3 | loop fusion | flops 8355840 | bytes 17170432 | tf_op jit(solution)/shard_map/reduce_sum | solution.py:56
  100.8 5.4 convolution_multiply_fusion.1
  106.3 226.4 %all-reduce.3.cloned.1.call-done = f32[64,512]{1,0:T(8,128)} async-done(((f32[64,512]{1,0:T(8,128)}), f32[64,512]{1,0:T(8,128)}) %all-reduce.3.cloned.1.call-update) | async-done | bytes 131088 | tf_op jit(solution)/shard_map/psum | solution.py:67
  332.7 1.0 fusion.16
  334.5 24.6 %all_gather.14 = bf16[128,512]{1,0:T(8,128)(2,1)S(1)} all-gather(bf16[8,512]{1,0:T(8,128)(2,1)S(1)} %fusion.35), channel_id=1, replica_groups=mesh['row'=16,'col'=16] {'col'}, dimensions={0}, use_global_device_ids=true | all-gather | bytes 139264 | tf_op jit(solution)/shard_map/all_gather | solution.py:93
  359.3 6.5 multiply_convert_fusion
  365.8 0.7 fusion.36
  366.5 23.4 %all_gather.15 = bf16[128,512]{1,0:T(8,128)(2,1)S(1)} all-gather(bf16[8,512]{1,0:T(8,128)(2,1)S(1)} %fusion.36), channel_id=1, replica_groups=mesh['row'=16,'col'=16] {'row'}, dimensions={0}, use_global_device_ids=true | all-gather | bytes 139264 | tf_op jit(solution)/shard_map/all_gather | solution.py:94
  389.9 6.7 fusion.3
  396.6 8.1 %multiply_reduce_fusion.1 = (f32[128,512]{1,0:T(8,128)S(1)}, f32[8192,512]{1,0:T(8,128)}) fusion(f32[64,512]{1,0:T(8,128)S(1)} %fusion.16, bf16[8192,128]{1,0:T(8,128)(2,1)S(1)} %fusion.3, bf16[128,512]{1,0:T(8,128)(2,1)S(1)} %all_gather.15), kind=kOutput, calls=%fused_computation.1 | convolution fusion | flops 1082064896 | bytes 19398656 | tf_op jit(solution)/shard_map/dot_general | solution.py:52
  404.7 8.4 %multiply_reduce_fusion = f32[64,512]{1,0:T(8,128)S(1)} fusion(f32[128,64,512]{2,1,0:T(8,128)} %bitcast.31, f32[128,512]{1,0:T(8,128)S(1)} %convert_element_type.68), kind=kLoop, calls=%fused_computation | loop fusion | flops 8355840 | bytes 17170432 | tf_op jit(solution)/shard_map/reduce_sum | solution.py:56
  414.7 5.4 convolution_multiply_fusion
  420.1 236.0 %all-reduce.5.cloned.1.call-done = f32[64,512]{1,0:T(8,128)} async-done(((f32[64,512]{1,0:T(8,128)}), f32[64,512]{1,0:T(8,128)}) %all-reduce.5.cloned.1.call-update) | async-done | bytes 131088 | tf_op jit(solution)/shard_map/psum | solution.py:67
  656.0 1.7 fusion.14
  657.8 1.4 fusion.34
  659.2 1.4 fusion.33
  (54 shorter events, 5.6 us)
Async XLA Ops:
  8.0 324.7 %all-reduce.3.cloned.1.call-start = ((), (), s32[]{:S(2)}) async-start(), calls=%async_computation.5 | async-start | bytes 262144 | tf_op jit(solution)/shard_map/psum | solution.py:67
  75.9 3.4 copy-start.2
  76.0 3.4 copy-start.14
  79.3 3.2 copy-start
  99.7 234.1 %reduce-scatter.5.cloned.1.call-start = ((), (), s32[]{:S(2)}) async-start(), calls=%async_computation.4 | async-start | bytes 278528 | tf_op jit(solution)/shard_map/reduce_scatter | solution.py:98
  100.5 232.2 %copy-start.1 = (f32[64,512]{1,0:T(8,128)S(1)}, f32[64,512]{1,0:T(8,128)}, u32[]{:S(2)}) copy-start(f32[64,512]{1,0:T(8,128)} %param.15) | copy-start | bytes 393220
  100.5 232.2 %copy-start.3 = (f32[64,512]{1,0:T(8,128)S(1)}, f32[64,512]{1,0:T(8,128)}, u32[]{:S(2)}) copy-start(f32[64,512]{1,0:T(8,128)} %param.20) | copy-start | bytes 393220
  100.5 232.2 %copy-start.4 = (f32[64,512]{1,0:T(8,128)S(1)}, f32[64,512]{1,0:T(8,128)}, u32[]{:S(2)}) copy-start(f32[64,512]{1,0:T(8,128)} %param.21) | copy-start | bytes 393220
  100.5 233.2 %copy-start.6 = (f32[8,512]{1,0:T(8,128)S(1)}, f32[8,512]{1,0:T(8,128)}, u32[]{:S(2)}) copy-start(f32[8,512]{1,0:T(8,128)} %param.13) | copy-start | bytes 49156
  100.6 233.2 %copy-start.8 = (f32[8,512]{1,0:T(8,128)S(1)}, f32[8,512]{1,0:T(8,128)}, u32[]{:S(2)}) copy-start(f32[8,512]{1,0:T(8,128)} %param.16) | copy-start | bytes 49156
  100.6 233.2 %copy-start.9 = (f32[8,512]{1,0:T(8,128)S(1)}, f32[8,512]{1,0:T(8,128)}, u32[]{:S(2)}) copy-start(f32[8,512]{1,0:T(8,128)} %param.17) | copy-start | bytes 49156
  100.6 265.2 %reduce-scatter.7.cloned.1.call-start = ((), (), s32[]{:S(2)}) async-start(), calls=%async_computation.6 | async-start | bytes 278528 | tf_op jit(solution)/shard_map/reduce_scatter | solution.py:99
  106.2 549.8 %all-reduce.5.cloned.1.call-start = ((), (), s32[]{:S(2)}) async-start(), calls=%async_computation.9 | async-start | bytes 262144 | tf_op jit(solution)/shard_map/psum | solution.py:67
  359.2 6.5 copy-start.7
  359.2 6.5 copy-start.10
  359.2 6.5 copy-start.11
  413.8 244.0 %reduce-scatter.9.cloned.1.call-start = ((), (), s32[]{:S(2)}) async-start(), calls=%async_computation.7 | async-start | bytes 278528 | tf_op jit(solution)/shard_map/reduce_scatter | solution.py:98
  414.6 241.5 %copy-start.5 = (f32[64,512]{1,0:T(8,128)S(1)}, f32[64,512]{1,0:T(8,128)}, u32[]{:S(2)}) copy-start(f32[64,512]{1,0:T(8,128)} %all-reduce.3.cloned.1.call-done) | copy-start | bytes 393220
  414.6 243.2 %copy-start.12 = (f32[8,512]{1,0:T(8,128)S(1)}, f32[8,512]{1,0:T(8,128)}, u32[]{:S(2)}) copy-start(f32[8,512]{1,0:T(8,128)} %reduce-scatter.5.cloned.1.call-done) | copy-start | bytes 49156
  414.6 244.6 %copy-start.13 = (f32[8,512]{1,0:T(8,128)S(1)}, f32[8,512]{1,0:T(8,128)}, u32[]{:S(2)}) copy-start(f32[8,512]{1,0:T(8,128)} %reduce-scatter.7.cloned.1.call-done) | copy-start | bytes 49156
  414.6 244.6 %reduce-scatter.11.cloned.1.call-start = ((), (), s32[]{:S(2)}) async-start(), calls=%async_computation.8 | async-start | bytes 278528 | tf_op jit(solution)/shard_map/reduce_scatter | solution.py:99
Sparse Core Ops, SparseCore 0:
  99.8 232.8 all-reduce.2
  413.9 242.0 all-reduce.4
Sparse Core Ops, SparseCore 1:
  104.2 62.8 reduce-scatter.4
  169.6 58.7 reduce-scatter.6
  418.3 72.0 reduce-scatter.8
  493.0 58.9 reduce-scatter.10
where the time goes:
time: 669 us; the launch traced here: 668 us
  waiting for transfers between devices  463 us (69%)
  blocking collectives  111 us (17%)
  other arithmetic  41.6 us (6%)
  matrix products  36 us (5%)
  between operations  15.9 us (2%)
    psum x2, waiting for transfers between devices, third_sum(): return lax.psum(grad_three, ('row', 'col'))  462 us
    all_gather x2, blocking collectives, shards(): lax.all_gather(factor_one.astype(jnp.bfloat16), 'col', axis=0, tiled=True)  56.5 us
    all_gather x2, blocking collectives, shards(): lax.all_gather(factor_two.astype(jnp.bfloat16), 'row', axis=0, tiled=True)  54.2 us
    reduce_sum x2, other arithmetic, tile_grads(): grad_three = jnp.sum(projected * one_f[:, None, :], axis=0) * scales[2]  16.8 us
    dot_general x2, matrix products, tile_grads(): jnp.dot(deriv_bf, half_two, preferred_element_type=jnp.float32)  16.1 us
  transfers between devices with their start and end apart: 6, of which 2 were waited for; matrix products, arithmetic and copies ran while one was open for 4% of the time, Pallas kernels for 0%

commit v1 on v0

v1 whole, which is shorter than its diff:
```python
import functools
import math

import jax
import jax.numpy as jnp
from jax import lax
from jax.experimental import pallas as pl
from jax.experimental.pallas import tpu as pltpu
from jax.sharding import PartitionSpec as P

ITERS = 2
STEP = 10
BLOCK = 8

learn_rate = 0.05
beta_one = 0.8
beta_two = 0.95
adam_eps = 1e-08

f32 = jnp.float32
bf16 = jnp.bfloat16


def adam_step(param, first, second, grad, counter):
    first = beta_one * first + (1.0 - beta_one) * grad
    second = beta_two * second + (1.0 - beta_two) * grad * grad
    corr_one = 1.0 - beta_one**counter
    corr_two = 1.0 - beta_two**counter
    param = param - learn_rate * (first / corr_one) / (jnp.sqrt(second / corr_two) + adam_eps)
    return (param, first, second)


def grads_kernel(scales, kind_ref, data_ref, one_ref, two_ref, three_ref, ga_ref, gb_ref, gc_ref, acc_b, acc_c):
    step = pl.program_id(0)
    depth, rank = three_ref.shape
    cols = two_ref.shape[0]

    @pl.when(step == 0)
    def _():
        acc_b[...] = jnp.zeros_like(acc_b)
        acc_c[...] = jnp.zeros_like(acc_c)

    one_f = one_ref[...].astype(f32)
    three_f = three_ref[...].astype(f32)
    two = two_ref[...]
    scaled = (one_f[:, None, :] * three_f[None, :, :]).astype(bf16).reshape(BLOCK * depth, rank)
    rebuilt = lax.dot_general(scaled, two, (((1,), (1,)), ((), ())), preferred_element_type=f32)
    values = data_ref[...].reshape(BLOCK * depth, cols).astype(f32)

    def finish(deriv):
        deriv = deriv.astype(bf16)
        proj = jnp.dot(deriv, two, preferred_element_type=f32).reshape(BLOCK, depth, rank)
        ga_ref[...] = (jnp.sum(proj * three_f[None], axis=1) * scales[0]).astype(ga_ref.dtype)
        acc_c[...] += jnp.sum(proj * one_f[:, None, :], axis=0)
        acc_b[...] += lax.dot_general(
            deriv, scaled, (((0,), (0,)), ((), ())), preferred_element_type=f32
        )

    logit = 0.5 * jnp.tanh(0.5 * rebuilt) + jnp.where(values > 0, -0.5, 0.5)
    huber = jnp.clip(rebuilt - values, -1.0, 1.0)
    finish(jnp.where(kind_ref[0] == 1, logit, huber))

    @pl.when(step == pl.num_programs(0) - 1)
    def _():
        gb_ref[...] = (acc_b[...] * scales[1]).astype(gb_ref.dtype)
        gc_ref[...] = (acc_c[...] * scales[2]).astype(gc_ref.dtype)


def tile_grads(kind, tensor, half_one, half_two, half_three, scales):
    rows, depth, cols = tensor.shape
    rank = half_one.shape[1]
    whole = lambda shape: pl.BlockSpec(shape, lambda i: (0,) * len(shape))
    return pl.pallas_call(
        functools.partial(grads_kernel, scales),
        grid=(rows // BLOCK,),
        in_specs=[
            pl.BlockSpec(memory_space=pltpu.SMEM),
            pl.BlockSpec((BLOCK, depth, cols), lambda i: (i, 0, 0)),
            pl.BlockSpec((BLOCK, rank), lambda i: (i, 0)),
            whole((cols, rank)),
            whole((depth, rank)),
        ],
        out_specs=[
            pl.BlockSpec((BLOCK, rank), lambda i: (i, 0)),
            whole((cols, rank)),
            whole((depth, rank)),
        ],
        out_shape=[
            jax.ShapeDtypeStruct((rows, rank), f32),
            jax.ShapeDtypeStruct((cols, rank), bf16),
            jax.ShapeDtypeStruct((depth, rank), bf16),
        ],
        scratch_shapes=[pltpu.VMEM((cols, rank), f32), pltpu.VMEM((depth, rank), f32)],
        compiler_params=pltpu.CompilerParams(vmem_limit_bytes=32 << 20),
        cost_estimate=pl.CostEstimate(
            flops=6 * rows * depth * cols * rank, bytes_accessed=4 << 20, transcendentals=rows * depth * cols
        ),
    )(kind, tensor, half_one, half_two, half_three)


def spread_out(part, axis):
    size = lax.axis_size(axis)
    return lax.all_to_all(jnp.broadcast_to(part[None], (size,) + part.shape), axis, 0, 0)


def swap_sum(parts, axis):
    return jnp.sum(lax.all_to_all(parts, axis, 0, 0).astype(f32), axis=0)


def shards(
    tensor, loss_kind, factor_one, factor_two, factor_three,
    first_one, second_one, first_two, second_two, first_three, second_three,
):
    tile_rows, tile_depth, tile_cols = tensor.shape
    n_row, n_col = lax.axis_size("row"), lax.axis_size("col")
    rank = factor_one.shape[1]
    own = factor_one.shape[0]
    own_two = factor_two.shape[0]
    own_three = tile_depth // n_col
    full_rows, full_cols = tile_rows * n_row, tile_cols * n_col
    scales = (
        1.0 / math.sqrt(full_cols * tile_depth),
        1.0 / math.sqrt(full_rows * tile_depth),
        1.0 / math.sqrt(full_rows * full_cols),
    )
    kind = loss_kind[0, 0, :1]
    place = lax.axis_index("col") * own_three
    mine = lambda x: lax.dynamic_slice_in_dim(x, place, own_three, 0)
    half_three = factor_three.astype(bf16)
    part_three, first_three, second_three = mine(factor_three), mine(first_three), mine(second_three)
    start_one, start_two, start_three = (factor_one, factor_two, part_three)
    half_one = spread_out(factor_one.astype(bf16), "col").reshape(tile_rows, rank)
    half_two = spread_out(factor_two.astype(bf16), "row").reshape(tile_cols, rank)
    for iteration in range(ITERS):
        grad_one, grad_two, grad_three = tile_grads(kind, tensor, half_one, half_two, half_three, scales)
        sent = jnp.concatenate(
            [grad_one.astype(bf16).reshape(n_col, own, rank), grad_three.reshape(n_col, own_three, rank)], axis=1
        )
        got = swap_sum(sent, "col")
        grad_one, grad_three = got[:own], got[own:]
        sent = jnp.concatenate(
            [
                grad_two.reshape(n_row, own_two, rank),
                jnp.broadcast_to(grad_three.astype(bf16)[None], (n_row, own_three, rank)),
            ],
            axis=1,
        )
        got = swap_sum(sent, "row")
        grad_two, grad_three = got[:own_two], got[own_two:]
        counter = STEP + iteration + 1
        factor_one, first_one, second_one = adam_step(factor_one, first_one, second_one, grad_one, counter)
        factor_two, first_two, second_two = adam_step(factor_two, first_two, second_two, grad_two, counter)
        part_three, first_three, second_three = adam_step(
            part_three, first_three, second_three, grad_three, counter
        )
        if iteration < ITERS - 1:
            halves = spread_out(jnp.concatenate([factor_one, part_three]).astype(bf16), "col")
            half_one = halves[:, :own].reshape(tile_rows, rank)
            half_three = halves[:, own:].reshape(tile_depth, rank)
            half_two = spread_out(factor_two.astype(bf16), "row").reshape(tile_cols, rank)
    spread = learn_rate * ITERS
    new_three = spread_out((start_three - part_three) / spread, "col").reshape(tile_depth, rank)
    return ((start_one - factor_one) / spread, (start_two - factor_two) / spread, new_three)


def solution(mesh):
    in_specs = (
        P("row", None, "col"),
        P("row", None, "col"),
        P(("row", "col"), None),
        P(("col", "row"), None),
        P(),
        P(("row", "col"), None),
        P(("row", "col"), None),
        P(("col", "row"), None),
        P(("col", "row"), None),
        P(),
        P(),
    )
    out_specs = (P(("row", "col"), None), P(("col", "row"), None), P())
    return jax.shard_map(shards, mesh=mesh, in_specs=in_specs, out_specs=out_specs, check_vma=False)
```

time: 669 us -> 168 us (0.25)
  waiting for transfers between devices: 463 us -> 60 us
  blocking collectives: 111 us -> 27.6 us
  starting transfers between devices: 0.44 us -> 38.2 us
  matrix products: 36 us -> 0 us
  other arithmetic: 41.6 us -> 7.04 us
  Pallas kernels: 0 us -> 26.3 us
  between operations: 15.9 us -> 0.88 us
    psum x2 -> x0, waiting for transfers between devices: 462 us -> none  [third_sum(): return lax.psum(grad_three, ('row', 'col'))]
    all_gather x4 -> x0, blocking collectives: 111 us -> none  [the longest x2 56.5 us: shards(): lax.all_gather(factor_one.astype(jnp.bfloat16), 'col', axis=0, tiled=True)]
    all_to_all x0 -> x7, waiting for transfers between devices: none -> 60 us  [the longest x5 38 us: spread_out(): lax.all_to_all(jnp.broadcast_to(part[None], (size,) + part.shape), axis,...]
    all_to_all x0 -> x7, starting transfers between devices: none -> 38.2 us  [the longest x5 31.1 us: spread_out(): lax.all_to_all(jnp.broadcast_to(part[None], (size,) + part.shape), axis,...]
    dot_general x6 -> x0, matrix products: 36 us -> none  [the longest x2 16.1 us: tile_grads(): jnp.dot(deriv_bf, half_two, preferred_element_type=jnp.float32)]
    all_to_all x0 -> x2, blocking collectives: none -> 27.6 us  [swap_sum(): return jnp.sum(lax.all_to_all(parts, axis, 0, 0).astype(f32), axis=0)]
    pallas_call x0 -> x2, Pallas kernels: none -> 26.3 us  [tile_grads(): pl.pallas_call(functools.partial(grads_kernel, scales), grid=(rows // BLO...]
    reduce_sum x2 -> x4, other arithmetic: 16.8 us -> 0.2 us  [swap_sum(): return jnp.sum(lax.all_to_all(parts, axis, 0, 0).astype(f32), axis=0)]
  transfers between devices with their start and end apart: 6 -> 7, of which waited for: 2 -> 7; matrix products, arithmetic and copies ran while one was open for 4% -> 3% of each run, Pallas kernels for 0% -> 0%
where the time goes in v1:
time: 168 us; the launch traced here: 167 us
  waiting for transfers between devices  60 us (36%)
  starting transfers between devices  38.2 us (23%)
  blocking collectives  27.6 us (16%)
  Pallas kernels  26.3 us (16%)
  local copies, waits for them, and re-layouts  7.07 us (4%)
  other arithmetic  7.04 us (4%)
    all_to_all x5, waiting for transfers between devices, spread_out(): lax.all_to_all(jnp.broadcast_to(part[None], (size,) + part.shape), axis,...  38 us
    all_to_all x5, starting transfers between devices, spread_out(): lax.all_to_all(jnp.broadcast_to(part[None], (size,) + part.shape), axis,...  31.1 us
    all_to_all x2, blocking collectives, swap_sum(): return jnp.sum(lax.all_to_all(parts, axis, 0, 0).astype(f32), axis=0)  27.6 us
    pallas_call x2, Pallas kernels, tile_grads(): pl.pallas_call(functools.partial(grads_kernel, scales), grid=(rows // BLO...  26.3 us
    all_to_all x2, waiting for transfers between devices, swap_sum(): return jnp.sum(lax.all_to_all(parts, axis, 0, 0).astype(f32), axis=0)  21.9 us
    all_to_all x2, starting transfers between devices, swap_sum(): return jnp.sum(lax.all_to_all(parts, axis, 0, 0).astype(f32), axis=0)  7.06 us
    broadcast_in_dim x5, local copies, waits for them, and re-layouts, spread_out(): jnp.broadcast_to(part[None], (size,) + part.shape)  3.39 us
  transfers between devices with their start and end apart: 7, of which 7 were waited for; matrix products, arithmetic and copies ran while one was open for 3% of the time, Pallas kernels for 0%

profile of v1, /device:TPU:1, one launch (start us, length us, event | category | flops | bytes accessed | tf_op | source)
XLA Modules:
  0.0 167.0 jit_solution(13504507809033601616)
XLA Ops:
  2.0 8.4 %all-to-all-start = ((bf16[16,8,512]{2,1,0:T(8,128)(2,1)}), bf16[16,8,512]{2,1,0:T(8,128)(2,1)S(1)}, u32[]{:S(2)}, u32[]{:S(2)}) async-start(bf16[16,8,512]{2,1,0:T(8,128)(2,1)} %broadcast_in_dim.14), calls=%async_computation | async-start | bytes 262144 | tf_op jit(solution)/shard_map/all_to_all | solution.py:103
  11.2 7.0 %all-to-all-done = bf16[16,8,512]{2,1,0:T(8,128)(2,1)S(1)} async-done(((bf16[16,8,512]{2,1,0:T(8,128)(2,1)}), bf16[16,8,512]{2,1,0:T(8,128)(2,1)S(1)}, u32[]{:S(2)}, u32[]{:S(2)}) %all-to-all-start) | async-done | bytes 131104 | tf_op jit(solution)/shard_map/all_to_all | solution.py:103
  18.8 8.4 %all-to-all-start.1 = ((bf16[16,8,512]{2,1,0:T(8,128)(2,1)}), bf16[16,8,512]{2,1,0:T(8,128)(2,1)S(1)}, u32[]{:S(2)}, u32[]{:S(2)}) async-start(bf16[16,8,512]{2,1,0:T(8,128)(2,1)} %broadcast_in_dim.15), calls=%async_computation.1 | async-start | bytes 262144 | tf_op jit(solution)/shard_map/all_to_all | solution.py:103
  27.2 1.2 slice.35
  28.4 0.9 convert_element_type.39.three_ref
  29.3 6.4 %all-to-all-done.1 = bf16[16,8,512]{2,1,0:T(8,128)(2,1)S(1)} async-done(((bf16[16,8,512]{2,1,0:T(8,128)(2,1)}), bf16[16,8,512]{2,1,0:T(8,128)(2,1)S(1)}, u32[]{:S(2)}, u32[]{:S(2)}) %all-to-all-start.1) | async-done | bytes 131104 | tf_op jit(solution)/shard_map/all_to_all | solution.py:103
  35.7 1.6 copy-done
  37.3 13.2 %shard_map.130 = (f32[128,512]{1,0:T(8,128)S(1)}, bf16[128,512]{1,0:T(8,128)(2,1)S(1)}, bf16[64,512]{1,0:T(8,128)(2,1)S(1)}) custom-call(s32[1]{0:T(128)} %bitcast.kind_ref, bf16[128,64,128]{2,1,0:T(8,128)(2,1)S(1)} %copy-done, bf16[128,512]{1,0:T(8,128)(2,1)S(1)} %bitcast.14, bf16[128,512]{1,0:T(8,128)(2,1)S(1)} %bitcast.16, ...), custom_call_target="tpu_custom_call" | custom-call | flops 3221225472 | bytes 4194304 | tf_op jit(solution)/shard_map/pallas_call | solution.py:73
  50.6 14.2 %all_to_all.45 = bf16[16,12,512]{2,1,0:T(8,128)(2,1)S(1)} all-to-all(bf16[16,12,512]{2,1,0:T(8,128)(2,1)S(1)} %pad_maximum_fusion), channel_id=1, replica_groups=mesh['row'=16,'col'=16] {'col'}, dimensions={0} | all-to-all | bytes 393216 | tf_op jit(solution)/shard_map/all_to_all | solution.py:107
  65.6 3.5 %all-to-all-start.3 = ((bf16[16,12,512]{2,1,0:T(8,128)(2,1)}), bf16[16,12,512]{2,1,0:T(8,128)(2,1)S(1)}, u32[]{:S(2)}, u32[]{:S(2)}) async-start(bf16[16,12,512]{2,1,0:T(8,128)(2,1)} %pad_maximum_fusion.1), calls=%async_computation.3 | async-start | bytes 524288 | tf_op jit(solution)/shard_map/all_to_all | solution.py:107
  69.2 11.2 %all-to-all-done.3 = bf16[16,12,512]{2,1,0:T(8,128)(2,1)S(1)} async-done(((bf16[16,12,512]{2,1,0:T(8,128)(2,1)}), bf16[16,12,512]{2,1,0:T(8,128)(2,1)S(1)}, u32[]{:S(2)}, u32[]{:S(2)}) %all-to-all-start.3) | async-done | bytes 196640 | tf_op jit(solution)/shard_map/all_to_all | solution.py:107
  80.5 0.8 fusion.26
  82.0 5.4 %all-to-all-start.4 = ((bf16[16,12,512]{2,1,0:T(8,128)(2,1)}), bf16[16,12,512]{2,1,0:T(8,128)(2,1)S(1)}, u32[]{:S(2)}, u32[]{:S(2)}) async-start(bf16[16,12,512]{2,1,0:T(8,128)(2,1)} %broadcast_in_dim.17), calls=%async_computation.4 | async-start | bytes 524288 | tf_op jit(solution)/shard_map/all_to_all | solution.py:103
  87.5 8.9 %all-to-all-done.4 = bf16[16,12,512]{2,1,0:T(8,128)(2,1)S(1)} async-done(((bf16[16,12,512]{2,1,0:T(8,128)(2,1)}), bf16[16,12,512]{2,1,0:T(8,128)(2,1)S(1)}, u32[]{:S(2)}, u32[]{:S(2)}) %all-to-all-start.4) | async-done | bytes 196640 | tf_op jit(solution)/shard_map/all_to_all | solution.py:103
  97.0 3.5 %all-to-all-start.5 = ((bf16[16,8,512]{2,1,0:T(8,128)(2,1)}), bf16[16,8,512]{2,1,0:T(8,128)(2,1)S(1)}, u32[]{:S(2)}, u32[]{:S(2)}) async-start(bf16[16,8,512]{2,1,0:T(8,128)(2,1)} %broadcast_in_dim.18), calls=%async_computation.5 | async-start | bytes 262144 | tf_op jit(solution)/shard_map/all_to_all | solution.py:103
  100.6 8.7 %all-to-all-done.5 = bf16[16,8,512]{2,1,0:T(8,128)(2,1)S(1)} async-done(((bf16[16,8,512]{2,1,0:T(8,128)(2,1)}), bf16[16,8,512]{2,1,0:T(8,128)(2,1)S(1)}, u32[]{:S(2)}, u32[]{:S(2)}) %all-to-all-start.5) | async-done | bytes 131104 | tf_op jit(solution)/shard_map/all_to_all | solution.py:103
  109.4 13.1 %shard_map.131 = (f32[128,512]{1,0:T(8,128)S(1)}, bf16[128,512]{1,0:T(8,128)(2,1)S(1)}, bf16[64,512]{1,0:T(8,128)(2,1)S(1)}) custom-call(s32[1]{0:T(128)} %bitcast.kind_ref, bf16[128,64,128]{2,1,0:T(8,128)(2,1)S(1)} %copy-done.1, bf16[128,512]{1,0:T(8,128)(2,1)S(1)} %slice_bitcast_fusion.one_ref, bf16[128,512]{1,0:T(8,128)(2,1)S(1)} %bitcast.15, ...), custom_call_target="tpu_custom_call" | custom-call | flops 3221225472 | bytes 4194304 | tf_op jit(solution)/shard_map/pallas_call | solution.py:73
  122.6 13.4 %all_to_all.46 = bf16[16,12,512]{2,1,0:T(8,128)(2,1)S(1)} all-to-all(bf16[16,12,512]{2,1,0:T(8,128)(2,1)S(1)} %pad_maximum_fusion.2), channel_id=1, replica_groups=mesh['row'=16,'col'=16] {'col'}, dimensions={0} | all-to-all | bytes 393216 | tf_op jit(solution)/shard_map/all_to_all | solution.py:107
  136.1 0.7 pad_maximum_fusion.3
  136.8 3.5 %all-to-all-start.7 = ((bf16[16,12,512]{2,1,0:T(8,128)(2,1)}), bf16[16,12,512]{2,1,0:T(8,128)(2,1)S(1)}, u32[]{:S(2)}, u32[]{:S(2)}) async-start(bf16[16,12,512]{2,1,0:T(8,128)(2,1)} %pad_maximum_fusion.3), calls=%async_computation.7 | async-start | bytes 524288 | tf_op jit(solution)/shard_map/all_to_all | solution.py:107
  141.0 10.7 %all-to-all-done.7 = bf16[16,12,512]{2,1,0:T(8,128)(2,1)S(1)} async-done(((bf16[16,12,512]{2,1,0:T(8,128)(2,1)}), bf16[16,12,512]{2,1,0:T(8,128)(2,1)S(1)}, u32[]{:S(2)}, u32[]{:S(2)}) %all-to-all-start.7) | async-done | bytes 196640 | tf_op jit(solution)/shard_map/all_to_all | solution.py:107
  151.7 0.8 subtract_multiply_fusion
  153.2 5.4 %all-to-all-start.8 = ((f32[16,4,512]{2,1,0:T(4,128)}), f32[16,4,512]{2,1,0:T(4,128)S(1)}, u32[]{:S(2)}, u32[]{:S(2)}) async-start(f32[16,4,512]{2,1,0:T(4,128)} %broadcast_in_dim.20), calls=%async_computation.8 | async-start | bytes 262144 | tf_op jit(solution)/shard_map/all_to_all | solution.py:103
  159.2 7.1 %all-to-all-done.8 = f32[16,4,512]{2,1,0:T(4,128)S(1)} async-done(((f32[16,4,512]{2,1,0:T(4,128)}), f32[16,4,512]{2,1,0:T(4,128)S(1)}, u32[]{:S(2)}, u32[]{:S(2)}) %all-to-all-start.8) | async-done | bytes 131104 | tf_op jit(solution)/shard_map/all_to_all | solution.py:103
  (46 shorter events, 8.1 us)
Async XLA Ops:
  2.0 16.1 %all-to-all-start = ((bf16[16,8,512]{2,1,0:T(8,128)(2,1)}), bf16[16,8,512]{2,1,0:T(8,128)(2,1)S(1)}, u32[]{:S(2)}, u32[]{:S(2)}) async-start(bf16[16,8,512]{2,1,0:T(8,128)(2,1)} %broadcast_in_dim.14), calls=%async_computation | async-start | bytes 262144 | tf_op jit(solution)/shard_map/all_to_all | solution.py:103
  18.8 16.9 %all-to-all-start.1 = ((bf16[16,8,512]{2,1,0:T(8,128)(2,1)}), bf16[16,8,512]{2,1,0:T(8,128)(2,1)S(1)}, u32[]{:S(2)}, u32[]{:S(2)}) async-start(bf16[16,8,512]{2,1,0:T(8,128)(2,1)} %broadcast_in_dim.15), calls=%async_computation.1 | async-start | bytes 262144 | tf_op jit(solution)/shard_map/all_to_all | solution.py:103
  35.7 1.6 copy-start
  37.3 31.8 %copy-start.2 = (f32[8,512]{1,0:T(8,128)S(1)}, f32[8,512]{1,0:T(8,128)}, u32[]{:S(2)}) copy-start(f32[8,512]{1,0:T(8,128)} %param.13) | copy-start | bytes 49156
  37.3 31.8 %copy-start.4 = (f32[8,512]{1,0:T(8,128)S(1)}, f32[8,512]{1,0:T(8,128)}, u32[]{:S(2)}) copy-start(f32[8,512]{1,0:T(8,128)} %param.16) | copy-start | bytes 49156
  37.3 31.9 %copy-start.5 = (f32[8,512]{1,0:T(8,128)S(1)}, f32[8,512]{1,0:T(8,128)}, u32[]{:S(2)}) copy-start(f32[8,512]{1,0:T(8,128)} %param.17) | copy-start | bytes 49156
  37.3 50.1 %copy-start.3 = (f32[8,512]{1,0:T(8,128)S(1)}, f32[8,512]{1,0:T(8,128)}, u32[]{:S(2)}) copy-start(f32[8,512]{1,0:T(8,128)} %param.14) | copy-start | bytes 49156
  37.3 50.1 %copy-start.6 = (f32[8,512]{1,0:T(8,128)S(1)}, f32[8,512]{1,0:T(8,128)}, u32[]{:S(2)}) copy-start(f32[8,512]{1,0:T(8,128)} %param.18) | copy-start | bytes 49156
  37.3 50.1 %copy-start.7 = (f32[8,512]{1,0:T(8,128)S(1)}, f32[8,512]{1,0:T(8,128)}, u32[]{:S(2)}) copy-start(f32[8,512]{1,0:T(8,128)} %param.19) | copy-start | bytes 49156
  50.5 58.9 %copy-start.1 = (bf16[128,64,128]{2,1,0:T(8,128)(2,1)S(1)}, bf16[128,64,128]{2,1,0:T(8,128)(2,1)}, u32[]{:S(2)}) copy-start(bf16[128,64,128]{2,1,0:T(8,128)(2,1)} %data_ref.3) | copy-start | bytes 6291460
  65.6 14.9 %all-to-all-start.3 = ((bf16[16,12,512]{2,1,0:T(8,128)(2,1)}), bf16[16,12,512]{2,1,0:T(8,128)(2,1)S(1)}, u32[]{:S(2)}, u32[]{:S(2)}) async-start(bf16[16,12,512]{2,1,0:T(8,128)(2,1)} %pad_maximum_fusion.1), calls=%async_computation.3 | async-start | bytes 524288 | tf_op jit(solution)/shard_map/all_to_all | solution.py:107
  82.0 14.4 %all-to-all-start.4 = ((bf16[16,12,512]{2,1,0:T(8,128)(2,1)}), bf16[16,12,512]{2,1,0:T(8,128)(2,1)S(1)}, u32[]{:S(2)}, u32[]{:S(2)}) async-start(bf16[16,12,512]{2,1,0:T(8,128)(2,1)} %broadcast_in_dim.17), calls=%async_computation.4 | async-start | bytes 524288 | tf_op jit(solution)/shard_map/all_to_all | solution.py:103
  97.0 12.3 %all-to-all-start.5 = ((bf16[16,8,512]{2,1,0:T(8,128)(2,1)}), bf16[16,8,512]{2,1,0:T(8,128)(2,1)S(1)}, u32[]{:S(2)}, u32[]{:S(2)}) async-start(bf16[16,8,512]{2,1,0:T(8,128)(2,1)} %broadcast_in_dim.18), calls=%async_computation.5 | async-start | bytes 262144 | tf_op jit(solution)/shard_map/all_to_all | solution.py:103
  136.8 14.9 %all-to-all-start.7 = ((bf16[16,12,512]{2,1,0:T(8,128)(2,1)}), bf16[16,12,512]{2,1,0:T(8,128)(2,1)S(1)}, u32[]{:S(2)}, u32[]{:S(2)}) async-start(bf16[16,12,512]{2,1,0:T(8,128)(2,1)} %pad_maximum_fusion.3), calls=%async_computation.7 | async-start | bytes 524288 | tf_op jit(solution)/shard_map/all_to_all | solution.py:107
  153.2 13.1 %all-to-all-start.8 = ((f32[16,4,512]{2,1,0:T(4,128)}), f32[16,4,512]{2,1,0:T(4,128)S(1)}, u32[]{:S(2)}, u32[]{:S(2)}) async-start(f32[16,4,512]{2,1,0:T(4,128)} %broadcast_in_dim.20), calls=%async_computation.8 | async-start | bytes 262144 | tf_op jit(solution)/shard_map/all_to_all | solution.py:103

commit v2 on v1

v2 whole, which is shorter than its diff:
```python
import functools
import math

import jax
import jax.numpy as jnp
from jax import lax
from jax.experimental import pallas as pl
from jax.experimental.pallas import tpu as pltpu
from jax.sharding import PartitionSpec as P

ITERS = 2
STEP = 10
BLOCK = 64
SUB = 4

learn_rate = 0.05
beta_one = 0.8
beta_two = 0.95
adam_eps = 1e-08

f32 = jnp.float32
bf16 = jnp.bfloat16

CORE, Y_HI, X_ONE = 1, 2, 4


def adam_step(param, first, second, grad, counter):
    first = beta_one * first + (1.0 - beta_one) * grad
    second = beta_two * second + (1.0 - beta_two) * grad * grad
    corr_one = 1.0 - beta_one**counter
    corr_two = 1.0 - beta_two**counter
    param = param - learn_rate * (first / corr_one) / (jnp.sqrt(second / corr_two) + adam_eps)
    return (param, first, second)


def piece_codes():
    return [y + x for y in (0, Y_HI) for x in (0, X_ONE, 2 * X_ONE, 3 * X_ONE)]


def slope_kernel(scales, with_three, ids_ref, data_ref, near_ref, far_ref, two_ref, three_ref,
                 sent_ref, slope_ref, one_ref, three_out_ref, ga_acc, gc_acc):
    step = pl.program_id(0)
    n_slab, own, rank = one_ref.shape
    depth = three_out_ref.shape[0] * three_out_ref.shape[1]
    cols = two_ref.shape[0]

    @pl.when(step == 0)
    def _():
        here = ids_ref[1]
        for place, code in enumerate(piece_codes()):
            slab = here ^ code
            one_ref[slab] = near_ref[place][:own]
            one_ref[slab ^ CORE] = far_ref[place][:own]
            if with_three:
                three_out_ref[slab // 2] = near_ref[place][own:]
        if not with_three:
            three_out_ref[...] = three_ref[...]
        gc_acc[...] = jnp.zeros_like(gc_acc)

    def run(logistic):
        two = two_ref[...]
        three = three_out_ref[...].reshape(depth, rank)
        three_f = three.astype(f32)
        slabs = BLOCK // own
        one = one_ref[pl.ds(step * slabs, slabs)].reshape(BLOCK, rank)
        n = BLOCK // SUB

        def rows(s):
            return slice(s * SUB, (s + 1) * SUB)

        def rebuild(s):
            scaled = (one[rows(s)][:, None, :] * three[None]).reshape(SUB * depth, rank)
            return lax.dot_general(scaled, two, (((1,), (1,)), ((), ())), preferred_element_type=f32)

        def slope(s, rebuilt):
            values = data_ref[rows(s)].reshape(SUB * depth, cols).astype(f32)
            if logistic:
                out = 0.5 * jnp.tanh(0.5 * rebuilt) + jnp.where(values > 0, -0.5, 0.5)
            else:
                out = jnp.clip(rebuilt - values, -1.0, 1.0)
            out = out.astype(bf16)
            slope_ref[rows(s)] = out.reshape(SUB, depth, cols)
            return out

        def project(deriv):
            return jnp.dot(deriv, two, preferred_element_type=f32).reshape(SUB, depth, rank)

        rebuilt, derivs, projs = {}, {}, {}
        grad_one, grad_three = [], None
        for t in range(n + 3):
            if t < n:
                rebuilt[t] = rebuild(t)
            if 0 <= t - 1 < n:
                derivs[t - 1] = slope(t - 1, rebuilt.pop(t - 1))
            if 0 <= t - 2 < n:
                projs[t - 2] = project(derivs.pop(t - 2))
            if 0 <= t - 3 < n:
                proj = projs.pop(t - 3)
                one_f = one[rows(t - 3)].astype(f32)
                grad_one.append(jnp.sum(proj * three_f[None], axis=1))
                part = jnp.sum(proj * one_f[:, None, :], axis=0)
                grad_three = part if grad_three is None else grad_three + part
        ga_acc[pl.ds(step * BLOCK, BLOCK)] = jnp.concatenate(grad_one)
        gc_acc[...] += grad_three

    pl.when(ids_ref[0] == 1)(lambda: run(True))
    pl.when(ids_ref[0] != 1)(lambda: run(False))

    @pl.when(step == pl.num_programs(0) - 1)
    def _():
        deep = three_out_ref.shape[1]
        for slab in range(n_slab):
            low = slab // 2 * deep
            sent_ref[slab] = jnp.concatenate(
                [ga_acc[slab * own:(slab + 1) * own] * scales[0], gc_acc[low:low + deep] * scales[2]]
            ).astype(bf16)


def slopes(ids, tensor, near, far, half_two, half_three, scales, with_three):
    rows, depth, cols = tensor.shape
    rank = half_two.shape[1]
    slabs, own = 2 * near.shape[0], rows // (2 * near.shape[0])
    deep = 2 * depth // slabs
    whole = lambda shape: pl.BlockSpec(shape, lambda i: (0,) * len(shape))
    return pl.pallas_call(
        functools.partial(slope_kernel, scales, with_three),
        grid=(rows // BLOCK,),
        in_specs=[
            pl.BlockSpec(memory_space=pltpu.SMEM),
            pl.BlockSpec((BLOCK, depth, cols), lambda i: (i, 0, 0)),
            whole(near.shape),
            whole(far.shape),
            whole((cols, rank)),
            whole(half_three.shape),
        ],
        out_specs=[
            whole((slabs, own + deep, rank)),
            pl.BlockSpec((BLOCK, depth, cols), lambda i: (i, 0, 0)),
            whole((slabs, own, rank)),
            whole((slabs // 2, deep, rank)),
        ],
        out_shape=[
            jax.ShapeDtypeStruct((slabs, own + deep, rank), bf16),
            jax.ShapeDtypeStruct((rows, depth, cols), bf16),
            jax.ShapeDtypeStruct((slabs, own, rank), bf16),
            jax.ShapeDtypeStruct((slabs // 2, deep, rank), bf16),
        ],
        scratch_shapes=[pltpu.VMEM((rows, rank), f32), pltpu.VMEM((depth, rank), f32)],
        compiler_params=pltpu.CompilerParams(vmem_limit_bytes=48 << 20),
        cost_estimate=pl.CostEstimate(
            flops=8 * rows * depth * cols * rank, bytes_accessed=4 << 20, transcendentals=rows * depth * cols
        ),
    )(ids, tensor, near, far, half_two, half_three)


def second_kernel(scale, slope_ref, one_ref, three_ref, out_ref, acc):
    step = pl.program_id(0)
    block, depth, cols = slope_ref.shape
    rank = one_ref.shape[2]
    one = one_ref[...].reshape(block, rank)
    three = three_ref[...].reshape(depth, rank)
    scaled = (one[:, None, :] * three[None]).reshape(block * depth, rank)
    part = lax.dot_general(
        slope_ref[...].reshape(block * depth, cols), scaled, (((0,), (0,)), ((), ())), preferred_element_type=f32
    )

    @pl.when(step == 0)
    def _():
        acc[...] = part

    @pl.when(step != 0)
    def _():
        acc[...] += part

    @pl.when(step == pl.num_programs(0) - 1)
    def _():
        out_ref[...] = (acc[...] * scale).astype(bf16)


def second_grad(slope, ones, threes, scale):
    rows, depth, cols = slope.shape
    slabs, own, rank = ones.shape
    block = 32
    return pl.pallas_call(
        functools.partial(second_kernel, scale),
        grid=(rows // block,),
        in_specs=[
            pl.BlockSpec((block, depth, cols), lambda i: (i, 0, 0)),
            pl.BlockSpec((block // own, own, rank), lambda i: (i, 0, 0)),
            pl.BlockSpec(threes.shape, lambda i: (0, 0, 0)),
        ],
        out_specs=pl.BlockSpec((cols, rank), lambda i: (0, 0)),
        out_shape=jax.ShapeDtypeStruct((cols, rank), bf16),
        scratch_shapes=[pltpu.VMEM((cols, rank), f32)],
        compiler_params=pltpu.CompilerParams(vmem_limit_bytes=32 << 20),
        cost_estimate=pl.CostEstimate(
            flops=4 * rows * depth * cols * rank, bytes_accessed=2 << 20, transcendentals=0
        ),
    )(slope, ones, threes)


def spread_out(part, axis, groups=None):
    size = lax.axis_size(axis) if groups is None else len(groups[0])
    whole = jnp.broadcast_to(part[None], (size,) + part.shape)
    return lax.all_to_all(whole, axis, 0, 0, axis_index_groups=groups)


def swap_sum(parts, axis):
    return jnp.sum(lax.all_to_all(parts, axis, 0, 0).astype(f32), axis=0)


def swap(part, code):
    size = lax.axis_size("col")
    return lax.ppermute(part, "col", [(i, i ^ code) for i in range(size)])


def gather_col(part):
    pieces = [part] + [swap(part, m * X_ONE) for m in (1, 2, 3)]
    half = jnp.stack(pieces)
    near = jnp.concatenate([half, swap(half, Y_HI)])
    return near, swap(near, CORE)


def shards(
    tensor, loss_kind, factor_one, factor_two, factor_three,
    first_one, second_one, first_two, second_two, first_three, second_three,
):
    tile_rows, tile_depth, tile_cols = tensor.shape
    n_row, n_col = lax.axis_size("row"), lax.axis_size("col")
    rank = factor_one.shape[1]
    own, own_two = factor_one.shape[0], factor_two.shape[0]
    deep = 2 * tile_depth // n_col
    full_rows, full_cols = tile_rows * n_row, tile_cols * n_col
    scales = (
        1.0 / math.sqrt(full_cols * tile_depth),
        1.0 / math.sqrt(full_rows * tile_depth),
        1.0 / math.sqrt(full_rows * full_cols),
    )
    here = lax.axis_index("col")
    ids = jnp.stack([loss_kind[0, 0, 0], here.astype(jnp.int32)])
    mine = lambda x: lax.dynamic_slice_in_dim(x, here // 2 * deep, deep, 0)
    half_three = factor_three.astype(bf16).reshape(n_col // 2, deep, rank)
    part_three, first_three, second_three = mine(factor_three), mine(first_three), mine(second_three)
    start_one, start_two, start_three = (factor_one, factor_two, part_three)
    half_two = spread_out(factor_two.astype(bf16), "row").reshape(tile_cols, rank)
    near, far = gather_col(factor_one.astype(bf16))
    for iteration in range(ITERS):
        sent, slope, ones, threes = slopes(
            ids, tensor, near, far, half_two, half_three, scales, iteration > 0
        )
        grad_two = second_grad(slope, ones, threes, scales[1])
        got = swap_sum(sent, "col")
        grad_one, grad_three = got[:own], got[own:]
        sent = jnp.concatenate(
            [
                grad_two.reshape(n_row, own_two, rank),
                jnp.broadcast_to(grad_three.astype(bf16)[None], (n_row, deep, rank)),
            ],
            axis=1,
        )
        got = swap_sum(sent, "row")
        grad_two, grad_three = got[:own_two], got[own_two:]
        counter = STEP + iteration + 1
        factor_one, first_one, second_one = adam_step(factor_one, first_one, second_one, grad_one, counter)
        factor_two, first_two, second_two = adam_step(factor_two, first_two, second_two, grad_two, counter)
        part_three, first_three, second_three = adam_step(
            part_three, first_three, second_three, grad_three, counter
        )
        if iteration < ITERS - 1:
            half_two = spread_out(factor_two.astype(bf16), "row").reshape(tile_cols, rank)
            near, far = gather_col(jnp.concatenate([factor_one, part_three]).astype(bf16))
            half_three = threes
    spread = learn_rate * ITERS
    chips = [[c for c in range(core, n_col, 2)] for core in range(2)]
    new_three = spread_out((start_three - part_three) / spread, "col", chips).reshape(tile_depth, rank)
    return ((start_one - factor_one) / spread, (start_two - factor_two) / spread, new_three)


def solution(mesh):
    in_specs = (
        P("row", None, "col"),
        P("row", None, "col"),
        P(("row", "col"), None),
        P(("col", "row"), None),
        P(),
        P(("row", "col"), None),
        P(("row", "col"), None),
        P(("col", "row"), None),
        P(("col", "row"), None),
        P(),
        P(),
    )
    out_specs = (P(("row", "col"), None), P(("col", "row"), None), P())
    return jax.shard_map(shards, mesh=mesh, in_specs=in_specs, out_specs=out_specs, check_vma=False)
```

time: 168 us -> 142 us (0.85)
  waiting for transfers between devices: 60 us -> 35.2 us
  starting transfers between devices: 38.2 us -> 55.2 us
  blocking collectives: 27.6 us -> 15.9 us
  Pallas kernels: 26.3 us -> 16.9 us
    all_to_all x5 -> x3, waiting for transfers between devices: 38 us -> 6.14 us  [spread_out(): return lax.all_to_all(whole, axis, 0, 0, axis_index_groups=groups)]
    ppermute x0 -> x10, starting transfers between devices: none -> 18.4 us  [swap(): return lax.ppermute(part, 'col', [(i, i ^ code) for i in range(size)])]
    all_to_all x5 -> x3, starting transfers between devices: 31.1 us -> 16.5 us  [spread_out(): return lax.all_to_all(whole, axis, 0, 0, axis_index_groups=groups)]
    all_to_all x2 -> x3, starting transfers between devices: 7.06 us -> 20.4 us  [swap_sum(): return jnp.sum(lax.all_to_all(parts, axis, 0, 0).astype(f32), axis=0)]
    all_to_all x2 -> x1, blocking collectives: 27.6 us -> 15.9 us  [swap_sum(): return jnp.sum(lax.all_to_all(parts, axis, 0, 0).astype(f32), axis=0)]
    pallas_call x2 -> x4, Pallas kernels: 26.3 us -> 16.9 us  [the longest x2 12.8 us: slopes(): pl.pallas_call(functools.partial(slope_kernel, scales, with_three), grid=...]
    ppermute x0 -> x10, waiting for transfers between devices: none -> 6.13 us  [swap(): return lax.ppermute(part, 'col', [(i, i ^ code) for i in range(size)])]
    unnamed x16 -> x27, local copies, waits for them, and re-layouts: 1.62 us -> 5.22 us
  transfers between devices with their start and end apart: 7 -> 16, of which waited for: 7 -> 8; matrix products, arithmetic and copies ran while one was open for 3% -> 4% of each run, Pallas kernels for 0% -> 3%
where the time goes in v2:
time: 142 us; the launch traced here: 140 us
  starting transfers between devices  55.2 us (39%)
  waiting for transfers between devices  35.2 us (25%)
  Pallas kernels  16.9 us (12%)
  blocking collectives  15.9 us (11%)
  local copies, waits for them, and re-layouts  8.45 us (6%)
  other arithmetic  6.88 us (5%)
    all_to_all x3, waiting for transfers between devices, swap_sum(): return jnp.sum(lax.all_to_all(parts, axis, 0, 0).astype(f32), axis=0)  23 us
    all_to_all x3, starting transfers between devices, swap_sum(): return jnp.sum(lax.all_to_all(parts, axis, 0, 0).astype(f32), axis=0)  20.4 us
    ppermute x10, starting transfers between devices, swap(): return lax.ppermute(part, 'col', [(i, i ^ code) for i in range(size)])  18.4 us
    all_to_all x3, starting transfers between devices, spread_out(): return lax.all_to_all(whole, axis, 0, 0, axis_index_groups=groups)  16.5 us
    all_to_all x1, blocking collectives, swap_sum(): return jnp.sum(lax.all_to_all(parts, axis, 0, 0).astype(f32), axis=0)  15.9 us
    pallas_call x2, Pallas kernels, slopes(): pl.pallas_call(functools.partial(slope_kernel, scales, with_three), grid=...  12.8 us
    all_to_all x3, waiting for transfers between devices, spread_out(): return lax.all_to_all(whole, axis, 0, 0, axis_index_groups=groups)  6.14 us
    ppermute x10, waiting for transfers between devices, swap(): return lax.ppermute(part, 'col', [(i, i ^ code) for i in range(size)])  6.13 us
  transfers between devices with their start and end apart: 16, of which 8 were waited for; matrix products, arithmetic and copies ran while one was open for 4% of the time, Pallas kernels for 3%

profile of v2, /device:TPU:1, one launch (start us, length us, event | category | flops | bytes accessed | tf_op | source)
XLA Modules:
  0.0 139.6 jit_solution(7980629038424194673)
XLA Ops:
  1.4 3.3 %collective-permute-start.2 = (bf16[8,512]{1,0:T(8,128)(2,1)S(1)}, bf16[8,512]{1,0:T(8,128)(2,1)S(1)}, u32[]{:S(2)}, u32[]{:S(2)}) collective-permute-start(bf16[8,512]{1,0:T(8,128)(2,1)S(1)} %get-tuple-element.22), channel_id=1, source_target_pairs={{0,12},{1,13},{2,14},{3,15},{4,8},{5,9},{6,10},{7,11},{8,4},{9,5},... | collective-permute-start | bytes 24584 | tf_op jit(solution)/shard_map/ppermute | solution.py:214
  6.6 9.5 %all-to-all-start = ((bf16[16,8,512]{2,1,0:T(8,128)(2,1)}), bf16[16,8,512]{2,1,0:T(8,128)(2,1)S(1)}, u32[]{:S(2)}, u32[]{:S(2)}) async-start(bf16[16,8,512]{2,1,0:T(8,128)(2,1)} %broadcast_in_dim.10), calls=%async_computation | async-start | bytes 262144 | tf_op jit(solution)/shard_map/all_to_all | solution.py:205
  18.3 2.7 %collective-permute-start.3 = (bf16[4,8,512]{2,1,0:T(8,128)(2,1)S(1)}, bf16[4,8,512]{2,1,0:T(8,128)(2,1)S(1)}, u32[]{:S(2)}, u32[]{:S(2)}) collective-permute-start(bf16[4,8,512]{2,1,0:T(8,128)(2,1)S(1)} %pad_maximum_fusion.3), channel_id=1, source_target_pairs={{0,2},{1,3},{2,0},{3,1},{4,6},{5,7},{6,4},{7,5},{8,10},{9,11},{10,... | collective-permute-start | bytes 98312 | tf_op jit(solution)/shard_map/ppermute | solution.py:214
  21.0 1.8 %collective-permute-done.3 = bf16[4,8,512]{2,1,0:T(8,128)(2,1)S(1)} collective-permute-done((bf16[4,8,512]{2,1,0:T(8,128)(2,1)S(1)}, bf16[4,8,512]{2,1,0:T(8,128)(2,1)S(1)}, u32[]{:S(2)}, u32[]{:S(2)}) %collective-permute-start.3) | collective-permute-done | bytes 32800 | tf_op jit(solution)/shard_map/ppermute | solution.py:214
  22.8 2.9 %collective-permute-start.4 = (bf16[8,8,512]{2,1,0:T(8,128)(2,1)S(1)}, bf16[8,8,512]{2,1,0:T(8,128)(2,1)S(1)}, u32[]{:S(2)}, u32[]{:S(2)}) collective-permute-start(bf16[8,8,512]{2,1,0:T(8,128)(2,1)S(1)} %constant_dynamic-update-slice_fusion.near_ref), channel_id=1, source_target_pairs={{0,1},{1,0},{2,3},{3,2},{4,5},{5,4},{6,7},{7,6},{8,9},{9,8},{10,11... | collective-permute-start | bytes 196616 | tf_op jit(solution)/shard_map/ppermute | solution.py:214
  26.6 1.6 %copy-done = bf16[128,64,128]{2,1,0:T(8,128)(2,1)S(1)} copy-done((bf16[128,64,128]{2,1,0:T(8,128)(2,1)S(1)}, bf16[128,64,128]{2,1,0:T(8,128)(2,1)}, u32[]{:S(2)}) %copy-start) | copy-done | bytes 2097176
  28.2 6.4 %shard_map.130 = (bf16[16,16,512]{2,1,0:T(8,128)(2,1)}, bf16[128,64,128]{2,1,0:T(8,128)(2,1)S(1)}, bf16[16,8,512]{2,1,0:T(8,128)(2,1)S(1)}, bf16[8,8,512]{2,1,0:T(8,128)(2,1)S(1)}) custom-call(s32[2]{0:T(128)S(1)} %pad_add_fusion.ids_ref, bf16[128,64,128]{2,1,0:T(8,128)(2,1)S(1)} %copy-done, ...), custom_call_target="tpu_custom_call" | custom-call | flops 4294967296 | bytes 4194304 | tf_op jit(solution)/shard_map/pallas_call | solution.py:125
  34.6 7.6 %all-to-all-start.1 = ((bf16[16,16,512]{2,1,0:T(8,128)(2,1)}), bf16[16,16,512]{2,1,0:T(8,128)(2,1)S(1)}, u32[]{:S(2)}, u32[]{:S(2)}) async-start(bf16[16,16,512]{2,1,0:T(8,128)(2,1)} %get-tuple-element.11), calls=%async_computation.1 | async-start | bytes 524288 | tf_op jit(solution)/shard_map/all_to_all | solution.py:209
  42.3 2.1 %shard_map.131 = bf16[128,512]{1,0:T(8,128)(2,1)S(1)} custom-call(bf16[128,64,128]{2,1,0:T(8,128)(2,1)S(1)} %get-tuple-element.12.slope_ref, bf16[16,8,512]{2,1,0:T(8,128)(2,1)S(1)} %get-tuple-element.13.one_ref, bf16[8,8,512]{2,1,0:T(8,128)(2,1)S(1)} %get-tuple-element.14.three_ref), custom_call_target="tpu_custom_call" | custom-call | flops 2147483648 | bytes 2097152 | tf_op jit(solution)/shard_map/pallas_call | solution.py:184
  44.4 6.8 %all-to-all-done.1 = bf16[16,16,512]{2,1,0:T(8,128)(2,1)S(1)} async-done(((bf16[16,16,512]{2,1,0:T(8,128)(2,1)}), bf16[16,16,512]{2,1,0:T(8,128)(2,1)S(1)}, u32[]{:S(2)}, u32[]{:S(2)}) %all-to-all-start.1) | async-done | bytes 262176 | tf_op jit(solution)/shard_map/all_to_all | solution.py:209
  52.0 6.5 %all-to-all-start.2 = ((bf16[16,16,512]{2,1,0:T(8,128)(2,1)}), bf16[16,16,512]{2,1,0:T(8,128)(2,1)S(1)}, u32[]{:S(2)}, u32[]{:S(2)}) async-start(bf16[16,16,512]{2,1,0:T(8,128)(2,1)} %pad_maximum_fusion), calls=%async_computation.2 | async-start | bytes 524288 | tf_op jit(solution)/shard_map/all_to_all | solution.py:209
  58.5 10.9 %all-to-all-done.2 = bf16[16,16,512]{2,1,0:T(8,128)(2,1)S(1)} async-done(((bf16[16,16,512]{2,1,0:T(8,128)(2,1)}), bf16[16,16,512]{2,1,0:T(8,128)(2,1)S(1)}, u32[]{:S(2)}, u32[]{:S(2)}) %all-to-all-start.2) | async-done | bytes 262176 | tf_op jit(solution)/shard_map/all_to_all | solution.py:209
  70.7 2.2 %collective-permute-start.6 = (bf16[16,512]{1,0:T(8,128)(2,1)S(1)}, bf16[16,512]{1,0:T(8,128)(2,1)S(1)}, u32[]{:S(2)}, u32[]{:S(2)}) collective-permute-start(bf16[16,512]{1,0:T(8,128)(2,1)S(1)} %pad_maximum_fusion.4), channel_id=1, source_target_pairs={{0,8},{1,9},{2,10},{3,11},{4,12},{5,13},{6,14},{7,15},{8,0},{9,1},... | collective-permute-start | bytes 49160 | tf_op jit(solution)/shard_map/ppermute | solution.py:214
  74.3 3.5 %all-to-all-start.3 = ((bf16[16,8,512]{2,1,0:T(8,128)(2,1)}), bf16[16,8,512]{2,1,0:T(8,128)(2,1)S(1)}, u32[]{:S(2)}, u32[]{:S(2)}) async-start(bf16[16,8,512]{2,1,0:T(8,128)(2,1)} %broadcast_in_dim.12), calls=%async_computation.3 | async-start | bytes 262144 | tf_op jit(solution)/shard_map/all_to_all | solution.py:205
  77.9 1.6 %collective-permute-start.8 = (bf16[4,16,512]{2,1,0:T(8,128)(2,1)S(1)}, bf16[4,16,512]{2,1,0:T(8,128)(2,1)S(1)}, u32[]{:S(2)}, u32[]{:S(2)}) collective-permute-start(bf16[4,16,512]{2,1,0:T(8,128)(2,1)S(1)} %pad_maximum_fusion.2), channel_id=1, source_target_pairs={{0,2},{1,3},{2,0},{3,1},{4,6},{5,7},{6,4},{7,5},{8,10},{9,11},{10,... | collective-permute-start | bytes 196616 | tf_op jit(solution)/shard_map/ppermute | solution.py:214
  79.5 3.2 %collective-permute-done.8 = bf16[4,16,512]{2,1,0:T(8,128)(2,1)S(1)} collective-permute-done((bf16[4,16,512]{2,1,0:T(8,128)(2,1)S(1)}, bf16[4,16,512]{2,1,0:T(8,128)(2,1)S(1)}, u32[]{:S(2)}, u32[]{:S(2)}) %collective-permute-start.8) | collective-permute-done | bytes 65568 | tf_op jit(solution)/shard_map/ppermute | solution.py:214
  82.7 3.9 %collective-permute-start.9 = (bf16[8,16,512]{2,1,0:T(8,128)(2,1)S(1)}, bf16[8,16,512]{2,1,0:T(8,128)(2,1)S(1)}, u32[]{:S(2)}, u32[]{:S(2)}) collective-permute-start(bf16[8,16,512]{2,1,0:T(8,128)(2,1)S(1)} %constant_dynamic-update-slice_fusion.5.near_ref), channel_id=1, source_target_pairs={{0,1},{1,0},{2,3},{3,2},{4,5},{5,4},{6,7},{7,6},{8,9},{9,8},{10,11... | collective-permute-start | bytes 393224 | tf_op jit(solution)/shard_map/ppermute | solution.py:214
  87.6 6.4 %shard_map.132 = (bf16[16,16,512]{2,1,0:T(8,128)(2,1)}, bf16[128,64,128]{2,1,0:T(8,128)(2,1)S(1)}, bf16[16,8,512]{2,1,0:T(8,128)(2,1)S(1)}, bf16[8,8,512]{2,1,0:T(8,128)(2,1)S(1)}) custom-call(s32[2]{0:T(128)S(1)} %pad_add_fusion.ids_ref, bf16[128,64,128]{2,1,0:T(8,128)(2,1)S(1)} %copy-done.1, ...), custom_call_target="tpu_custom_call" | custom-call | flops 4294967296 | bytes 4194304 | tf_op jit(solution)/shard_map/pallas_call | solution.py:125
  95.4 6.3 %all-to-all-start.4 = ((bf16[16,16,512]{2,1,0:T(8,128)(2,1)}), bf16[16,16,512]{2,1,0:T(8,128)(2,1)S(1)}, u32[]{:S(2)}, u32[]{:S(2)}) async-start(bf16[16,16,512]{2,1,0:T(8,128)(2,1)} %get-tuple-element.15), calls=%async_computation.4 | async-start | bytes 524288 | tf_op jit(solution)/shard_map/all_to_all | solution.py:209
  103.2 2.0 %shard_map.133 = bf16[128,512]{1,0:T(8,128)(2,1)S(1)} custom-call(bf16[128,64,128]{2,1,0:T(8,128)(2,1)S(1)} %copy-done.3, bf16[16,8,512]{2,1,0:T(8,128)(2,1)S(1)} %get-tuple-element.17.one_ref, bf16[8,8,512]{2,1,0:T(8,128)(2,1)S(1)} %get-tuple-element.18.three_ref), custom_call_target="tpu_custom_call" | custom-call | flops 2147483648 | bytes 2097152 | tf_op jit(solution)/shard_map/pallas_call | solution.py:184
  105.3 5.3 %all-to-all-done.4 = bf16[16,16,512]{2,1,0:T(8,128)(2,1)S(1)} async-done(((bf16[16,16,512]{2,1,0:T(8,128)(2,1)}), bf16[16,16,512]{2,1,0:T(8,128)(2,1)S(1)}, u32[]{:S(2)}, u32[]{:S(2)}) %all-to-all-start.4) | async-done | bytes 262176 | tf_op jit(solution)/shard_map/all_to_all | solution.py:209
  110.6 15.9 %all_to_all.35 = bf16[16,16,512]{2,1,0:T(8,128)(2,1)S(1)} all-to-all(bf16[16,16,512]{2,1,0:T(8,128)(2,1)S(1)} %pad_maximum_fusion.1), channel_id=1, replica_groups=mesh['row'=16,'col'=16] {'row'}, dimensions={0} | all-to-all | bytes 524288 | tf_op jit(solution)/shard_map/all_to_all | solution.py:209
  128.7 3.5 %all-to-all-start.6 = ((f32[8,8,512]{2,1,0:T(8,128)}), f32[8,8,512]{2,1,0:T(8,128)S(1)}, u32[]{:S(2)}, u32[]{:S(2)}) async-start(f32[8,8,512]{2,1,0:T(8,128)} %broadcast_in_dim.14), calls=%async_computation.6 | async-start | bytes 262144 | tf_op jit(solution)/shard_map/all_to_all | solution.py:205
  132.8 6.1 %all-to-all-done.6 = f32[8,8,512]{2,1,0:T(8,128)S(1)} async-done(((f32[8,8,512]{2,1,0:T(8,128)}), f32[8,8,512]{2,1,0:T(8,128)S(1)}, u32[]{:S(2)}, u32[]{:S(2)}) %all-to-all-start.6) | async-done | bytes 131104 | tf_op jit(solution)/shard_map/all_to_all | solution.py:205
  (67 shorter events, 16.6 us)
Async XLA Ops:
  1.4 16.9 %collective-permute-start.2 = (bf16[8,512]{1,0:T(8,128)(2,1)S(1)}, bf16[8,512]{1,0:T(8,128)(2,1)S(1)}, u32[]{:S(2)}, u32[]{:S(2)}) collective-permute-start(bf16[8,512]{1,0:T(8,128)(2,1)S(1)} %get-tuple-element.22), channel_id=1, source_target_pairs={{0,12},{1,13},{2,14},{3,15},{4,8},{5,9},{6,10},{7,11},{8,4},{9,5},... | collective-permute-start | bytes 24584 | tf_op jit(solution)/shard_map/ppermute | solution.py:214
  4.7 13.6 %collective-permute-start.1 = (bf16[8,512]{1,0:T(8,128)(2,1)S(1)}, bf16[8,512]{1,0:T(8,128)(2,1)S(1)}, u32[]{:S(2)}, u32[]{:S(2)}) collective-permute-start(bf16[8,512]{1,0:T(8,128)(2,1)S(1)} %get-tuple-element.22), channel_id=1, source_target_pairs={{0,8},{1,9},{2,10},{3,11},{4,12},{5,13},{6,14},{7,15},{8,0},{9,1},... | collective-permute-start | bytes 24584 | tf_op jit(solution)/shard_map/ppermute | solution.py:214
  5.2 13.1 %collective-permute-start = (bf16[8,512]{1,0:T(8,128)(2,1)S(1)}, bf16[8,512]{1,0:T(8,128)(2,1)S(1)}, u32[]{:S(2)}, u32[]{:S(2)}) collective-permute-start(bf16[8,512]{1,0:T(8,128)(2,1)S(1)} %get-tuple-element.22), channel_id=1, source_target_pairs={{0,4},{1,5},{2,6},{3,7},{4,0},{5,1},{6,2},{7,3},{8,12},{9,13},{10,... | collective-permute-start | bytes 24584 | tf_op jit(solution)/shard_map/ppermute | solution.py:214
  6.6 20.0 %all-to-all-start = ((bf16[16,8,512]{2,1,0:T(8,128)(2,1)}), bf16[16,8,512]{2,1,0:T(8,128)(2,1)S(1)}, u32[]{:S(2)}, u32[]{:S(2)}) async-start(bf16[16,8,512]{2,1,0:T(8,128)(2,1)} %broadcast_in_dim.10), calls=%async_computation | async-start | bytes 262144 | tf_op jit(solution)/shard_map/all_to_all | solution.py:205
  18.3 4.5 %collective-permute-start.3 = (bf16[4,8,512]{2,1,0:T(8,128)(2,1)S(1)}, bf16[4,8,512]{2,1,0:T(8,128)(2,1)S(1)}, u32[]{:S(2)}, u32[]{:S(2)}) collective-permute-start(bf16[4,8,512]{2,1,0:T(8,128)(2,1)S(1)} %pad_maximum_fusion.3), channel_id=1, source_target_pairs={{0,2},{1,3},{2,0},{3,1},{4,6},{5,7},{6,4},{7,5},{8,10},{9,11},{10,... | collective-permute-start | bytes 98312 | tf_op jit(solution)/shard_map/ppermute | solution.py:214
  22.8 3.8 %collective-permute-start.4 = (bf16[8,8,512]{2,1,0:T(8,128)(2,1)S(1)}, bf16[8,8,512]{2,1,0:T(8,128)(2,1)S(1)}, u32[]{:S(2)}, u32[]{:S(2)}) collective-permute-start(bf16[8,8,512]{2,1,0:T(8,128)(2,1)S(1)} %constant_dynamic-update-slice_fusion.near_ref), channel_id=1, source_target_pairs={{0,1},{1,0},{2,3},{3,2},{4,5},{5,4},{6,7},{7,6},{8,9},{9,8},{10,11... | collective-permute-start | bytes 196616 | tf_op jit(solution)/shard_map/ppermute | solution.py:214
  26.6 1.6 %copy-start = (bf16[128,64,128]{2,1,0:T(8,128)(2,1)S(1)}, bf16[128,64,128]{2,1,0:T(8,128)(2,1)}, u32[]{:S(2)}) copy-start(bf16[128,64,128]{2,1,0:T(8,128)(2,1)} %data_ref.3) | copy-start | bytes 6291460
  34.6 16.5 %all-to-all-start.1 = ((bf16[16,16,512]{2,1,0:T(8,128)(2,1)}), bf16[16,16,512]{2,1,0:T(8,128)(2,1)S(1)}, u32[]{:S(2)}, u32[]{:S(2)}) async-start(bf16[16,16,512]{2,1,0:T(8,128)(2,1)} %get-tuple-element.11), calls=%async_computation.1 | async-start | bytes 524288 | tf_op jit(solution)/shard_map/all_to_all | solution.py:209
  42.2 27.2 %copy-start.4 = (f32[8,512]{1,0:T(8,128)S(1)}, f32[8,512]{1,0:T(8,128)}, u32[]{:S(2)}) copy-start(f32[8,512]{1,0:T(8,128)} %param.13) | copy-start | bytes 49156
  42.3 27.2 %copy-start.5 = (f32[8,512]{1,0:T(8,128)S(1)}, f32[8,512]{1,0:T(8,128)}, u32[]{:S(2)}) copy-start(f32[8,512]{1,0:T(8,128)} %param.14) | copy-start | bytes 49156
  42.3 27.2 %copy-start.6 = (f32[8,512]{1,0:T(8,128)S(1)}, f32[8,512]{1,0:T(8,128)}, u32[]{:S(2)}) copy-start(f32[8,512]{1,0:T(8,128)} %param.17) | copy-start | bytes 49156
  42.3 27.2 %copy-start.7 = (f32[8,512]{1,0:T(8,128)S(1)}, f32[8,512]{1,0:T(8,128)}, u32[]{:S(2)}) copy-start(f32[8,512]{1,0:T(8,128)} %param.16) | copy-start | bytes 49156
  42.3 27.2 %copy-start.8 = (f32[8,512]{1,0:T(8,128)S(1)}, f32[8,512]{1,0:T(8,128)}, u32[]{:S(2)}) copy-start(f32[8,512]{1,0:T(8,128)} %param.19) | copy-start | bytes 49156
  42.3 27.2 %copy-start.9 = (f32[8,512]{1,0:T(8,128)S(1)}, f32[8,512]{1,0:T(8,128)}, u32[]{:S(2)}) copy-start(f32[8,512]{1,0:T(8,128)} %param.18) | copy-start | bytes 49156
  44.4 43.2 %copy-start.1 = (bf16[128,64,128]{2,1,0:T(8,128)(2,1)S(1)}, bf16[128,64,128]{2,1,0:T(8,128)(2,1)}, u32[]{:S(2)}) copy-start(bf16[128,64,128]{2,1,0:T(8,128)(2,1)} %data_ref.3) | copy-start | bytes 6291460
  52.0 17.4 %all-to-all-start.2 = ((bf16[16,16,512]{2,1,0:T(8,128)(2,1)}), bf16[16,16,512]{2,1,0:T(8,128)(2,1)S(1)}, u32[]{:S(2)}, u32[]{:S(2)}) async-start(bf16[16,16,512]{2,1,0:T(8,128)(2,1)} %pad_maximum_fusion), calls=%async_computation.2 | async-start | bytes 524288 | tf_op jit(solution)/shard_map/all_to_all | solution.py:209
  70.3 7.5 %collective-permute-start.7 = (bf16[16,512]{1,0:T(8,128)(2,1)S(1)}, bf16[16,512]{1,0:T(8,128)(2,1)S(1)}, u32[]{:S(2)}, u32[]{:S(2)}) collective-permute-start(bf16[16,512]{1,0:T(8,128)(2,1)S(1)} %pad_maximum_fusion.4), channel_id=1, source_target_pairs={{0,12},{1,13},{2,14},{3,15},{4,8},{5,9},{6,10},{7,11},{8,4},{9,5},... | collective-permute-start | bytes 49160 | tf_op jit(solution)/shard_map/ppermute | solution.py:214
  70.7 7.2 %collective-permute-start.6 = (bf16[16,512]{1,0:T(8,128)(2,1)S(1)}, bf16[16,512]{1,0:T(8,128)(2,1)S(1)}, u32[]{:S(2)}, u32[]{:S(2)}) collective-permute-start(bf16[16,512]{1,0:T(8,128)(2,1)S(1)} %pad_maximum_fusion.4), channel_id=1, source_target_pairs={{0,8},{1,9},{2,10},{3,11},{4,12},{5,13},{6,14},{7,15},{8,0},{9,1},... | collective-permute-start | bytes 49160 | tf_op jit(solution)/shard_map/ppermute | solution.py:214
  72.9 4.9 %collective-permute-start.5 = (bf16[16,512]{1,0:T(8,128)(2,1)S(1)}, bf16[16,512]{1,0:T(8,128)(2,1)S(1)}, u32[]{:S(2)}, u32[]{:S(2)}) collective-permute-start(bf16[16,512]{1,0:T(8,128)(2,1)S(1)} %pad_maximum_fusion.4), channel_id=1, source_target_pairs={{0,4},{1,5},{2,6},{3,7},{4,0},{5,1},{6,2},{7,3},{8,12},{9,13},{10,... | collective-permute-start | bytes 49160 | tf_op jit(solution)/shard_map/ppermute | solution.py:214
  74.3 13.3 %all-to-all-start.3 = ((bf16[16,8,512]{2,1,0:T(8,128)(2,1)}), bf16[16,8,512]{2,1,0:T(8,128)(2,1)S(1)}, u32[]{:S(2)}, u32[]{:S(2)}) async-start(bf16[16,8,512]{2,1,0:T(8,128)(2,1)} %broadcast_in_dim.12), calls=%async_computation.3 | async-start | bytes 262144 | tf_op jit(solution)/shard_map/all_to_all | solution.py:205
  77.9 4.8 %collective-permute-start.8 = (bf16[4,16,512]{2,1,0:T(8,128)(2,1)S(1)}, bf16[4,16,512]{2,1,0:T(8,128)(2,1)S(1)}, u32[]{:S(2)}, u32[]{:S(2)}) collective-permute-start(bf16[4,16,512]{2,1,0:T(8,128)(2,1)S(1)} %pad_maximum_fusion.2), channel_id=1, source_target_pairs={{0,2},{1,3},{2,0},{3,1},{4,6},{5,7},{6,4},{7,5},{8,10},{9,11},{10,... | collective-permute-start | bytes 196616 | tf_op jit(solution)/shard_map/ppermute | solution.py:214
  82.7 4.9 %collective-permute-start.9 = (bf16[8,16,512]{2,1,0:T(8,128)(2,1)S(1)}, bf16[8,16,512]{2,1,0:T(8,128)(2,1)S(1)}, u32[]{:S(2)}, u32[]{:S(2)}) collective-permute-start(bf16[8,16,512]{2,1,0:T(8,128)(2,1)S(1)} %constant_dynamic-update-slice_fusion.5.near_ref), channel_id=1, source_target_pairs={{0,1},{1,0},{2,3},{3,2},{4,5},{5,4},{6,7},{7,6},{8,9},{9,8},{10,11... | collective-permute-start | bytes 393224 | tf_op jit(solution)/shard_map/ppermute | solution.py:214
  95.4 15.2 %all-to-all-start.4 = ((bf16[16,16,512]{2,1,0:T(8,128)(2,1)}), bf16[16,16,512]{2,1,0:T(8,128)(2,1)S(1)}, u32[]{:S(2)}, u32[]{:S(2)}) async-start(bf16[16,16,512]{2,1,0:T(8,128)(2,1)} %get-tuple-element.15), calls=%async_computation.4 | async-start | bytes 524288 | tf_op jit(solution)/shard_map/all_to_all | solution.py:209
  128.7 10.3 %all-to-all-start.6 = ((f32[8,8,512]{2,1,0:T(8,128)}), f32[8,8,512]{2,1,0:T(8,128)S(1)}, u32[]{:S(2)}, u32[]{:S(2)}) async-start(f32[8,8,512]{2,1,0:T(8,128)} %broadcast_in_dim.14), calls=%async_computation.6 | async-start | bytes 262144 | tf_op jit(solution)/shard_map/all_to_all | solution.py:205
  (2 other events, 2.9 us)

commit v3 on v2

v3 whole, which is shorter than its diff:
```python
import functools
import math

import jax
import jax.numpy as jnp
from jax import lax
from jax.experimental import pallas as pl
from jax.experimental.pallas import tpu as pltpu
from jax.sharding import PartitionSpec as P

ITERS = 2
STEP = 10
BLOCK = 64
SUB = 4
VMEM_LIMIT = 53 << 20

learn_rate = 0.05
beta_one = 0.8
beta_two = 0.95
adam_eps = 1e-08

f32 = jnp.float32
bf16 = jnp.bfloat16

CORE, Y_HI, X_ONE = 1, 2, 4


def adam_step(param, first, second, grad, counter):
    first = beta_one * first + (1.0 - beta_one) * grad
    second = beta_two * second + (1.0 - beta_two) * grad * grad
    corr_one = 1.0 - beta_one**counter
    corr_two = 1.0 - beta_two**counter
    param = param - learn_rate * (first / corr_one) / (jnp.sqrt(second / corr_two) + adam_eps)
    return (param, first, second)


def gather_codes():
    return [y + x * X_ONE for y in (0, Y_HI) for x in range(4)]


def third_slab(col):
    return col // X_ONE * 2 + col % 2


def slope_kernel(scales, stepped, ids_ref, data_ref, near_ref, far_ref, two_in_ref, *refs):
    if stepped:
        near_three_ref, far_three_ref, *refs = refs
    else:
        three_in_ref, *refs = refs
    (sent_ref, kept_ref, slope_ref, one_ref, three_ref, two_ref, ga_acc, gc_acc) = refs
    step = pl.program_id(0)
    n_slab, own, rank = one_ref.shape
    depth = three_ref.shape[0] * three_ref.shape[1]
    cols = two_ref.shape[0] * two_ref.shape[1]
    here = ids_ref[1]

    @pl.when(step == 0)
    def _():
        for place, code in enumerate(gather_codes()):
            one_ref[here ^ code] = near_ref[place]
            one_ref[here ^ code ^ CORE] = far_ref[place]
        if stepped:
            for m in range(4):
                col = here ^ (m * X_ONE)
                three_ref[third_slab(col)] = near_three_ref[m]
                three_ref[third_slab(col ^ CORE)] = far_three_ref[m]
        else:
            three_ref[...] = three_in_ref[...]
        for slab in range(two_ref.shape[0]):
            two_ref[slab] = two_in_ref[slab][:two_ref.shape[1]]
        gc_acc[...] = jnp.zeros_like(gc_acc)

    def run(logistic):
        two = two_ref[...].reshape(cols, rank)
        three = three_ref[...].reshape(depth, rank)
        three_f = three.astype(f32)
        slabs = BLOCK // own
        one = one_ref[pl.ds(step * slabs, slabs)].reshape(BLOCK, rank)
        n = BLOCK // SUB

        def rows(s):
            return slice(s * SUB, (s + 1) * SUB)

        def rebuild(s):
            scaled = (one[rows(s)][:, None, :] * three[None]).reshape(SUB * depth, rank)
            return lax.dot_general(scaled, two, (((1,), (1,)), ((), ())), preferred_element_type=f32)

        def slope(s, rebuilt):
            values = data_ref[rows(s)].reshape(SUB * depth, cols).astype(f32)
            if logistic:
                out = 0.5 * jnp.tanh(0.5 * rebuilt) + jnp.where(values > 0, -0.5, 0.5)
            else:
                out = jnp.clip(rebuilt - values, -1.0, 1.0)
            out = out.astype(bf16)
            slope_ref[rows(s)] = out.reshape(SUB, depth, cols)
            return out

        def project(deriv):
            return jnp.dot(deriv, two, preferred_element_type=f32).reshape(SUB, depth, rank)

        rebuilt, derivs, projs = {}, {}, {}
        grad_one, grad_three = [], None
        for t in range(n + 3):
            if t < n:
                rebuilt[t] = rebuild(t)
            if 0 <= t - 1 < n:
                derivs[t - 1] = slope(t - 1, rebuilt.pop(t - 1))
            if 0 <= t - 2 < n:
                projs[t - 2] = project(derivs.pop(t - 2))
            if 0 <= t - 3 < n:
                proj = projs.pop(t - 3)
                one_f = one[rows(t - 3)].astype(f32)
                grad_one.append(jnp.sum(proj * three_f[None], axis=1))
                part = jnp.sum(proj * one_f[:, None, :], axis=0)
                grad_three = part if grad_three is None else grad_three + part
        ga_acc[pl.ds(step * slabs, slabs)] = jnp.concatenate(grad_one).reshape(slabs, own, rank)
        gc_acc[...] += grad_three.reshape(gc_acc.shape)

    pl.when(ids_ref[0] == 1)(lambda: run(True))
    pl.when(ids_ref[0] != 1)(lambda: run(False))

    @pl.when(step == pl.num_programs(0) - 1)
    def _():
        for side, out_ref in ((here, kept_ref), (here ^ CORE, sent_ref)):
            for m in range(4):
                col = side ^ (m * X_ONE)
                out_ref[m] = (ga_acc[col] * scales[0]).astype(bf16)
                out_ref[4 + m] = (gc_acc[third_slab(col)] * scales[2]).astype(bf16)
                out_ref[8 + m] = (ga_acc[col ^ Y_HI] * scales[0]).astype(bf16)


def slopes(ids, tensor, near, far, twos, threes, scales):
    rows, depth, cols = tensor.shape
    own, rank = near.shape[1:]
    slabs = rows // own
    own_two = cols // twos.shape[0]
    own_three = threes[0].shape[1]
    whole = lambda shape: pl.BlockSpec(shape, lambda i: (0,) * len(shape))
    swapped = (12, own, rank)
    return pl.pallas_call(
        functools.partial(slope_kernel, scales, len(threes) == 2),
        grid=(rows // BLOCK,),
        in_specs=[
            pl.BlockSpec(memory_space=pltpu.SMEM),
            pl.BlockSpec((BLOCK, depth, cols), lambda i: (i, 0, 0)),
            whole(near.shape),
            whole(far.shape),
            whole(twos.shape),
            *[whole(x.shape) for x in threes],
        ],
        out_specs=[
            whole(swapped),
            whole(swapped),
            pl.BlockSpec((BLOCK, depth, cols), lambda i: (i, 0, 0)),
            whole((slabs, own, rank)),
            whole((depth // own_three, own_three, rank)),
        ],
        out_shape=[
            jax.ShapeDtypeStruct(swapped, bf16),
            jax.ShapeDtypeStruct(swapped, bf16),
            jax.ShapeDtypeStruct((rows, depth, cols), bf16),
            jax.ShapeDtypeStruct((slabs, own, rank), bf16),
            jax.ShapeDtypeStruct((depth // own_three, own_three, rank), bf16),
        ],
        scratch_shapes=[
            pltpu.VMEM((twos.shape[0], own_two, rank), bf16),
            pltpu.VMEM((slabs, own, rank), f32),
            pltpu.VMEM((depth // own_three, own_three, rank), f32),
        ],
        compiler_params=pltpu.CompilerParams(vmem_limit_bytes=VMEM_LIMIT),
        cost_estimate=pl.CostEstimate(
            flops=8 * rows * depth * cols * rank, bytes_accessed=4 << 20, transcendentals=rows * depth * cols
        ),
    )(ids, tensor, near, far, twos, *threes)


def second_kernel(scale, slope_ref, one_ref, three_ref, out_ref, acc):
    step = pl.program_id(0)
    block, depth, cols = slope_ref.shape
    rank = one_ref.shape[2]
    one = one_ref[...].reshape(block, rank)
    three = three_ref[...].reshape(depth, rank)
    scaled = (one[:, None, :] * three[None]).reshape(block * depth, rank)
    part = lax.dot_general(
        slope_ref[...].reshape(block * depth, cols), scaled, (((0,), (0,)), ((), ())), preferred_element_type=f32
    )

    @pl.when(step == 0)
    def _():
        acc[...] = part

    @pl.when(step != 0)
    def _():
        acc[...] += part

    @pl.when(step == pl.num_programs(0) - 1)
    def _():
        out_ref[...] = (acc[...] * scale).astype(bf16)


def second_grad(slope, ones, threes, scale):
    rows, depth, cols = slope.shape
    slabs, own, rank = ones.shape
    block = 32
    return pl.pallas_call(
        functools.partial(second_kernel, scale),
        grid=(rows // block,),
        in_specs=[
            pl.BlockSpec((block, depth, cols), lambda i: (i, 0, 0)),
            pl.BlockSpec((block // own, own, rank), lambda i: (i, 0, 0)),
            pl.BlockSpec(threes.shape, lambda i: (0, 0, 0)),
        ],
        out_specs=pl.BlockSpec((cols, rank), lambda i: (0, 0)),
        out_shape=jax.ShapeDtypeStruct((cols, rank), bf16),
        scratch_shapes=[pltpu.VMEM((cols, rank), f32)],
        compiler_params=pltpu.CompilerParams(vmem_limit_bytes=VMEM_LIMIT),
        cost_estimate=pl.CostEstimate(
            flops=4 * rows * depth * cols * rank, bytes_accessed=2 << 20, transcendentals=0
        ),
    )(slope, ones, threes)


def place_kernel(ids_ref, near_ref, far_ref, out_ref):
    for m in range(4):
        col = ids_ref[1] ^ (m * X_ONE)
        out_ref[third_slab(col)] = near_ref[m]
        out_ref[third_slab(col ^ CORE)] = far_ref[m]


def place_third(ids, near, far):
    slabs, own, rank = near.shape
    return pl.pallas_call(
        place_kernel,
        in_specs=[pl.BlockSpec(memory_space=pltpu.SMEM)] + [pl.BlockSpec(memory_space=pltpu.VMEM)] * 2,
        out_specs=pl.BlockSpec(memory_space=pltpu.VMEM),
        out_shape=jax.ShapeDtypeStruct((2 * slabs, own, rank), near.dtype),
        compiler_params=pltpu.CompilerParams(vmem_limit_bytes=8 << 20),
    )(ids, near, far)


def swap_all(parts, axis):
    return lax.all_to_all(parts, axis, 0, 0)


def to_all(part, size):
    return jnp.broadcast_to(part[None], (size,) + part.shape)


def total(parts):
    return jnp.sum(parts.astype(f32), axis=0)


def swap(part, code):
    size = lax.axis_size("col")
    return lax.ppermute(part, "col", [(i, i ^ code) for i in range(size)])


def plus(left, right):
    return (left.astype(f32) + right.astype(f32)).astype(bf16)


def gather_col(part):
    half = jnp.stack([part] + [swap(part, m * X_ONE) for m in (1, 2, 3)])
    near = jnp.concatenate([half, swap(half, Y_HI)])
    return near, swap(near, CORE)


def gather_third(part):
    near = jnp.stack([part] + [swap(part, m * X_ONE) for m in (1, 2, 3)])
    return near, swap(near, CORE)


def fold_kernel(both_ref, got_ref, out_ref):
    half = got_ref.shape[0] // 2
    for m in range(half):
        out_ref[m, 0] = plus(both_ref[m], got_ref[half + m])
        out_ref[m, 1] = plus(both_ref[half + m], got_ref[m])


def fold(both, got):
    slabs, own, rank = got.shape
    return pl.pallas_call(
        fold_kernel,
        in_specs=[pl.BlockSpec(memory_space=pltpu.VMEM)] * 2,
        out_specs=pl.BlockSpec(memory_space=pltpu.VMEM),
        out_shape=jax.ShapeDtypeStruct((slabs // 2, 2, own, rank), bf16),
        compiler_params=pltpu.CompilerParams(vmem_limit_bytes=8 << 20),
        cost_estimate=pl.CostEstimate(flops=1 << 16, bytes_accessed=1 << 18, transcendentals=0),
    )(both, got)


def reduce_col(both):
    pairs = fold(both, swap(both[4:], Y_HI))
    got = [swap(pairs[m], m * X_ONE) for m in (1, 2, 3)]
    out = pairs[0].astype(f32)
    for part in got:
        out = out + part.astype(f32)
    return out[0], out[1]


def shards(
    tensor, loss_kind, factor_one, factor_two, factor_three,
    first_one, second_one, first_two, second_two, first_three, second_three,
):
    tile_rows, tile_depth, tile_cols = tensor.shape
    n_row, n_col = lax.axis_size("row"), lax.axis_size("col")
    rank = factor_one.shape[1]
    own_two = factor_two.shape[0]
    deep = 2 * tile_depth // n_col
    full_rows, full_cols = tile_rows * n_row, tile_cols * n_col
    scales = (
        1.0 / math.sqrt(full_cols * tile_depth),
        1.0 / math.sqrt(full_rows * tile_depth),
        1.0 / math.sqrt(full_rows * full_cols),
    )
    here = lax.axis_index("col")
    ids = jnp.stack([loss_kind[0, 0, 0], here.astype(jnp.int32)])
    mine = lambda x: lax.dynamic_slice_in_dim(x, third_slab(here) * deep, deep, 0)
    part_three, first_three, second_three = mine(factor_three), mine(first_three), mine(second_three)
    start_one, start_two, start_three = (factor_one, factor_two, part_three)
    twos = swap_all(to_all(factor_two.astype(bf16), n_row), "row")
    near, far = gather_col(factor_one.astype(bf16))
    threes = (factor_three.astype(bf16).reshape(tile_depth // deep, deep, rank),)
    for iteration in range(ITERS):
        last = iteration == ITERS - 1
        counter = STEP + iteration + 1
        sent, kept, slope, ones, all_threes = slopes(ids, tensor, near, far, twos, threes, scales)
        grad_two = second_grad(slope, ones, all_threes, scales[1]).reshape(n_row, own_two, rank)
        both = plus(kept, swap(sent, CORE))
        if not last:
            both, grad_two = lax.optimization_barrier((both, grad_two))
        grad_one, grad_three = reduce_col(both)
        factor_one, first_one, second_one = adam_step(factor_one, first_one, second_one, grad_one, counter)
        grad_three = grad_three.astype(bf16)
        if last:
            sent = jnp.concatenate([grad_two, to_all(grad_three, n_row)], axis=1)
            got = total(swap_all(sent, "row"))
            grad_two, grad_three = got[:own_two], got[own_two:]
        else:
            grad_two = total(swap_all(grad_two, "row"))
        factor_two, first_two, second_two = adam_step(factor_two, first_two, second_two, grad_two, counter)
        if not last:
            near, far = gather_col(factor_one.astype(bf16))
            sent = jnp.concatenate([factor_two.astype(bf16), grad_three])
            twos = swap_all(to_all(sent, n_row), "row")
            grad_three = total(twos[:, own_two:])
        part_three, first_three, second_three = adam_step(
            part_three, first_three, second_three, grad_three, counter
        )
        if not last:
            threes = gather_third(part_three.astype(bf16))
    spread = learn_rate * ITERS
    new_three = place_third(ids, *gather_third((start_three - part_three) / spread)).reshape(tile_depth, rank)
    return ((start_one - factor_one) / spread, (start_two - factor_two) / spread, new_three)


def solution(mesh):
    in_specs = (
        P("row", None, "col"),
        P("row", None, "col"),
        P(("row", "col"), None),
        P(("col", "row"), None),
        P(),
        P(("row", "col"), None),
        P(("row", "col"), None),
        P(("col", "row"), None),
        P(("col", "row"), None),
        P(),
        P(),
    )
    out_specs = (P(("row", "col"), None), P(("col", "row"), None), P())
    return jax.shard_map(shards, mesh=mesh, in_specs=in_specs, out_specs=out_specs, check_vma=False)
```

time: 142 us -> 144 us (1.014); the launches traced: 140 us -> 143 us
  starting transfers between devices: 55.2 us -> 72.8 us
  waiting for transfers between devices: 35.2 us -> 24.5 us
  Pallas kernels: 16.9 us -> 24 us
  local copies, waits for them, and re-layouts: 8.45 us -> 2.68 us
  blocking collectives: 15.9 us -> 12.2 us
    ppermute x10 -> x28, starting transfers between devices: 18.4 us -> 49.3 us  [swap(): return lax.ppermute(part, 'col', [(i, i ^ code) for i in range(size)])]
    all_to_all x6 -> x3, waiting for transfers between devices: 29.1 us -> 9.59 us  [swap_all(): return lax.all_to_all(parts, axis, 0, 0)]
    all_to_all x6 -> x3, starting transfers between devices: 36.9 us -> 23.5 us  [swap_all(): return lax.all_to_all(parts, axis, 0, 0)]
    ppermute x10 -> x28, waiting for transfers between devices: 6.13 us -> 14.9 us  [swap(): return lax.ppermute(part, 'col', [(i, i ^ code) for i in range(size)])]
    unnamed x27 -> x18, local copies, waits for them, and re-layouts: 5.22 us -> 0.04 us
    pallas_call x2, Pallas kernels: 4.08 us -> 8.02 us  [second_grad(): pl.pallas_call(functools.partial(second_kernel, scale), grid=(rows // blo...]
    all_to_all x1, blocking collectives: 15.9 us -> 12.2 us  [swap_all(): return lax.all_to_all(parts, axis, 0, 0)]
    pallas_call x2 -> x5, Pallas kernels: 12.8 us -> 16 us  [the longest x2 14.7 us: slopes(): pl.pallas_call(functools.partial(slope_kernel, scales, len(threes) == 2),...]
  transfers between devices with their start and end apart: 16 -> 31, of which waited for: 8 -> 12; matrix products, arithmetic and copies ran while one was open for 4% -> 5% of each run, Pallas kernels for 3% -> 6%
where the time goes in v3:
time: 144 us; the launch traced here: 143 us
  starting transfers between devices  72.8 us (51%)
  waiting for transfers between devices  24.5 us (17%)
  Pallas kernels  24 us (17%)
  blocking collectives  12.2 us (8%)
  other arithmetic  6.19 us (4%)
  local copies, waits for them, and re-layouts  2.68 us (2%)
    ppermute x28, starting transfers between devices, swap(): return lax.ppermute(part, 'col', [(i, i ^ code) for i in range(size)])  49.3 us
    all_to_all x3, starting transfers between devices, swap_all(): return lax.all_to_all(parts, axis, 0, 0)  23.5 us
    ppermute x28, waiting for transfers between devices, swap(): return lax.ppermute(part, 'col', [(i, i ^ code) for i in range(size)])  14.9 us
    pallas_call x2, Pallas kernels, slopes(): pl.pallas_call(functools.partial(slope_kernel, scales, len(threes) == 2),...  14.7 us
    all_to_all x1, blocking collectives, swap_all(): return lax.all_to_all(parts, axis, 0, 0)  12.2 us
    all_to_all x3, waiting for transfers between devices, swap_all(): return lax.all_to_all(parts, axis, 0, 0)  9.59 us
    pallas_call x2, Pallas kernels, second_grad(): pl.pallas_call(functools.partial(second_kernel, scale), grid=(rows // blo...  8.02 us
  transfers between devices with their start and end apart: 31, of which 12 were waited for; matrix products, arithmetic and copies ran while one was open for 5% of the time, Pallas kernels for 6%

profile of v3, /device:TPU:1, one launch (start us, length us, event | category | flops | bytes accessed | tf_op | source)
XLA Modules:
  0.0 143.4 jit_solution(4711965634314435065)
XLA Ops:
  1.4 3.3 %collective-permute-start.2 = (bf16[8,512]{1,0:T(8,128)(2,1)S(1)}, bf16[8,512]{1,0:T(8,128)(2,1)S(1)}, u32[]{:S(2)}, u32[]{:S(2)}) collective-permute-start(bf16[8,512]{1,0:T(8,128)(2,1)S(1)} %get-tuple-element.32), channel_id=1, source_target_pairs={{0,12},{1,13},{2,14},{3,15},{4,8},{5,9},{6,10},{7,11},{8,4},{9,5},... | collective-permute-start | bytes 24584 | tf_op jit(solution)/shard_map/ppermute | solution.py:255
  6.6 9.5 %all-to-all-start = ((bf16[16,8,512]{2,1,0:T(8,128)(2,1)}), bf16[16,8,512]{2,1,0:T(8,128)(2,1)S(1)}, u32[]{:S(2)}, u32[]{:S(2)}) async-start(bf16[16,8,512]{2,1,0:T(8,128)(2,1)} %broadcast_in_dim.8), calls=%async_computation | async-start | bytes 262144 | tf_op jit(solution)/shard_map/all_to_all | solution.py:242
  18.3 2.7 %collective-permute-start.3 = (bf16[4,8,512]{2,1,0:T(8,128)(2,1)S(1)}, bf16[4,8,512]{2,1,0:T(8,128)(2,1)S(1)}, u32[]{:S(2)}, u32[]{:S(2)}) collective-permute-start(bf16[4,8,512]{2,1,0:T(8,128)(2,1)S(1)} %pad_maximum_fusion.2), channel_id=1, source_target_pairs={{0,2},{1,3},{2,0},{3,1},{4,6},{5,7},{6,4},{7,5},{8,10},{9,11},{10,... | collective-permute-start | bytes 98312 | tf_op jit(solution)/shard_map/ppermute | solution.py:255
  21.0 1.8 %collective-permute-done.3 = bf16[4,8,512]{2,1,0:T(8,128)(2,1)S(1)} collective-permute-done((bf16[4,8,512]{2,1,0:T(8,128)(2,1)S(1)}, bf16[4,8,512]{2,1,0:T(8,128)(2,1)S(1)}, u32[]{:S(2)}, u32[]{:S(2)}) %collective-permute-start.3) | collective-permute-done | bytes 32800 | tf_op jit(solution)/shard_map/ppermute | solution.py:255
  22.8 2.9 %collective-permute-start.4 = (bf16[8,8,512]{2,1,0:T(8,128)(2,1)S(1)}, bf16[8,8,512]{2,1,0:T(8,128)(2,1)S(1)}, u32[]{:S(2)}, u32[]{:S(2)}) collective-permute-start(bf16[8,8,512]{2,1,0:T(8,128)(2,1)S(1)} %constant_dynamic-update-slice_fusion.near_ref), channel_id=1, source_target_pairs={{0,1},{1,0},{2,3},{3,2},{4,5},{5,4},{6,7},{7,6},{8,9},{9,8},{10,11... | collective-permute-start | bytes 196616 | tf_op jit(solution)/shard_map/ppermute | solution.py:255
  26.6 7.3 %shard_map.130 = (bf16[12,8,512]{2,1,0:T(8,128)(2,1)S(1)}, bf16[12,8,512]{2,1,0:T(8,128)(2,1)S(1)}, bf16[128,64,128]{2,1,0:T(8,128)(2,1)}, bf16[16,8,512]{2,1,0:T(8,128)(2,1)S(1)}, bf16[8,8,512]{2,1,0:T(8,128)(2,1)S(1)}) custom-call(s32[2]{0:T(128)S(1)} %pad_add_fusion.ids_ref, bf16[128,64,128]{2,1,0:T(8,128)(2,1)} %data_ref.3, ...), custom_call_target="tpu_custom_call" | custom-call | flops 4294967296 | bytes 4194304 | tf_op jit(solution)/shard_map/pallas_call | solution.py:140
  34.9 4.4 %shard_map.131 = bf16[128,512]{1,0:T(8,128)(2,1)} custom-call(bf16[128,64,128]{2,1,0:T(8,128)(2,1)} %get-tuple-element.17.slope_ref, bf16[16,8,512]{2,1,0:T(8,128)(2,1)S(1)} %get-tuple-element.18.one_ref, bf16[8,8,512]{2,1,0:T(8,128)(2,1)S(1)} %get-tuple-element.19.three_ref), custom_call_target="tpu_custom_call" | custom-call | flops 2147483648 | bytes 2097152 | tf_op jit(solution)/shard_map/pallas_call | solution.py:205
  39.3 2.7 %collective-permute-start.6 = (bf16[8,8,512]{2,1,0:T(8,128)(2,1)S(1)}, bf16[8,8,512]{2,1,0:T(8,128)(2,1)S(1)}, u32[]{:S(2)}, u32[]{:S(2)}) collective-permute-start(bf16[8,8,512]{2,1,0:T(8,128)(2,1)S(1)} %slice.57), channel_id=1, source_target_pairs={{0,2},{1,3},{2,0},{3,1},{4,6},{5,7},{6,4},{7,5},{8,10},{9,11},{10,... | collective-permute-start | bytes 196616 | tf_op jit(solution)/shard_map/ppermute | solution.py:255
  42.1 2.6 %collective-permute-done.6.got_ref = bf16[8,8,512]{2,1,0:T(8,128)(2,1)S(1)} collective-permute-done((bf16[8,8,512]{2,1,0:T(8,128)(2,1)S(1)}, bf16[8,8,512]{2,1,0:T(8,128)(2,1)S(1)}, u32[]{:S(2)}, u32[]{:S(2)}) %collective-permute-start.6) | collective-permute-done | bytes 65568 | tf_op jit(solution)/shard_map/ppermute | solution.py:255
  46.0 1.8 %collective-permute-start.9 = (bf16[2,8,512]{2,1,0:T(8,128)(2,1)S(1)}, bf16[2,8,512]{2,1,0:T(8,128)(2,1)S(1)}, u32[]{:S(2)}, u32[]{:S(2)}) collective-permute-start(bf16[2,8,512]{2,1,0:T(8,128)(2,1)S(1)} %get-tuple-element.37), channel_id=1, source_target_pairs={{0,12},{1,13},{2,14},{3,15},{4,8},{5,9},{6,10},{7,11},{8,4},{9,5},... | collective-permute-start | bytes 49160 | tf_op jit(solution)/shard_map/ppermute | solution.py:255
  48.5 7.1 %all-to-all-start.1 = ((bf16[16,8,512]{2,1,0:T(8,128)(2,1)}), bf16[16,8,512]{2,1,0:T(8,128)(2,1)S(1)}, u32[]{:S(2)}, u32[]{:S(2)}) async-start(bf16[16,8,512]{2,1,0:T(8,128)(2,1)} %bitcast.7), calls=%async_computation.1 | async-start | bytes 262144 | tf_op jit(solution)/shard_map/all_to_all | solution.py:242
  55.6 2.3 %collective-permute-start.12 = (bf16[8,512]{1,0:T(8,128)(2,1)S(1)}, bf16[8,512]{1,0:T(8,128)(2,1)S(1)}, u32[]{:S(2)}, u32[]{:S(2)}) collective-permute-start(bf16[8,512]{1,0:T(8,128)(2,1)S(1)} %get-tuple-element.30), channel_id=1, source_target_pairs={{0,12},{1,13},{2,14},{3,15},{4,8},{5,9},{6,10},{7,11},{8,4},{9,5},... | collective-permute-start | bytes 24584 | tf_op jit(solution)/shard_map/ppermute | solution.py:255
  59.6 2.4 %collective-permute-done.11 = bf16[8,512]{1,0:T(8,128)(2,1)S(1)} collective-permute-done((bf16[8,512]{1,0:T(8,128)(2,1)S(1)}, bf16[8,512]{1,0:T(8,128)(2,1)S(1)}, u32[]{:S(2)}, u32[]{:S(2)}) %collective-permute-start.11) | collective-permute-done | bytes 8224 | tf_op jit(solution)/shard_map/ppermute | solution.py:255
  62.0 2.5 %collective-permute-start.13 = (bf16[4,8,512]{2,1,0:T(8,128)(2,1)S(1)}, bf16[4,8,512]{2,1,0:T(8,128)(2,1)S(1)}, u32[]{:S(2)}, u32[]{:S(2)}) collective-permute-start(bf16[4,8,512]{2,1,0:T(8,128)(2,1)S(1)} %pad_maximum_fusion.3), channel_id=1, source_target_pairs={{0,2},{1,3},{2,0},{3,1},{4,6},{5,7},{6,4},{7,5},{8,10},{9,11},{10,... | collective-permute-start | bytes 98312 | tf_op jit(solution)/shard_map/ppermute | solution.py:255
  65.4 6.9 %all-to-all-start.2 = ((bf16[16,16,512]{2,1,0:T(8,128)(2,1)}), bf16[16,16,512]{2,1,0:T(8,128)(2,1)S(1)}, u32[]{:S(2)}, u32[]{:S(2)}) async-start(bf16[16,16,512]{2,1,0:T(8,128)(2,1)} %broadcast_in_dim.9), calls=%async_computation.2 | async-start | bytes 524288 | tf_op jit(solution)/shard_map/all_to_all | solution.py:242
  72.3 9.6 %all-to-all-done.2.two_in_ref = bf16[16,16,512]{2,1,0:T(8,128)(2,1)S(1)} async-done(((bf16[16,16,512]{2,1,0:T(8,128)(2,1)}), bf16[16,16,512]{2,1,0:T(8,128)(2,1)S(1)}, u32[]{:S(2)}, u32[]{:S(2)}) %all-to-all-start.2) | async-done | bytes 262176 | tf_op jit(solution)/shard_map/all_to_all | solution.py:242
  86.1 6.4 %collective-permute-start.14 = (bf16[8,8,512]{2,1,0:T(8,128)(2,1)S(1)}, bf16[8,8,512]{2,1,0:T(8,128)(2,1)S(1)}, u32[]{:S(2)}, u32[]{:S(2)}) collective-permute-start(bf16[8,8,512]{2,1,0:T(8,128)(2,1)S(1)} %constant_dynamic-update-slice_fusion.5.near_ref), channel_id=1, source_target_pairs={{0,1},{1,0},{2,3},{3,2},{4,5},{5,4},{6,7},{7,6},{8,9},{9,8},{10,11... | collective-permute-start | bytes 196616 | tf_op jit(solution)/shard_map/ppermute | solution.py:255
  92.5 2.5 %collective-permute-start.18 = (bf16[4,8,512]{2,1,0:T(8,128)(2,1)S(1)}, bf16[4,8,512]{2,1,0:T(8,128)(2,1)S(1)}, u32[]{:S(2)}, u32[]{:S(2)}) collective-permute-start(bf16[4,8,512]{2,1,0:T(8,128)(2,1)S(1)} %pad_maximum_fusion.4.refs_0_), channel_id=1, source_target_pairs={{0,1},{1,0},{2,3},{3,2},{4,5},{5,4},{6,7},{7,6},{8,9},{9,8},{10,11... | collective-permute-start | bytes 98312 | tf_op jit(solution)/shard_map/ppermute | solution.py:255
  95.9 7.4 %shard_map.133 = (bf16[12,8,512]{2,1,0:T(8,128)(2,1)S(1)}, bf16[12,8,512]{2,1,0:T(8,128)(2,1)S(1)}, bf16[128,64,128]{2,1,0:T(8,128)(2,1)}, bf16[16,8,512]{2,1,0:T(8,128)(2,1)S(1)}, bf16[8,8,512]{2,1,0:T(8,128)(2,1)S(1)}) custom-call(s32[2]{0:T(128)S(1)} %pad_add_fusion.ids_ref, bf16[128,64,128]{2,1,0:T(8,128)(2,1)} %data_ref.3, ...), custom_call_target="tpu_custom_call" | custom-call | flops 4294967296 | bytes 4194304 | tf_op jit(solution)/shard_map/pallas_call | solution.py:140
  106.4 3.0 %collective-permute-done.20.got_ref = bf16[8,8,512]{2,1,0:T(8,128)(2,1)S(1)} collective-permute-done((bf16[8,8,512]{2,1,0:T(8,128)(2,1)S(1)}, bf16[8,8,512]{2,1,0:T(8,128)(2,1)S(1)}, u32[]{:S(2)}, u32[]{:S(2)}) %collective-permute-start.20) | collective-permute-done | bytes 65568 | tf_op jit(solution)/shard_map/ppermute | solution.py:255
  112.7 3.7 %shard_map.135 = bf16[128,512]{1,0:T(8,128)(2,1)S(1)} custom-call(bf16[128,64,128]{2,1,0:T(8,128)(2,1)} %get-tuple-element.24.slope_ref, bf16[16,8,512]{2,1,0:T(8,128)(2,1)S(1)} %get-tuple-element.25.one_ref, bf16[8,8,512]{2,1,0:T(8,128)(2,1)S(1)} %get-tuple-element.26.three_ref), custom_call_target="tpu_custom_call" | custom-call | flops 2147483648 | bytes 2097152 | tf_op jit(solution)/shard_map/pallas_call | solution.py:205
  116.5 12.2 %all_to_all.20 = bf16[16,16,512]{2,1,0:T(8,128)(2,1)S(1)} all-to-all(bf16[16,16,512]{2,1,0:T(8,128)(2,1)S(1)} %pad_maximum_fusion), channel_id=1, replica_groups=mesh['row'=16,'col'=16] {'row'}, dimensions={0} | all-to-all | bytes 524288 | tf_op jit(solution)/shard_map/all_to_all | solution.py:242
  134.0 1.9 %collective-permute-done.25 = f32[8,512]{1,0:T(8,128)S(1)} collective-permute-done((f32[8,512]{1,0:T(8,128)S(1)}, f32[8,512]{1,0:T(8,128)S(1)}, u32[]{:S(2)}, u32[]{:S(2)}) %collective-permute-start.25) | collective-permute-done | bytes 16416 | tf_op jit(solution)/shard_map/ppermute | solution.py:255
  135.9 5.3 %collective-permute-start.27 = (f32[4,8,512]{2,1,0:T(8,128)S(1)}, f32[4,8,512]{2,1,0:T(8,128)S(1)}, u32[]{:S(2)}, u32[]{:S(2)}) collective-permute-start(f32[4,8,512]{2,1,0:T(8,128)S(1)} %pad_maximum_fusion.1.near_ref), channel_id=1, source_target_pairs={{0,1},{1,0},{2,3},{3,2},{4,5},{5,4},{6,7},{7,6},{8,9},{9,8},{10,11... | collective-permute-start | bytes 196616 | tf_op jit(solution)/shard_map/ppermute | solution.py:255
  (97 shorter events, 30.2 us)
Async XLA Ops:
  1.4 16.9 %collective-permute-start.2 = (bf16[8,512]{1,0:T(8,128)(2,1)S(1)}, bf16[8,512]{1,0:T(8,128)(2,1)S(1)}, u32[]{:S(2)}, u32[]{:S(2)}) collective-permute-start(bf16[8,512]{1,0:T(8,128)(2,1)S(1)} %get-tuple-element.32), channel_id=1, source_target_pairs={{0,12},{1,13},{2,14},{3,15},{4,8},{5,9},{6,10},{7,11},{8,4},{9,5},... | collective-permute-start | bytes 24584 | tf_op jit(solution)/shard_map/ppermute | solution.py:255
  4.7 13.6 %collective-permute-start.1 = (bf16[8,512]{1,0:T(8,128)(2,1)S(1)}, bf16[8,512]{1,0:T(8,128)(2,1)S(1)}, u32[]{:S(2)}, u32[]{:S(2)}) collective-permute-start(bf16[8,512]{1,0:T(8,128)(2,1)S(1)} %get-tuple-element.32), channel_id=1, source_target_pairs={{0,8},{1,9},{2,10},{3,11},{4,12},{5,13},{6,14},{7,15},{8,0},{9,1},... | collective-permute-start | bytes 24584 | tf_op jit(solution)/shard_map/ppermute | solution.py:255
  5.2 13.1 %collective-permute-start = (bf16[8,512]{1,0:T(8,128)(2,1)S(1)}, bf16[8,512]{1,0:T(8,128)(2,1)S(1)}, u32[]{:S(2)}, u32[]{:S(2)}) collective-permute-start(bf16[8,512]{1,0:T(8,128)(2,1)S(1)} %get-tuple-element.32), channel_id=1, source_target_pairs={{0,4},{1,5},{2,6},{3,7},{4,0},{5,1},{6,2},{7,3},{8,12},{9,13},{10,... | collective-permute-start | bytes 24584 | tf_op jit(solution)/shard_map/ppermute | solution.py:255
  6.6 20.0 %all-to-all-start = ((bf16[16,8,512]{2,1,0:T(8,128)(2,1)}), bf16[16,8,512]{2,1,0:T(8,128)(2,1)S(1)}, u32[]{:S(2)}, u32[]{:S(2)}) async-start(bf16[16,8,512]{2,1,0:T(8,128)(2,1)} %broadcast_in_dim.8), calls=%async_computation | async-start | bytes 262144 | tf_op jit(solution)/shard_map/all_to_all | solution.py:242
  18.3 4.5 %collective-permute-start.3 = (bf16[4,8,512]{2,1,0:T(8,128)(2,1)S(1)}, bf16[4,8,512]{2,1,0:T(8,128)(2,1)S(1)}, u32[]{:S(2)}, u32[]{:S(2)}) collective-permute-start(bf16[4,8,512]{2,1,0:T(8,128)(2,1)S(1)} %pad_maximum_fusion.2), channel_id=1, source_target_pairs={{0,2},{1,3},{2,0},{3,1},{4,6},{5,7},{6,4},{7,5},{8,10},{9,11},{10,... | collective-permute-start | bytes 98312 | tf_op jit(solution)/shard_map/ppermute | solution.py:255
  33.9 5.4 %collective-permute-start.5 = (bf16[12,8,512]{2,1,0:T(8,128)(2,1)S(1)}, bf16[12,8,512]{2,1,0:T(8,128)(2,1)S(1)}, u32[]{:S(2)}, u32[]{:S(2)}) collective-permute-start(bf16[12,8,512]{2,1,0:T(8,128)(2,1)S(1)} %get-tuple-element.16), channel_id=1, source_target_pairs={{0,1},{1,0},{2,3},{3,2},{4,5},{5,4},{6,7},{7,6},{8,9},{9,8},{10,11... | collective-permute-start | bytes 294920 | tf_op jit(solution)/shard_map/ppermute | solution.py:255
  39.3 5.3 %collective-permute-start.6 = (bf16[8,8,512]{2,1,0:T(8,128)(2,1)S(1)}, bf16[8,8,512]{2,1,0:T(8,128)(2,1)S(1)}, u32[]{:S(2)}, u32[]{:S(2)}) collective-permute-start(bf16[8,8,512]{2,1,0:T(8,128)(2,1)S(1)} %slice.57), channel_id=1, source_target_pairs={{0,2},{1,3},{2,0},{3,1},{4,6},{5,7},{6,4},{7,5},{8,10},{9,11},{10,... | collective-permute-start | bytes 196616 | tf_op jit(solution)/shard_map/ppermute | solution.py:255
  44.7 10.8 %collective-permute-start.7 = (bf16[2,8,512]{2,1,0:T(8,128)(2,1)S(1)}, bf16[2,8,512]{2,1,0:T(8,128)(2,1)S(1)}, u32[]{:S(2)}, u32[]{:S(2)}) collective-permute-start(bf16[2,8,512]{2,1,0:T(8,128)(2,1)S(1)} %get-tuple-element.36), channel_id=1, source_target_pairs={{0,4},{1,5},{2,6},{3,7},{4,0},{5,1},{6,2},{7,3},{8,12},{9,13},{10,... | collective-permute-start | bytes 49160 | tf_op jit(solution)/shard_map/ppermute | solution.py:255
  46.0 9.5 %collective-permute-start.9 = (bf16[2,8,512]{2,1,0:T(8,128)(2,1)S(1)}, bf16[2,8,512]{2,1,0:T(8,128)(2,1)S(1)}, u32[]{:S(2)}, u32[]{:S(2)}) collective-permute-start(bf16[2,8,512]{2,1,0:T(8,128)(2,1)S(1)} %get-tuple-element.37), channel_id=1, source_target_pairs={{0,12},{1,13},{2,14},{3,15},{4,8},{5,9},{6,10},{7,11},{8,4},{9,5},... | collective-permute-start | bytes 49160 | tf_op jit(solution)/shard_map/ppermute | solution.py:255
  47.8 7.7 %collective-permute-start.8 = (bf16[2,8,512]{2,1,0:T(8,128)(2,1)S(1)}, bf16[2,8,512]{2,1,0:T(8,128)(2,1)S(1)}, u32[]{:S(2)}, u32[]{:S(2)}) collective-permute-start(bf16[2,8,512]{2,1,0:T(8,128)(2,1)S(1)} %get-tuple-element.38), channel_id=1, source_target_pairs={{0,8},{1,9},{2,10},{3,11},{4,12},{5,13},{6,14},{7,15},{8,0},{9,1},... | collective-permute-start | bytes 49160 | tf_op jit(solution)/shard_map/ppermute | solution.py:255
  48.5 16.1 %all-to-all-start.1 = ((bf16[16,8,512]{2,1,0:T(8,128)(2,1)}), bf16[16,8,512]{2,1,0:T(8,128)(2,1)S(1)}, u32[]{:S(2)}, u32[]{:S(2)}) async-start(bf16[16,8,512]{2,1,0:T(8,128)(2,1)} %bitcast.7), calls=%async_computation.1 | async-start | bytes 262144 | tf_op jit(solution)/shard_map/all_to_all | solution.py:242
  58.0 4.0 %collective-permute-start.11 = (bf16[8,512]{1,0:T(8,128)(2,1)S(1)}, bf16[8,512]{1,0:T(8,128)(2,1)S(1)}, u32[]{:S(2)}, u32[]{:S(2)}) collective-permute-start(bf16[8,512]{1,0:T(8,128)(2,1)S(1)} %get-tuple-element.30), channel_id=1, source_target_pairs={{0,8},{1,9},{2,10},{3,11},{4,12},{5,13},{6,14},{7,15},{8,0},{9,1},... | collective-permute-start | bytes 24584 | tf_op jit(solution)/shard_map/ppermute | solution.py:255
  62.0 24.1 %collective-permute-start.13 = (bf16[4,8,512]{2,1,0:T(8,128)(2,1)S(1)}, bf16[4,8,512]{2,1,0:T(8,128)(2,1)S(1)}, u32[]{:S(2)}, u32[]{:S(2)}) collective-permute-start(bf16[4,8,512]{2,1,0:T(8,128)(2,1)S(1)} %pad_maximum_fusion.3), channel_id=1, source_target_pairs={{0,2},{1,3},{2,0},{3,1},{4,6},{5,7},{6,4},{7,5},{8,10},{9,11},{10,... | collective-permute-start | bytes 98312 | tf_op jit(solution)/shard_map/ppermute | solution.py:255
  65.4 16.5 %all-to-all-start.2 = ((bf16[16,16,512]{2,1,0:T(8,128)(2,1)}), bf16[16,16,512]{2,1,0:T(8,128)(2,1)S(1)}, u32[]{:S(2)}, u32[]{:S(2)}) async-start(bf16[16,16,512]{2,1,0:T(8,128)(2,1)} %broadcast_in_dim.9), calls=%async_computation.2 | async-start | bytes 524288 | tf_op jit(solution)/shard_map/all_to_all | solution.py:242
  82.7 9.7 %collective-permute-start.17 = (bf16[8,512]{1,0:T(8,128)(2,1)S(1)}, bf16[8,512]{1,0:T(8,128)(2,1)S(1)}, u32[]{:S(2)}, u32[]{:S(2)}) collective-permute-start(bf16[8,512]{1,0:T(8,128)(2,1)S(1)} %get-tuple-element.27), channel_id=1, source_target_pairs={{0,12},{1,13},{2,14},{3,15},{4,8},{5,9},{6,10},{7,11},{8,4},{9,5},... | collective-permute-start | bytes 24584 | tf_op jit(solution)/shard_map/ppermute | solution.py:255
  84.1 8.3 %collective-permute-start.16 = (bf16[8,512]{1,0:T(8,128)(2,1)S(1)}, bf16[8,512]{1,0:T(8,128)(2,1)S(1)}, u32[]{:S(2)}, u32[]{:S(2)}) collective-permute-start(bf16[8,512]{1,0:T(8,128)(2,1)S(1)} %get-tuple-element.27), channel_id=1, source_target_pairs={{0,8},{1,9},{2,10},{3,11},{4,12},{5,13},{6,14},{7,15},{8,0},{9,1},... | collective-permute-start | bytes 24584 | tf_op jit(solution)/shard_map/ppermute | solution.py:255
  84.8 7.7 %collective-permute-start.15 = (bf16[8,512]{1,0:T(8,128)(2,1)S(1)}, bf16[8,512]{1,0:T(8,128)(2,1)S(1)}, u32[]{:S(2)}, u32[]{:S(2)}) collective-permute-start(bf16[8,512]{1,0:T(8,128)(2,1)S(1)} %get-tuple-element.27), channel_id=1, source_target_pairs={{0,4},{1,5},{2,6},{3,7},{4,0},{5,1},{6,2},{7,3},{8,12},{9,13},{10,... | collective-permute-start | bytes 24584 | tf_op jit(solution)/shard_map/ppermute | solution.py:255
  86.1 8.9 %collective-permute-start.14 = (bf16[8,8,512]{2,1,0:T(8,128)(2,1)S(1)}, bf16[8,8,512]{2,1,0:T(8,128)(2,1)S(1)}, u32[]{:S(2)}, u32[]{:S(2)}) collective-permute-start(bf16[8,8,512]{2,1,0:T(8,128)(2,1)S(1)} %constant_dynamic-update-slice_fusion.5.near_ref), channel_id=1, source_target_pairs={{0,1},{1,0},{2,3},{3,2},{4,5},{5,4},{6,7},{7,6},{8,9},{9,8},{10,11... | collective-permute-start | bytes 196616 | tf_op jit(solution)/shard_map/ppermute | solution.py:255
  104.6 4.7 %collective-permute-start.20 = (bf16[8,8,512]{2,1,0:T(8,128)(2,1)S(1)}, bf16[8,8,512]{2,1,0:T(8,128)(2,1)S(1)}, u32[]{:S(2)}, u32[]{:S(2)}) collective-permute-start(bf16[8,8,512]{2,1,0:T(8,128)(2,1)S(1)} %slice.81), channel_id=1, source_target_pairs={{0,2},{1,3},{2,0},{3,1},{4,6},{5,7},{6,4},{7,5},{8,10},{9,11},{10,... | collective-permute-start | bytes 196616 | tf_op jit(solution)/shard_map/ppermute | solution.py:255
  109.4 7.0 %collective-permute-start.21 = (bf16[2,8,512]{2,1,0:T(8,128)(2,1)S(1)}, bf16[2,8,512]{2,1,0:T(8,128)(2,1)S(1)}, u32[]{:S(2)}, u32[]{:S(2)}) collective-permute-start(bf16[2,8,512]{2,1,0:T(8,128)(2,1)S(1)} %get-tuple-element.33), channel_id=1, source_target_pairs={{0,4},{1,5},{2,6},{3,7},{4,0},{5,1},{6,2},{7,3},{8,12},{9,13},{10,... | collective-permute-start | bytes 49160 | tf_op jit(solution)/shard_map/ppermute | solution.py:255
  110.4 6.0 %collective-permute-start.23 = (bf16[2,8,512]{2,1,0:T(8,128)(2,1)S(1)}, bf16[2,8,512]{2,1,0:T(8,128)(2,1)S(1)}, u32[]{:S(2)}, u32[]{:S(2)}) collective-permute-start(bf16[2,8,512]{2,1,0:T(8,128)(2,1)S(1)} %get-tuple-element.34), channel_id=1, source_target_pairs={{0,12},{1,13},{2,14},{3,15},{4,8},{5,9},{6,10},{7,11},{8,4},{9,5},... | collective-permute-start | bytes 49160 | tf_op jit(solution)/shard_map/ppermute | solution.py:255
  111.6 4.8 %collective-permute-start.22 = (bf16[2,8,512]{2,1,0:T(8,128)(2,1)S(1)}, bf16[2,8,512]{2,1,0:T(8,128)(2,1)S(1)}, u32[]{:S(2)}, u32[]{:S(2)}) collective-permute-start(bf16[2,8,512]{2,1,0:T(8,128)(2,1)S(1)} %get-tuple-element.35), channel_id=1, source_target_pairs={{0,8},{1,9},{2,10},{3,11},{4,12},{5,13},{6,14},{7,15},{8,0},{9,1},... | collective-permute-start | bytes 49160 | tf_op jit(solution)/shard_map/ppermute | solution.py:255
  131.8 4.1 %collective-permute-start.25 = (f32[8,512]{1,0:T(8,128)S(1)}, f32[8,512]{1,0:T(8,128)S(1)}, u32[]{:S(2)}, u32[]{:S(2)}) collective-permute-start(f32[8,512]{1,0:T(8,128)S(1)} %get-tuple-element.39), channel_id=1, source_target_pairs={{0,8},{1,9},{2,10},{3,11},{4,12},{5,13},{6,14},{7,15},{8,0},{9,1},... | collective-permute-start | bytes 49160 | tf_op jit(solution)/shard_map/ppermute | solution.py:255
  135.9 6.2 %collective-permute-start.27 = (f32[4,8,512]{2,1,0:T(8,128)S(1)}, f32[4,8,512]{2,1,0:T(8,128)S(1)}, u32[]{:S(2)}, u32[]{:S(2)}) collective-permute-start(f32[4,8,512]{2,1,0:T(8,128)S(1)} %pad_maximum_fusion.1.near_ref), channel_id=1, source_target_pairs={{0,1},{1,0},{2,3},{3,2},{4,5},{5,4},{6,7},{7,6},{8,9},{9,8},{10,11... | collective-permute-start | bytes 196616 | tf_op jit(solution)/shard_map/ppermute | solution.py:255
  (13 other events, 174.0 us)

commit v4 on v3

--- a/solution.py
+++ b/solution.py
@@ -12,7 +12,7 @@
 STEP = 10
 BLOCK = 64
 SUB = 4
-VMEM_LIMIT = 53 << 20
+VMEM_LIMIT = 32 << 20
 
 learn_rate = 0.05
 beta_one = 0.8
@@ -42,12 +42,10 @@
     return col // X_ONE * 2 + col % 2
 
 
-def slope_kernel(scales, stepped, ids_ref, data_ref, near_ref, far_ref, two_in_ref, *refs):
-    if stepped:
-        near_three_ref, far_three_ref, *refs = refs
-    else:
+def slope_kernel(scales, stepped, ids_ref, data_ref, near_ref, far_ref, two_ref, *refs):
+    if not stepped:
         three_in_ref, *refs = refs
-    (sent_ref, kept_ref, slope_ref, one_ref, three_ref, two_ref, ga_acc, gc_acc) = refs
+    sent_ref, kept_ref, slope_ref, one_ref, three_ref, ga_acc, gc_acc = refs
     step = pl.program_id(0)
     n_slab, own, rank = one_ref.shape
     depth = three_ref.shape[0] * three_ref.shape[1]
@@ -62,12 +60,10 @@
         if stepped:
             for m in range(4):
                 col = here ^ (m * X_ONE)
-                three_ref[third_slab(col)] = near_three_ref[m]
-                three_ref[third_slab(col ^ CORE)] = far_three_ref[m]
+                three_ref[third_slab(col)] = near_ref[8 + m]
+                three_ref[third_slab(col ^ CORE)] = far_ref[8 + m]
         else:
             three_ref[...] = three_in_ref[...]
-        for slab in range(two_ref.shape[0]):
-            two_ref[slab] = two_in_ref[slab][:two_ref.shape[1]]
         gc_acc[...] = jnp.zeros_like(gc_acc)
 
     def run(logistic):
@@ -129,16 +125,15 @@
                 out_ref[8 + m] = (ga_acc[col ^ Y_HI] * scales[0]).astype(bf16)
 
 
-def slopes(ids, tensor, near, far, twos, threes, scales):
+def slopes(ids, tensor, near, far, twos, half_three, scales, stepped):
     rows, depth, cols = tensor.shape
     own, rank = near.shape[1:]
     slabs = rows // own
-    own_two = cols // twos.shape[0]
-    own_three = threes[0].shape[1]
+    threes = half_three.shape
     whole = lambda shape: pl.BlockSpec(shape, lambda i: (0,) * len(shape))
     swapped = (12, own, rank)
     return pl.pallas_call(
-        functools.partial(slope_kernel, scales, len(threes) == 2),
+        functools.partial(slope_kernel, scales, stepped),
         grid=(rows // BLOCK,),
         in_specs=[
             pl.BlockSpec(memory_space=pltpu.SMEM),
@@ -146,32 +141,31 @@
             whole(near.shape),
             whole(far.shape),
             whole(twos.shape),
-            *[whole(x.shape) for x in threes],
+            *([] if stepped else [whole(threes)]),
         ],
         out_specs=[
             whole(swapped),
             whole(swapped),
             pl.BlockSpec((BLOCK, depth, cols), lambda i: (i, 0, 0)),
             whole((slabs, own, rank)),
-            whole((depth // own_three, own_three, rank)),
+            whole(threes),
         ],
         out_shape=[
             jax.ShapeDtypeStruct(swapped, bf16),
             jax.ShapeDtypeStruct(swapped, bf16),
             jax.ShapeDtypeStruct((rows, depth, cols), bf16),
             jax.ShapeDtypeStruct((slabs, own, rank), bf16),
-            jax.ShapeDtypeStruct((depth // own_three, own_three, rank), bf16),
+            jax.ShapeDtypeStruct(threes, bf16),
         ],
         scratch_shapes=[
-            pltpu.VMEM((twos.shape[0], own_two, rank), bf16),
             pltpu.VMEM((slabs, own, rank), f32),
-            pltpu.VMEM((depth // own_three, own_three, rank), f32),
+            pltpu.VMEM(threes, f32),
         ],
         compiler_params=pltpu.CompilerParams(vmem_limit_bytes=VMEM_LIMIT),
         cost_estimate=pl.CostEstimate(
             flops=8 * rows * depth * cols * rank, bytes_accessed=4 << 20, transcendentals=rows * depth * cols
         ),
-    )(ids, tensor, near, far, twos, *threes)
+    )(ids, tensor, near, far, twos, *([] if stepped else [half_three]))
 
 
 def second_kernel(scale, slope_ref, one_ref, three_ref, out_ref, acc):
@@ -259,14 +253,19 @@
     return (left.astype(f32) + right.astype(f32)).astype(bf16)
 
 
-def gather_col(part):
-    half = jnp.stack([part] + [swap(part, m * X_ONE) for m in (1, 2, 3)])
+def gather_x(part):
+    return jnp.stack([part] + [swap(part, m * X_ONE) for m in (1, 2, 3)])
+
+
+def gather_first(part):
+    half = gather_x(part)
     near = jnp.concatenate([half, swap(half, Y_HI)])
     return near, swap(near, CORE)
 
 
-def gather_third(part):
-    near = jnp.stack([part] + [swap(part, m * X_ONE) for m in (1, 2, 3)])
+def gather_both(part_one, part_three):
+    half = gather_x(jnp.stack([part_one, part_three]))
+    near = jnp.concatenate([half[:, 0], swap(half[:, 0], Y_HI), half[:, 1]])
     return near, swap(near, CORE)
 
 
@@ -319,38 +318,32 @@
     part_three, first_three, second_three = mine(factor_three), mine(first_three), mine(second_three)
     start_one, start_two, start_three = (factor_one, factor_two, part_three)
     twos = swap_all(to_all(factor_two.astype(bf16), n_row), "row")
-    near, far = gather_col(factor_one.astype(bf16))
-    threes = (factor_three.astype(bf16).reshape(tile_depth // deep, deep, rank),)
+    near, far = gather_first(factor_one.astype(bf16))
+    threes = factor_three.astype(bf16).reshape(tile_depth // deep, deep, rank)
     for iteration in range(ITERS):
-        last = iteration == ITERS - 1
         counter = STEP + iteration + 1
-        sent, kept, slope, ones, all_threes = slopes(ids, tensor, near, far, twos, threes, scales)
-        grad_two = second_grad(slope, ones, all_threes, scales[1]).reshape(n_row, own_two, rank)
-        both = plus(kept, swap(sent, CORE))
-        if not last:
-            both, grad_two = lax.optimization_barrier((both, grad_two))
-        grad_one, grad_three = reduce_col(both)
+        sent, kept, slope, ones, threes = slopes(
+            ids, tensor, near, far, twos, threes, scales, iteration > 0
+        )
+        grad_two = second_grad(slope, ones, threes, scales[1]).reshape(n_row, own_two, rank)
+        grad_one, grad_three = reduce_col(plus(kept, swap(sent, CORE)))
+        sent = jnp.concatenate([grad_two, to_all(grad_three.astype(bf16), n_row)], axis=1)
         factor_one, first_one, second_one = adam_step(factor_one, first_one, second_one, grad_one, counter)
-        grad_three = grad_three.astype(bf16)
-        if last:
-            sent = jnp.concatenate([grad_two, to_all(grad_three, n_row)], axis=1)
-            got = total(swap_all(sent, "row"))
-            grad_two, grad_three = got[:own_two], got[own_two:]
-        else:
-            grad_two = total(swap_all(grad_two, "row"))
-        factor_two, first_two, second_two = adam_step(factor_two, first_two, second_two, grad_two, counter)
-        if not last:
-            near, far = gather_col(factor_one.astype(bf16))
-            sent = jnp.concatenate([factor_two.astype(bf16), grad_three])
-            twos = swap_all(to_all(sent, n_row), "row")
-            grad_three = total(twos[:, own_two:])
+        got = total(swap_all(sent, "row"))
+        grad_two, grad_three = got[:own_two], got[own_two:]
         part_three, first_three, second_three = adam_step(
             part_three, first_three, second_three, grad_three, counter
         )
-        if not last:
-            threes = gather_third(part_three.astype(bf16))
+        if iteration < ITERS - 1:
+            near, far = gather_both(factor_one.astype(bf16), part_three.astype(bf16))
+        else:
+            near = gather_x((start_three - part_three) / (learn_rate * ITERS))
+            near, grad_two = lax.optimization_barrier((near, grad_two))
+        factor_two, first_two, second_two = adam_step(factor_two, first_two, second_two, grad_two, counter)
+        if iteration < ITERS - 1:
+            twos = swap_all(to_all(factor_two.astype(bf16), n_row), "row")
     spread = learn_rate * ITERS
-    new_three = place_third(ids, *gather_third((start_three - part_three) / spread)).reshape(tile_depth, rank)
+    new_three = place_third(ids, near, swap(near, CORE)).reshape(tile_depth, rank)
     return ((start_one - factor_one) / spread, (start_two - factor_two) / spread, new_three)
 
 

time: 144 us -> 137 us (0.951)
  Pallas kernels: 24 us -> 17 us
  starting transfers between devices: 72.8 us -> 69.1 us
  blocking collectives: 12.2 us -> 14.8 us
  local copies, waits for them, and re-layouts: 2.68 us -> 4.22 us
    pallas_call x2, Pallas kernels: 8.02 us -> 4.08 us  [second_grad(): pl.pallas_call(functools.partial(second_kernel, scale), grid=(rows // blo...]
    all_to_all x3, starting transfers between devices: 23.5 us -> 20.1 us  [swap_all(): return lax.all_to_all(parts, axis, 0, 0)]
    pallas_call x2, Pallas kernels: 14.7 us -> 11.6 us  [slopes(): pl.pallas_call(functools.partial(slope_kernel, scales, stepped), grid=(ro...]
    all_to_all x1, blocking collectives: 12.2 us -> 14.8 us  [swap_all(): return lax.all_to_all(parts, axis, 0, 0)]
    unnamed x18 -> x19, local copies, waits for them, and re-layouts: 0.04 us -> 1.63 us
    ppermute x28 -> x24, waiting for transfers between devices: 14.9 us -> 14.2 us  [swap(): return lax.ppermute(part, 'col', [(i, i ^ code) for i in range(size)])]
    ppermute x28 -> x24, starting transfers between devices: 49.3 us -> 48.9 us  [swap(): return lax.ppermute(part, 'col', [(i, i ^ code) for i in range(size)])]
  transfers between devices with their start and end apart: 31 -> 27, of which waited for: 12 -> 13; matrix products, arithmetic and copies ran while one was open for 5% -> 4% of each run, Pallas kernels for 6% -> 3%
where the time goes in v4:
time: 137 us; the launch traced here: 136 us
  starting transfers between devices  69.1 us (50%)
  waiting for transfers between devices  23.9 us (17%)
  Pallas kernels  17 us (12%)
  blocking collectives  14.8 us (11%)
  other arithmetic  6.3 us (5%)
  local copies, waits for them, and re-layouts  4.22 us (3%)
    ppermute x24, starting transfers between devices, swap(): return lax.ppermute(part, 'col', [(i, i ^ code) for i in range(size)])  48.9 us
    all_to_all x3, starting transfers between devices, swap_all(): return lax.all_to_all(parts, axis, 0, 0)  20.1 us
    all_to_all x1, blocking collectives, swap_all(): return lax.all_to_all(parts, axis, 0, 0)  14.8 us
    ppermute x24, waiting for transfers between devices, swap(): return lax.ppermute(part, 'col', [(i, i ^ code) for i in range(size)])  14.2 us
    pallas_call x2, Pallas kernels, slopes(): pl.pallas_call(functools.partial(slope_kernel, scales, stepped), grid=(ro...  11.6 us
    all_to_all x3, waiting for transfers between devices, swap_all(): return lax.all_to_all(parts, axis, 0, 0)  9.69 us
    pallas_call x2, Pallas kernels, second_grad(): pl.pallas_call(functools.partial(second_kernel, scale), grid=(rows // blo...  4.08 us
  transfers between devices with their start and end apart: 27, of which 13 were waited for; matrix products, arithmetic and copies ran while one was open for 4% of the time, Pallas kernels for 3%

profile of v4, /device:TPU:1, one launch (start us, length us, event | category | flops | bytes accessed | tf_op | source)
XLA Modules:
  0.0 136.3 jit_solution(7640817488203668884)
XLA Ops:
  1.4 3.3 %collective-permute-start.2 = (bf16[8,512]{1,0:T(8,128)(2,1)S(1)}, bf16[8,512]{1,0:T(8,128)(2,1)S(1)}, u32[]{:S(2)}, u32[]{:S(2)}) collective-permute-start(bf16[8,512]{1,0:T(8,128)(2,1)S(1)} %get-tuple-element.30), channel_id=1, source_target_pairs={{0,12},{1,13},{2,14},{3,15},{4,8},{5,9},{6,10},{7,11},{8,4},{9,5},... | collective-permute-start | bytes 24584 | tf_op jit(solution)/shard_map/ppermute | solution.py:249
  6.6 9.5 %all-to-all-start = ((bf16[16,8,512]{2,1,0:T(8,128)(2,1)}), bf16[16,8,512]{2,1,0:T(8,128)(2,1)S(1)}, u32[]{:S(2)}, u32[]{:S(2)}) async-start(bf16[16,8,512]{2,1,0:T(8,128)(2,1)} %broadcast_in_dim.12), calls=%async_computation | async-start | bytes 262144 | tf_op jit(solution)/shard_map/all_to_all | solution.py:236
  18.3 2.7 %collective-permute-start.3 = (bf16[4,8,512]{2,1,0:T(8,128)(2,1)S(1)}, bf16[4,8,512]{2,1,0:T(8,128)(2,1)S(1)}, u32[]{:S(2)}, u32[]{:S(2)}) collective-permute-start(bf16[4,8,512]{2,1,0:T(8,128)(2,1)S(1)} %pad_maximum_fusion.5), channel_id=1, source_target_pairs={{0,2},{1,3},{2,0},{3,1},{4,6},{5,7},{6,4},{7,5},{8,10},{9,11},{10,... | collective-permute-start | bytes 98312 | tf_op jit(solution)/shard_map/ppermute | solution.py:249
  21.0 1.8 %collective-permute-done.3 = bf16[4,8,512]{2,1,0:T(8,128)(2,1)S(1)} collective-permute-done((bf16[4,8,512]{2,1,0:T(8,128)(2,1)S(1)}, bf16[4,8,512]{2,1,0:T(8,128)(2,1)S(1)}, u32[]{:S(2)}, u32[]{:S(2)}) %collective-permute-start.3) | collective-permute-done | bytes 32800 | tf_op jit(solution)/shard_map/ppermute | solution.py:249
  22.8 2.9 %collective-permute-start.4 = (bf16[8,8,512]{2,1,0:T(8,128)(2,1)S(1)}, bf16[8,8,512]{2,1,0:T(8,128)(2,1)S(1)}, u32[]{:S(2)}, u32[]{:S(2)}) collective-permute-start(bf16[8,8,512]{2,1,0:T(8,128)(2,1)S(1)} %constant_dynamic-update-slice_fusion.near_ref), channel_id=1, source_target_pairs={{0,1},{1,0},{2,3},{3,2},{4,5},{5,4},{6,7},{7,6},{8,9},{9,8},{10,11... | collective-permute-start | bytes 196616 | tf_op jit(solution)/shard_map/ppermute | solution.py:249
  28.2 5.8 %shard_map.130 = (bf16[12,8,512]{2,1,0:T(8,128)(2,1)S(1)}, bf16[12,8,512]{2,1,0:T(8,128)(2,1)S(1)}, bf16[128,64,128]{2,1,0:T(8,128)(2,1)S(1)}, bf16[16,8,512]{2,1,0:T(8,128)(2,1)S(1)}, bf16[8,8,512]{2,1,0:T(8,128)(2,1)S(1)}) custom-call(s32[2]{0:T(128)S(1)} %pad_add_fusion.ids_ref, bf16[128,64,128]{2,1,0:T(8,128)(2,1)S(1)} %copy-done, ...), custom_call_target="tpu_custom_call" | custom-call | flops 4294967296 | bytes 4194304 | tf_op jit(solution)/shard_map/pallas_call | solution.py:135
  36.0 2.9 %collective-permute-start.6 = (bf16[8,8,512]{2,1,0:T(8,128)(2,1)S(1)}, bf16[8,8,512]{2,1,0:T(8,128)(2,1)S(1)}, u32[]{:S(2)}, u32[]{:S(2)}) collective-permute-start(bf16[8,8,512]{2,1,0:T(8,128)(2,1)S(1)} %slice.87), channel_id=1, source_target_pairs={{0,2},{1,3},{2,0},{3,1},{4,6},{5,7},{6,4},{7,5},{8,10},{9,11},{10,... | collective-permute-start | bytes 196616 | tf_op jit(solution)/shard_map/ppermute | solution.py:249
  38.9 1.8 %collective-permute-done.6.got_ref = bf16[8,8,512]{2,1,0:T(8,128)(2,1)S(1)} collective-permute-done((bf16[8,8,512]{2,1,0:T(8,128)(2,1)S(1)}, bf16[8,8,512]{2,1,0:T(8,128)(2,1)S(1)}, u32[]{:S(2)}, u32[]{:S(2)}) %collective-permute-start.6) | collective-permute-done | bytes 65568 | tf_op jit(solution)/shard_map/ppermute | solution.py:249
  42.1 1.8 %collective-permute-start.9 = (bf16[2,8,512]{2,1,0:T(8,128)(2,1)S(1)}, bf16[2,8,512]{2,1,0:T(8,128)(2,1)S(1)}, u32[]{:S(2)}, u32[]{:S(2)}) collective-permute-start(bf16[2,8,512]{2,1,0:T(8,128)(2,1)S(1)} %get-tuple-element.37), channel_id=1, source_target_pairs={{0,12},{1,13},{2,14},{3,15},{4,8},{5,9},{6,10},{7,11},{8,4},{9,5},... | collective-permute-start | bytes 49160 | tf_op jit(solution)/shard_map/ppermute | solution.py:249
  44.6 2.0 %shard_map.132 = bf16[128,512]{1,0:T(8,128)(2,1)S(1)} custom-call(bf16[128,64,128]{2,1,0:T(8,128)(2,1)S(1)} %get-tuple-element.17.slope_ref, bf16[16,8,512]{2,1,0:T(8,128)(2,1)S(1)} %get-tuple-element.18.one_ref, bf16[8,8,512]{2,1,0:T(8,128)(2,1)S(1)} %get-tuple-element.19.three_ref), custom_call_target="tpu_custom_call" | custom-call | flops 2147483648 | bytes 2097152 | tf_op jit(solution)/shard_map/pallas_call | solution.py:199
  48.8 7.1 %all-to-all-start.1 = ((bf16[16,16,512]{2,1,0:T(8,128)(2,1)}), bf16[16,16,512]{2,1,0:T(8,128)(2,1)S(1)}, u32[]{:S(2)}, u32[]{:S(2)}) async-start(bf16[16,16,512]{2,1,0:T(8,128)(2,1)} %pad_maximum_fusion), calls=%async_computation.1 | async-start | bytes 524288 | tf_op jit(solution)/shard_map/all_to_all | solution.py:236
  56.0 9.7 %all-to-all-done.1 = bf16[16,16,512]{2,1,0:T(8,128)(2,1)S(1)} async-done(((bf16[16,16,512]{2,1,0:T(8,128)(2,1)}), bf16[16,16,512]{2,1,0:T(8,128)(2,1)S(1)}, u32[]{:S(2)}, u32[]{:S(2)}) %all-to-all-start.1) | async-done | bytes 262176 | tf_op jit(solution)/shard_map/all_to_all | solution.py:236
  70.7 3.5 %all-to-all-start.2 = ((bf16[16,8,512]{2,1,0:T(8,128)(2,1)}), bf16[16,8,512]{2,1,0:T(8,128)(2,1)S(1)}, u32[]{:S(2)}, u32[]{:S(2)}) async-start(bf16[16,8,512]{2,1,0:T(8,128)(2,1)} %broadcast_in_dim.15), calls=%async_computation.2 | async-start | bytes 262144 | tf_op jit(solution)/shard_map/all_to_all | solution.py:236
  74.3 2.9 %collective-permute-start.13 = (bf16[4,8,512]{2,1,0:T(8,128)(2,1)S(1)}, bf16[4,8,512]{2,1,0:T(8,128)(2,1)S(1)}, u32[]{:S(2)}, u32[]{:S(2)}) collective-permute-start(bf16[4,8,512]{2,1,0:T(8,128)(2,1)S(1)} %get-tuple-element.34), channel_id=1, source_target_pairs={{0,2},{1,3},{2,0},{3,1},{4,6},{5,7},{6,4},{7,5},{8,10},{9,11},{10,... | collective-permute-start | bytes 98312 | tf_op jit(solution)/shard_map/ppermute | solution.py:249
  78.7 6.6 %collective-permute-start.14 = (bf16[12,8,512]{2,1,0:T(8,128)(2,1)S(1)}, bf16[12,8,512]{2,1,0:T(8,128)(2,1)S(1)}, u32[]{:S(2)}, u32[]{:S(2)}) collective-permute-start(bf16[12,8,512]{2,1,0:T(8,128)(2,1)S(1)} %pad_maximum_fusion.2.near_ref), channel_id=1, source_target_pairs={{0,1},{1,0},{2,3},{3,2},{4,5},{5,4},{6,7},{7,6},{8,9},{9,8},{10,11... | collective-permute-start | bytes 294920 | tf_op jit(solution)/shard_map/ppermute | solution.py:249
  86.2 5.8 %shard_map.133 = (bf16[12,8,512]{2,1,0:T(8,128)(2,1)S(1)}, bf16[12,8,512]{2,1,0:T(8,128)(2,1)S(1)}, bf16[128,64,128]{2,1,0:T(8,128)(2,1)S(1)}, bf16[16,8,512]{2,1,0:T(8,128)(2,1)S(1)}, bf16[8,8,512]{2,1,0:T(8,128)(2,1)S(1)}) custom-call(s32[2]{0:T(128)S(1)} %pad_add_fusion.ids_ref, bf16[128,64,128]{2,1,0:T(8,128)(2,1)S(1)} %copy-done.1, ...), custom_call_target="tpu_custom_call" | custom-call | flops 4294967296 | bytes 4194304 | tf_op jit(solution)/shard_map/pallas_call | solution.py:135
  92.1 3.1 %collective-permute-start.15 = (bf16[12,8,512]{2,1,0:T(8,128)(2,1)S(1)}, bf16[12,8,512]{2,1,0:T(8,128)(2,1)S(1)}, u32[]{:S(2)}, u32[]{:S(2)}) collective-permute-start(bf16[12,8,512]{2,1,0:T(8,128)(2,1)S(1)} %get-tuple-element.21), channel_id=1, source_target_pairs={{0,1},{1,0},{2,3},{3,2},{4,5},{5,4},{6,7},{7,6},{8,9},{9,8},{10,11... | collective-permute-start | bytes 294920 | tf_op jit(solution)/shard_map/ppermute | solution.py:249
  96.1 3.0 %collective-permute-start.16 = (bf16[8,8,512]{2,1,0:T(8,128)(2,1)S(1)}, bf16[8,8,512]{2,1,0:T(8,128)(2,1)S(1)}, u32[]{:S(2)}, u32[]{:S(2)}) collective-permute-start(bf16[8,8,512]{2,1,0:T(8,128)(2,1)S(1)} %slice.98), channel_id=1, source_target_pairs={{0,2},{1,3},{2,0},{3,1},{4,6},{5,7},{6,4},{7,5},{8,10},{9,11},{10,... | collective-permute-start | bytes 196616 | tf_op jit(solution)/shard_map/ppermute | solution.py:249
  102.1 2.1 %collective-permute-start.18 = (bf16[2,8,512]{2,1,0:T(8,128)(2,1)S(1)}, bf16[2,8,512]{2,1,0:T(8,128)(2,1)S(1)}, u32[]{:S(2)}, u32[]{:S(2)}) collective-permute-start(bf16[2,8,512]{2,1,0:T(8,128)(2,1)S(1)} %get-tuple-element.33), channel_id=1, source_target_pairs={{0,8},{1,9},{2,10},{3,11},{4,12},{5,13},{6,14},{7,15},{8,0},{9,1},... | collective-permute-start | bytes 49160 | tf_op jit(solution)/shard_map/ppermute | solution.py:249
  104.2 2.0 %shard_map.135 = bf16[128,512]{1,0:T(8,128)(2,1)S(1)} custom-call(bf16[128,64,128]{2,1,0:T(8,128)(2,1)S(1)} %get-tuple-element.22.slope_ref, bf16[16,8,512]{2,1,0:T(8,128)(2,1)S(1)} %get-tuple-element.23.one_ref, bf16[8,8,512]{2,1,0:T(8,128)(2,1)S(1)} %get-tuple-element.24.three_ref), custom_call_target="tpu_custom_call" | custom-call | flops 2147483648 | bytes 2097152 | tf_op jit(solution)/shard_map/pallas_call | solution.py:199
  106.4 14.8 %all_to_all.20 = bf16[16,16,512]{2,1,0:T(8,128)(2,1)S(1)} all-to-all(bf16[16,16,512]{2,1,0:T(8,128)(2,1)S(1)} %pad_maximum_fusion.1), channel_id=1, replica_groups=mesh['row'=16,'col'=16] {'row'}, dimensions={0} | all-to-all | bytes 524288 | tf_op jit(solution)/shard_map/all_to_all | solution.py:236
  122.0 2.0 %collective-permute-start.22 = (f32[8,512]{1,0:T(8,128)S(1)}, f32[8,512]{1,0:T(8,128)S(1)}, u32[]{:S(2)}, u32[]{:S(2)}) collective-permute-start(f32[8,512]{1,0:T(8,128)S(1)} %get-tuple-element.40), channel_id=1, source_target_pairs={{0,12},{1,13},{2,14},{3,15},{4,8},{5,9},{6,10},{7,11},{8,4},{9,5},... | collective-permute-start | bytes 49160 | tf_op jit(solution)/shard_map/ppermute | solution.py:249
  125.9 2.2 %collective-permute-done.21 = f32[8,512]{1,0:T(8,128)S(1)} collective-permute-done((f32[8,512]{1,0:T(8,128)S(1)}, f32[8,512]{1,0:T(8,128)S(1)}, u32[]{:S(2)}, u32[]{:S(2)}) %collective-permute-start.21) | collective-permute-done | bytes 16416 | tf_op jit(solution)/shard_map/ppermute | solution.py:249
  128.1 6.0 %collective-permute-start.23 = (f32[4,8,512]{2,1,0:T(8,128)S(1)}, f32[4,8,512]{2,1,0:T(8,128)S(1)}, u32[]{:S(2)}, u32[]{:S(2)}) collective-permute-start(f32[4,8,512]{2,1,0:T(8,128)S(1)} %pad_maximum_fusion.4.near_ref), channel_id=1, source_target_pairs={{0,1},{1,0},{2,3},{3,2},{4,5},{5,4},{6,7},{7,6},{8,9},{9,8},{10,11... | collective-permute-start | bytes 196616 | tf_op jit(solution)/shard_map/ppermute | solution.py:249
  (91 shorter events, 29.7 us)
Async XLA Ops:
  1.4 16.9 %collective-permute-start.2 = (bf16[8,512]{1,0:T(8,128)(2,1)S(1)}, bf16[8,512]{1,0:T(8,128)(2,1)S(1)}, u32[]{:S(2)}, u32[]{:S(2)}) collective-permute-start(bf16[8,512]{1,0:T(8,128)(2,1)S(1)} %get-tuple-element.30), channel_id=1, source_target_pairs={{0,12},{1,13},{2,14},{3,15},{4,8},{5,9},{6,10},{7,11},{8,4},{9,5},... | collective-permute-start | bytes 24584 | tf_op jit(solution)/shard_map/ppermute | solution.py:249
  4.7 13.6 %collective-permute-start.1 = (bf16[8,512]{1,0:T(8,128)(2,1)S(1)}, bf16[8,512]{1,0:T(8,128)(2,1)S(1)}, u32[]{:S(2)}, u32[]{:S(2)}) collective-permute-start(bf16[8,512]{1,0:T(8,128)(2,1)S(1)} %get-tuple-element.30), channel_id=1, source_target_pairs={{0,8},{1,9},{2,10},{3,11},{4,12},{5,13},{6,14},{7,15},{8,0},{9,1},... | collective-permute-start | bytes 24584 | tf_op jit(solution)/shard_map/ppermute | solution.py:249
  5.2 13.1 %collective-permute-start = (bf16[8,512]{1,0:T(8,128)(2,1)S(1)}, bf16[8,512]{1,0:T(8,128)(2,1)S(1)}, u32[]{:S(2)}, u32[]{:S(2)}) collective-permute-start(bf16[8,512]{1,0:T(8,128)(2,1)S(1)} %get-tuple-element.30), channel_id=1, source_target_pairs={{0,4},{1,5},{2,6},{3,7},{4,0},{5,1},{6,2},{7,3},{8,12},{9,13},{10,... | collective-permute-start | bytes 24584 | tf_op jit(solution)/shard_map/ppermute | solution.py:249
  6.6 20.0 %all-to-all-start = ((bf16[16,8,512]{2,1,0:T(8,128)(2,1)}), bf16[16,8,512]{2,1,0:T(8,128)(2,1)S(1)}, u32[]{:S(2)}, u32[]{:S(2)}) async-start(bf16[16,8,512]{2,1,0:T(8,128)(2,1)} %broadcast_in_dim.12), calls=%async_computation | async-start | bytes 262144 | tf_op jit(solution)/shard_map/all_to_all | solution.py:236
  18.3 4.5 %collective-permute-start.3 = (bf16[4,8,512]{2,1,0:T(8,128)(2,1)S(1)}, bf16[4,8,512]{2,1,0:T(8,128)(2,1)S(1)}, u32[]{:S(2)}, u32[]{:S(2)}) collective-permute-start(bf16[4,8,512]{2,1,0:T(8,128)(2,1)S(1)} %pad_maximum_fusion.5), channel_id=1, source_target_pairs={{0,2},{1,3},{2,0},{3,1},{4,6},{5,7},{6,4},{7,5},{8,10},{9,11},{10,... | collective-permute-start | bytes 98312 | tf_op jit(solution)/shard_map/ppermute | solution.py:249
  36.0 4.7 %collective-permute-start.6 = (bf16[8,8,512]{2,1,0:T(8,128)(2,1)S(1)}, bf16[8,8,512]{2,1,0:T(8,128)(2,1)S(1)}, u32[]{:S(2)}, u32[]{:S(2)}) collective-permute-start(bf16[8,8,512]{2,1,0:T(8,128)(2,1)S(1)} %slice.87), channel_id=1, source_target_pairs={{0,2},{1,3},{2,0},{3,1},{4,6},{5,7},{6,4},{7,5},{8,10},{9,11},{10,... | collective-permute-start | bytes 196616 | tf_op jit(solution)/shard_map/ppermute | solution.py:249
  40.8 5.9 %collective-permute-start.7 = (bf16[2,8,512]{2,1,0:T(8,128)(2,1)S(1)}, bf16[2,8,512]{2,1,0:T(8,128)(2,1)S(1)}, u32[]{:S(2)}, u32[]{:S(2)}) collective-permute-start(bf16[2,8,512]{2,1,0:T(8,128)(2,1)S(1)} %get-tuple-element.36), channel_id=1, source_target_pairs={{0,4},{1,5},{2,6},{3,7},{4,0},{5,1},{6,2},{7,3},{8,12},{9,13},{10,... | collective-permute-start | bytes 49160 | tf_op jit(solution)/shard_map/ppermute | solution.py:249
  42.1 4.6 %collective-permute-start.9 = (bf16[2,8,512]{2,1,0:T(8,128)(2,1)S(1)}, bf16[2,8,512]{2,1,0:T(8,128)(2,1)S(1)}, u32[]{:S(2)}, u32[]{:S(2)}) collective-permute-start(bf16[2,8,512]{2,1,0:T(8,128)(2,1)S(1)} %get-tuple-element.37), channel_id=1, source_target_pairs={{0,12},{1,13},{2,14},{3,15},{4,8},{5,9},{6,10},{7,11},{8,4},{9,5},... | collective-permute-start | bytes 49160 | tf_op jit(solution)/shard_map/ppermute | solution.py:249
  43.9 4.1 %collective-permute-start.8 = (bf16[2,8,512]{2,1,0:T(8,128)(2,1)S(1)}, bf16[2,8,512]{2,1,0:T(8,128)(2,1)S(1)}, u32[]{:S(2)}, u32[]{:S(2)}) collective-permute-start(bf16[2,8,512]{2,1,0:T(8,128)(2,1)S(1)} %get-tuple-element.38), channel_id=1, source_target_pairs={{0,8},{1,9},{2,10},{3,11},{4,12},{5,13},{6,14},{7,15},{8,0},{9,1},... | collective-permute-start | bytes 49160 | tf_op jit(solution)/shard_map/ppermute | solution.py:249
  48.8 16.9 %all-to-all-start.1 = ((bf16[16,16,512]{2,1,0:T(8,128)(2,1)}), bf16[16,16,512]{2,1,0:T(8,128)(2,1)S(1)}, u32[]{:S(2)}, u32[]{:S(2)}) async-start(bf16[16,16,512]{2,1,0:T(8,128)(2,1)} %pad_maximum_fusion), calls=%async_computation.1 | async-start | bytes 524288 | tf_op jit(solution)/shard_map/all_to_all | solution.py:236
  66.5 7.7 %collective-permute-start.11 = (bf16[2,8,512]{2,1,0:T(8,128)(2,1)S(1)}, bf16[2,8,512]{2,1,0:T(8,128)(2,1)S(1)}, u32[]{:S(2)}, u32[]{:S(2)}) collective-permute-start(bf16[2,8,512]{2,1,0:T(8,128)(2,1)S(1)} %get-tuple-element.43), channel_id=1, source_target_pairs={{0,8},{1,9},{2,10},{3,11},{4,12},{5,13},{6,14},{7,15},{8,0},{9,1},... | collective-permute-start | bytes 49160 | tf_op jit(solution)/shard_map/ppermute | solution.py:249
  67.7 6.6 %collective-permute-start.10 = (bf16[2,8,512]{2,1,0:T(8,128)(2,1)S(1)}, bf16[2,8,512]{2,1,0:T(8,128)(2,1)S(1)}, u32[]{:S(2)}, u32[]{:S(2)}) collective-permute-start(bf16[2,8,512]{2,1,0:T(8,128)(2,1)S(1)} %get-tuple-element.43), channel_id=1, source_target_pairs={{0,4},{1,5},{2,6},{3,7},{4,0},{5,1},{6,2},{7,3},{8,12},{9,13},{10,... | collective-permute-start | bytes 49160 | tf_op jit(solution)/shard_map/ppermute | solution.py:249
  68.4 5.9 %collective-permute-start.12 = (bf16[2,8,512]{2,1,0:T(8,128)(2,1)S(1)}, bf16[2,8,512]{2,1,0:T(8,128)(2,1)S(1)}, u32[]{:S(2)}, u32[]{:S(2)}) collective-permute-start(bf16[2,8,512]{2,1,0:T(8,128)(2,1)S(1)} %get-tuple-element.43), channel_id=1, source_target_pairs={{0,12},{1,13},{2,14},{3,15},{4,8},{5,9},{6,10},{7,11},{8,4},{9,5},... | collective-permute-start | bytes 49160 | tf_op jit(solution)/shard_map/ppermute | solution.py:249
  70.7 15.5 %all-to-all-start.2 = ((bf16[16,8,512]{2,1,0:T(8,128)(2,1)}), bf16[16,8,512]{2,1,0:T(8,128)(2,1)S(1)}, u32[]{:S(2)}, u32[]{:S(2)}) async-start(bf16[16,8,512]{2,1,0:T(8,128)(2,1)} %broadcast_in_dim.15), calls=%async_computation.2 | async-start | bytes 262144 | tf_op jit(solution)/shard_map/all_to_all | solution.py:236
  74.3 4.4 %collective-permute-start.13 = (bf16[4,8,512]{2,1,0:T(8,128)(2,1)S(1)}, bf16[4,8,512]{2,1,0:T(8,128)(2,1)S(1)}, u32[]{:S(2)}, u32[]{:S(2)}) collective-permute-start(bf16[4,8,512]{2,1,0:T(8,128)(2,1)S(1)} %get-tuple-element.34), channel_id=1, source_target_pairs={{0,2},{1,3},{2,0},{3,1},{4,6},{5,7},{6,4},{7,5},{8,10},{9,11},{10,... | collective-permute-start | bytes 98312 | tf_op jit(solution)/shard_map/ppermute | solution.py:249
  78.7 7.6 %collective-permute-start.14 = (bf16[12,8,512]{2,1,0:T(8,128)(2,1)S(1)}, bf16[12,8,512]{2,1,0:T(8,128)(2,1)S(1)}, u32[]{:S(2)}, u32[]{:S(2)}) collective-permute-start(bf16[12,8,512]{2,1,0:T(8,128)(2,1)S(1)} %pad_maximum_fusion.2.near_ref), channel_id=1, source_target_pairs={{0,1},{1,0},{2,3},{3,2},{4,5},{5,4},{6,7},{7,6},{8,9},{9,8},{10,11... | collective-permute-start | bytes 294920 | tf_op jit(solution)/shard_map/ppermute | solution.py:249
  92.1 4.0 %collective-permute-start.15 = (bf16[12,8,512]{2,1,0:T(8,128)(2,1)S(1)}, bf16[12,8,512]{2,1,0:T(8,128)(2,1)S(1)}, u32[]{:S(2)}, u32[]{:S(2)}) collective-permute-start(bf16[12,8,512]{2,1,0:T(8,128)(2,1)S(1)} %get-tuple-element.21), channel_id=1, source_target_pairs={{0,1},{1,0},{2,3},{3,2},{4,5},{5,4},{6,7},{7,6},{8,9},{9,8},{10,11... | collective-permute-start | bytes 294920 | tf_op jit(solution)/shard_map/ppermute | solution.py:249
  96.1 4.7 %collective-permute-start.16 = (bf16[8,8,512]{2,1,0:T(8,128)(2,1)S(1)}, bf16[8,8,512]{2,1,0:T(8,128)(2,1)S(1)}, u32[]{:S(2)}, u32[]{:S(2)}) collective-permute-start(bf16[8,8,512]{2,1,0:T(8,128)(2,1)S(1)} %slice.98), channel_id=1, source_target_pairs={{0,2},{1,3},{2,0},{3,1},{4,6},{5,7},{6,4},{7,5},{8,10},{9,11},{10,... | collective-permute-start | bytes 196616 | tf_op jit(solution)/shard_map/ppermute | solution.py:249
  100.9 5.4 %collective-permute-start.17 = (bf16[2,8,512]{2,1,0:T(8,128)(2,1)S(1)}, bf16[2,8,512]{2,1,0:T(8,128)(2,1)S(1)}, u32[]{:S(2)}, u32[]{:S(2)}) collective-permute-start(bf16[2,8,512]{2,1,0:T(8,128)(2,1)S(1)} %get-tuple-element.31), channel_id=1, source_target_pairs={{0,4},{1,5},{2,6},{3,7},{4,0},{5,1},{6,2},{7,3},{8,12},{9,13},{10,... | collective-permute-start | bytes 49160 | tf_op jit(solution)/shard_map/ppermute | solution.py:249
  101.3 5.0 %collective-permute-start.19 = (bf16[2,8,512]{2,1,0:T(8,128)(2,1)S(1)}, bf16[2,8,512]{2,1,0:T(8,128)(2,1)S(1)}, u32[]{:S(2)}, u32[]{:S(2)}) collective-permute-start(bf16[2,8,512]{2,1,0:T(8,128)(2,1)S(1)} %get-tuple-element.32), channel_id=1, source_target_pairs={{0,12},{1,13},{2,14},{3,15},{4,8},{5,9},{6,10},{7,11},{8,4},{9,5},... | collective-permute-start | bytes 49160 | tf_op jit(solution)/shard_map/ppermute | solution.py:249
  102.1 4.2 %collective-permute-start.18 = (bf16[2,8,512]{2,1,0:T(8,128)(2,1)S(1)}, bf16[2,8,512]{2,1,0:T(8,128)(2,1)S(1)}, u32[]{:S(2)}, u32[]{:S(2)}) collective-permute-start(bf16[2,8,512]{2,1,0:T(8,128)(2,1)S(1)} %get-tuple-element.33), channel_id=1, source_target_pairs={{0,8},{1,9},{2,10},{3,11},{4,12},{5,13},{6,14},{7,15},{8,0},{9,1},... | collective-permute-start | bytes 49160 | tf_op jit(solution)/shard_map/ppermute | solution.py:249
  122.0 3.9 %collective-permute-start.22 = (f32[8,512]{1,0:T(8,128)S(1)}, f32[8,512]{1,0:T(8,128)S(1)}, u32[]{:S(2)}, u32[]{:S(2)}) collective-permute-start(f32[8,512]{1,0:T(8,128)S(1)} %get-tuple-element.40), channel_id=1, source_target_pairs={{0,12},{1,13},{2,14},{3,15},{4,8},{5,9},{6,10},{7,11},{8,4},{9,5},... | collective-permute-start | bytes 49160 | tf_op jit(solution)/shard_map/ppermute | solution.py:249
  124.0 4.1 %collective-permute-start.21 = (f32[8,512]{1,0:T(8,128)S(1)}, f32[8,512]{1,0:T(8,128)S(1)}, u32[]{:S(2)}, u32[]{:S(2)}) collective-permute-start(f32[8,512]{1,0:T(8,128)S(1)} %get-tuple-element.40), channel_id=1, source_target_pairs={{0,8},{1,9},{2,10},{3,11},{4,12},{5,13},{6,14},{7,15},{8,0},{9,1},... | collective-permute-start | bytes 49160 | tf_op jit(solution)/shard_map/ppermute | solution.py:249
  128.1 6.9 %collective-permute-start.23 = (f32[4,8,512]{2,1,0:T(8,128)S(1)}, f32[4,8,512]{2,1,0:T(8,128)S(1)}, u32[]{:S(2)}, u32[]{:S(2)}) collective-permute-start(f32[4,8,512]{2,1,0:T(8,128)S(1)} %pad_maximum_fusion.4.near_ref), channel_id=1, source_target_pairs={{0,1},{1,0},{2,3},{3,2},{4,5},{5,4},{6,7},{7,6},{8,9},{9,8},{10,11... | collective-permute-start | bytes 196616 | tf_op jit(solution)/shard_map/ppermute | solution.py:249
  (11 other events, 148.2 us)

commit v5 on v4

--- a/solution.py
+++ b/solution.py
@@ -12,7 +12,7 @@
 STEP = 10
 BLOCK = 64
 SUB = 4
-VMEM_LIMIT = 32 << 20
+VMEM_LIMIT = 50 << 20
 
 learn_rate = 0.05
 beta_one = 0.8
@@ -34,36 +34,35 @@
     return (param, first, second)
 
 
-def gather_codes():
-    return [y + x * X_ONE for y in (0, Y_HI) for x in range(4)]
-
-
 def third_slab(col):
     return col // X_ONE * 2 + col % 2
 
 
-def slope_kernel(scales, stepped, ids_ref, data_ref, near_ref, far_ref, two_ref, *refs):
-    if not stepped:
+def slope_kernel(scales, stepped, ids_ref, data_ref, two_ref, near_ref, near_y_ref, far_ref, far_y_ref, *refs):
+    if stepped:
+        near_three_ref, far_three_ref, *refs = refs
+    else:
         three_in_ref, *refs = refs
     sent_ref, kept_ref, slope_ref, one_ref, three_ref, ga_acc, gc_acc = refs
     step = pl.program_id(0)
     n_slab, own, rank = one_ref.shape
     depth = three_ref.shape[0] * three_ref.shape[1]
     cols = two_ref.shape[0] * two_ref.shape[1]
-    here = ids_ref[1]
+    here = ids_ref[0] // 2
 
     @pl.when(step == 0)
     def _():
-        for place, code in enumerate(gather_codes()):
-            one_ref[here ^ code] = near_ref[place]
-            one_ref[here ^ code ^ CORE] = far_ref[place]
-        if stepped:
-            for m in range(4):
-                col = here ^ (m * X_ONE)
-                three_ref[third_slab(col)] = near_ref[8 + m]
-                three_ref[third_slab(col ^ CORE)] = far_ref[8 + m]
-        else:
-            three_ref[...] = three_in_ref[...]
+        for m in range(4):
+            col = here ^ (m * X_ONE)
+            one_ref[col] = near_ref[m]
+            one_ref[col ^ Y_HI] = near_y_ref[m]
+            one_ref[col ^ CORE] = far_ref[m]
+            one_ref[col ^ CORE ^ Y_HI] = far_y_ref[m]
+            if stepped:
+                three_ref[third_slab(col)] = near_three_ref[m]
+                three_ref[third_slab(col ^ CORE)] = far_three_ref[m]
+        if not stepped:
+            three_ref[...] = three_in_ref[...].astype(bf16)
         gc_acc[...] = jnp.zeros_like(gc_acc)
 
     def run(logistic):
@@ -112,8 +111,8 @@
         ga_acc[pl.ds(step * slabs, slabs)] = jnp.concatenate(grad_one).reshape(slabs, own, rank)
         gc_acc[...] += grad_three.reshape(gc_acc.shape)
 
-    pl.when(ids_ref[0] == 1)(lambda: run(True))
-    pl.when(ids_ref[0] != 1)(lambda: run(False))
+    pl.when(ids_ref[0] % 2 == 1)(lambda: run(True))
+    pl.when(ids_ref[0] % 2 != 1)(lambda: run(False))
 
     @pl.when(step == pl.num_programs(0) - 1)
     def _():
@@ -125,11 +124,12 @@
                 out_ref[8 + m] = (ga_acc[col ^ Y_HI] * scales[0]).astype(bf16)
 
 
-def slopes(ids, tensor, near, far, twos, half_three, scales, stepped):
+def slopes(ids, tensor, twos, ones, threes, scales):
     rows, depth, cols = tensor.shape
-    own, rank = near.shape[1:]
+    own, rank = ones[0].shape[1:]
     slabs = rows // own
-    threes = half_three.shape
+    stepped = len(threes) == 2
+    all_threes = (depth // threes[0].shape[1],) + threes[0].shape[1:]
     whole = lambda shape: pl.BlockSpec(shape, lambda i: (0,) * len(shape))
     swapped = (12, own, rank)
     return pl.pallas_call(
@@ -138,34 +138,31 @@
         in_specs=[
             pl.BlockSpec(memory_space=pltpu.SMEM),
             pl.BlockSpec((BLOCK, depth, cols), lambda i: (i, 0, 0)),
-            whole(near.shape),
-            whole(far.shape),
-            whole(twos.shape),
-            *([] if stepped else [whole(threes)]),
+            *[whole(x.shape) for x in (twos, *ones, *threes)],
         ],
         out_specs=[
             whole(swapped),
             whole(swapped),
             pl.BlockSpec((BLOCK, depth, cols), lambda i: (i, 0, 0)),
             whole((slabs, own, rank)),
-            whole(threes),
+            whole(all_threes),
         ],
         out_shape=[
             jax.ShapeDtypeStruct(swapped, bf16),
             jax.ShapeDtypeStruct(swapped, bf16),
             jax.ShapeDtypeStruct((rows, depth, cols), bf16),
             jax.ShapeDtypeStruct((slabs, own, rank), bf16),
-            jax.ShapeDtypeStruct(threes, bf16),
+            jax.ShapeDtypeStruct(all_threes, bf16),
         ],
         scratch_shapes=[
             pltpu.VMEM((slabs, own, rank), f32),
-            pltpu.VMEM(threes, f32),
+            pltpu.VMEM(all_threes, f32),
         ],
         compiler_params=pltpu.CompilerParams(vmem_limit_bytes=VMEM_LIMIT),
         cost_estimate=pl.CostEstimate(
             flops=8 * rows * depth * cols * rank, bytes_accessed=4 << 20, transcendentals=rows * depth * cols
         ),
-    )(ids, tensor, near, far, twos, *([] if stepped else [half_three]))
+    )(ids, tensor, twos, *ones, *threes)
 
 
 def second_kernel(scale, slope_ref, one_ref, three_ref, out_ref, acc):
@@ -216,7 +213,7 @@
 
 def place_kernel(ids_ref, near_ref, far_ref, out_ref):
     for m in range(4):
-        col = ids_ref[1] ^ (m * X_ONE)
+        col = ids_ref[0] // 2 ^ (m * X_ONE)
         out_ref[third_slab(col)] = near_ref[m]
         out_ref[third_slab(col ^ CORE)] = far_ref[m]
 
@@ -255,18 +252,6 @@
 
 def gather_x(part):
     return jnp.stack([part] + [swap(part, m * X_ONE) for m in (1, 2, 3)])
-
-
-def gather_first(part):
-    half = gather_x(part)
-    near = jnp.concatenate([half, swap(half, Y_HI)])
-    return near, swap(near, CORE)
-
-
-def gather_both(part_one, part_three):
-    half = gather_x(jnp.stack([part_one, part_three]))
-    near = jnp.concatenate([half[:, 0], swap(half[:, 0], Y_HI), half[:, 1]])
-    return near, swap(near, CORE)
 
 
 def fold_kernel(both_ref, got_ref, out_ref):
@@ -313,35 +298,43 @@
         1.0 / math.sqrt(full_rows * full_cols),
     )
     here = lax.axis_index("col")
-    ids = jnp.stack([loss_kind[0, 0, 0], here.astype(jnp.int32)])
+    ids = loss_kind[0, 0, :1] + 2 * here
     mine = lambda x: lax.dynamic_slice_in_dim(x, third_slab(here) * deep, deep, 0)
     part_three, first_three, second_three = mine(factor_three), mine(first_three), mine(second_three)
     start_one, start_two, start_three = (factor_one, factor_two, part_three)
     twos = swap_all(to_all(factor_two.astype(bf16), n_row), "row")
-    near, far = gather_first(factor_one.astype(bf16))
-    threes = factor_three.astype(bf16).reshape(tile_depth // deep, deep, rank)
+    near = gather_x(factor_one.astype(bf16))
+    near_y = swap(near, Y_HI)
+    ones = (near, near_y, swap(near, CORE), swap(near_y, CORE))
+    threes = (factor_three.reshape(tile_depth // deep, deep, rank),)
     for iteration in range(ITERS):
+        last = iteration == ITERS - 1
         counter = STEP + iteration + 1
-        sent, kept, slope, ones, threes = slopes(
-            ids, tensor, near, far, twos, threes, scales, iteration > 0
-        )
-        grad_two = second_grad(slope, ones, threes, scales[1]).reshape(n_row, own_two, rank)
+        sent, kept, slope, all_ones, all_threes = slopes(ids, tensor, twos, ones, threes, scales)
+        grad_two = second_grad(slope, all_ones, all_threes, scales[1]).reshape(n_row, own_two, rank)
         grad_one, grad_three = reduce_col(plus(kept, swap(sent, CORE)))
         sent = jnp.concatenate([grad_two, to_all(grad_three.astype(bf16), n_row)], axis=1)
         factor_one, first_one, second_one = adam_step(factor_one, first_one, second_one, grad_one, counter)
-        got = total(swap_all(sent, "row"))
+        got = swap_all(sent, "row")
+        if not last:
+            near = gather_x(factor_one.astype(bf16))
+            got, near = lax.optimization_barrier((got, near))
+            near_y = swap(near, Y_HI)
+        got = total(got)
         grad_two, grad_three = got[:own_two], got[own_two:]
         part_three, first_three, second_three = adam_step(
             part_three, first_three, second_three, grad_three, counter
         )
-        if iteration < ITERS - 1:
-            near, far = gather_both(factor_one.astype(bf16), part_three.astype(bf16))
-        else:
+        if last:
             near = gather_x((start_three - part_three) / (learn_rate * ITERS))
             near, grad_two = lax.optimization_barrier((near, grad_two))
         factor_two, first_two, second_two = adam_step(factor_two, first_two, second_two, grad_two, counter)
-        if iteration < ITERS - 1:
+        if not last:
+            near_three = gather_x(part_three.astype(bf16))
             twos = swap_all(to_all(factor_two.astype(bf16), n_row), "row")
+            twos, near_y, near_three = lax.optimization_barrier((twos, near_y, near_three))
+            ones = (near, near_y, swap(near, CORE), swap(near_y, CORE))
+            threes = (near_three, swap(near_three, CORE))
     spread = learn_rate * ITERS
     new_three = place_third(ids, near, swap(near, CORE)).reshape(tile_depth, rank)
     return ((start_one - factor_one) / spread, (start_two - factor_two) / spread, new_three)

time: 137 us -> 137 us (level)
  waiting for transfers between devices: 23.9 us -> 21.1 us
  blocking collectives: 14.8 us -> 17 us
    all_to_all x3, waiting for transfers between devices: 9.69 us -> 4.56 us  [swap_all(): return lax.all_to_all(parts, axis, 0, 0)]
    ppermute x24 -> x30, waiting for transfers between devices: 14.2 us -> 16.5 us  [swap(): return lax.ppermute(part, 'col', [(i, i ^ code) for i in range(size)])]
    all_to_all x1, blocking collectives: 14.8 us -> 17 us  [swap_all(): return lax.all_to_all(parts, axis, 0, 0)]
    convert_element_type x0 -> x3, other arithmetic: none -> 1.54 us  [the longest x1 0.79 us: shards(): near_three = gather_x(part_three.astype(bf16))]
    another operation x3 -> x0, other arithmetic: 1.54 us -> none  [the longest x2 0.82 us: gather_both(): half = gather_x(jnp.stack([part_one, part_three]))]
    ppermute x24 -> x30, starting transfers between devices: 48.9 us -> 50.3 us  [swap(): return lax.ppermute(part, 'col', [(i, i ^ code) for i in range(size)])]
  transfers between devices with their start and end apart: 27 -> 33, of which waited for: 13 -> 15; matrix products, arithmetic and copies ran while one was open for 4% -> 3% of each run, Pallas kernels for 3% -> 3%
where the time goes in v5:
time: 137 us; the launch traced here: 136 us
  starting transfers between devices  70.2 us (51%)
  waiting for transfers between devices  21.1 us (15%)
  Pallas kernels  17.6 us (13%)
  blocking collectives  17 us (12%)
  other arithmetic  5.37 us (4%)
  local copies, waits for them, and re-layouts  3.51 us (3%)
  between operations  1.64 us (1%)
    ppermute x30, starting transfers between devices, swap(): return lax.ppermute(part, 'col', [(i, i ^ code) for i in range(size)])  50.3 us
    all_to_all x3, starting transfers between devices, swap_all(): return lax.all_to_all(parts, axis, 0, 0)  19.9 us
    all_to_all x1, blocking collectives, swap_all(): return lax.all_to_all(parts, axis, 0, 0)  17 us
    ppermute x30, waiting for transfers between devices, swap(): return lax.ppermute(part, 'col', [(i, i ^ code) for i in range(size)])  16.5 us
    pallas_call x2, Pallas kernels, slopes(): pl.pallas_call(functools.partial(slope_kernel, scales, stepped), grid=(ro...  12.8 us
    all_to_all x3, waiting for transfers between devices, swap_all(): return lax.all_to_all(parts, axis, 0, 0)  4.56 us
    pallas_call x2, Pallas kernels, second_grad(): pl.pallas_call(functools.partial(second_kernel, scale), grid=(rows // blo...  4.09 us
  transfers between devices with their start and end apart: 33, of which 15 were waited for; matrix products, arithmetic and copies ran while one was open for 3% of the time, Pallas kernels for 3%

profile of v5, /device:TPU:1, one launch (start us, length us, event | category | flops | bytes accessed | tf_op | source)
XLA Modules:
  0.0 136.4 jit_solution(2734987629316947492)
XLA Ops:
  1.4 3.6 %collective-permute-start.1 = (bf16[8,512]{1,0:T(8,128)(2,1)S(1)}, bf16[8,512]{1,0:T(8,128)(2,1)S(1)}, u32[]{:S(2)}, u32[]{:S(2)}) collective-permute-start(bf16[8,512]{1,0:T(8,128)(2,1)S(1)} %convert_element_type.74), channel_id=1, source_target_pairs={{0,8},{1,9},{2,10},{3,11},{4,12},{5,13},{6,14},{7,15},{8,0},{9,1},... | collective-permute-start | bytes 24584 | tf_op jit(solution)/shard_map/ppermute | solution.py:246
  7.2 9.3 %all-to-all-start = ((bf16[16,8,512]{2,1,0:T(8,128)(2,1)}), bf16[16,8,512]{2,1,0:T(8,128)(2,1)S(1)}, u32[]{:S(2)}, u32[]{:S(2)}) async-start(bf16[16,8,512]{2,1,0:T(8,128)(2,1)} %broadcast_in_dim.12), calls=%async_computation | async-start | bytes 262144 | tf_op jit(solution)/shard_map/all_to_all | solution.py:233
  17.2 2.7 %collective-permute-start.3 = (bf16[4,8,512]{2,1,0:T(8,128)(2,1)S(1)}, bf16[4,8,512]{2,1,0:T(8,128)(2,1)S(1)}, u32[]{:S(2)}, u32[]{:S(2)}) collective-permute-start(bf16[4,8,512]{2,1,0:T(8,128)(2,1)S(1)} %pad_maximum_fusion.3.near_ref), channel_id=1, source_target_pairs={{0,2},{1,3},{2,0},{3,1},{4,6},{5,7},{6,4},{7,5},{8,10},{9,11},{10,... | collective-permute-start | bytes 98312 | tf_op jit(solution)/shard_map/ppermute | solution.py:246
  20.0 1.8 %collective-permute-start.4 = (bf16[4,8,512]{2,1,0:T(8,128)(2,1)S(1)}, bf16[4,8,512]{2,1,0:T(8,128)(2,1)S(1)}, u32[]{:S(2)}, u32[]{:S(2)}) collective-permute-start(bf16[4,8,512]{2,1,0:T(8,128)(2,1)S(1)} %pad_maximum_fusion.3.near_ref), channel_id=1, source_target_pairs={{0,1},{1,0},{2,3},{3,2},{4,5},{5,4},{6,7},{7,6},{8,9},{9,8},{10,11... | collective-permute-start | bytes 98312 | tf_op jit(solution)/shard_map/ppermute | solution.py:246
  21.8 2.5 %collective-permute-start.5 = (bf16[4,8,512]{2,1,0:T(8,128)(2,1)S(1)}, bf16[4,8,512]{2,1,0:T(8,128)(2,1)S(1)}, u32[]{:S(2)}, u32[]{:S(2)}) collective-permute-start(bf16[4,8,512]{2,1,0:T(8,128)(2,1)S(1)} %collective-permute-done.3.near_y_ref), channel_id=1, source_target_pairs={{0,1},{1,0},{2,3},{3,2},{4,5},{5,4},{6,7},{7,6},{8,9},{9,8},{10,11... | collective-permute-start | bytes 98312 | tf_op jit(solution)/shard_map/ppermute | solution.py:246
  27.1 6.4 %shard_map.130 = (bf16[12,8,512]{2,1,0:T(8,128)(2,1)S(1)}, bf16[12,8,512]{2,1,0:T(8,128)(2,1)S(1)}, bf16[128,64,128]{2,1,0:T(8,128)(2,1)S(1)}, bf16[16,8,512]{2,1,0:T(8,128)(2,1)S(1)}, bf16[8,8,512]{2,1,0:T(8,128)(2,1)S(1)}) custom-call(s32[1]{0:T(128)S(6)} %add.102.ids_ref, bf16[128,64,128]{2,1,0:T(8,128)(2,1)} %data_ref.3, ...), custom_call_target="tpu_custom_call" | custom-call | flops 4294967296 | bytes 4194304 | tf_op jit(solution)/shard_map/pallas_call | solution.py:135
  36.0 2.7 %collective-permute-start.7 = (bf16[8,8,512]{2,1,0:T(8,128)(2,1)S(1)}, bf16[8,8,512]{2,1,0:T(8,128)(2,1)S(1)}, u32[]{:S(2)}, u32[]{:S(2)}) collective-permute-start(bf16[8,8,512]{2,1,0:T(8,128)(2,1)S(1)} %slice.78), channel_id=1, source_target_pairs={{0,2},{1,3},{2,0},{3,1},{4,6},{5,7},{6,4},{7,5},{8,10},{9,11},{10,... | collective-permute-start | bytes 196616 | tf_op jit(solution)/shard_map/ppermute | solution.py:246
  38.7 2.0 %collective-permute-done.7.got_ref = bf16[8,8,512]{2,1,0:T(8,128)(2,1)S(1)} collective-permute-done((bf16[8,8,512]{2,1,0:T(8,128)(2,1)S(1)}, bf16[8,8,512]{2,1,0:T(8,128)(2,1)S(1)}, u32[]{:S(2)}, u32[]{:S(2)}) %collective-permute-start.7) | collective-permute-done | bytes 65568 | tf_op jit(solution)/shard_map/ppermute | solution.py:246
  42.0 1.8 %collective-permute-start.10 = (bf16[2,8,512]{2,1,0:T(8,128)(2,1)S(1)}, bf16[2,8,512]{2,1,0:T(8,128)(2,1)S(1)}, u32[]{:S(2)}, u32[]{:S(2)}) collective-permute-start(bf16[2,8,512]{2,1,0:T(8,128)(2,1)S(1)} %get-tuple-element.43), channel_id=1, source_target_pairs={{0,12},{1,13},{2,14},{3,15},{4,8},{5,9},{6,10},{7,11},{8,4},{9,5},... | collective-permute-start | bytes 49160 | tf_op jit(solution)/shard_map/ppermute | solution.py:246
  44.5 2.1 %shard_map.132 = bf16[128,512]{1,0:T(8,128)(2,1)S(1)} custom-call(bf16[128,64,128]{2,1,0:T(8,128)(2,1)S(1)} %get-tuple-element.22.slope_ref, bf16[16,8,512]{2,1,0:T(8,128)(2,1)S(1)} %get-tuple-element.23.one_ref, bf16[8,8,512]{2,1,0:T(8,128)(2,1)S(1)} %get-tuple-element.24.three_ref), custom_call_target="tpu_custom_call" | custom-call | flops 2147483648 | bytes 2097152 | tf_op jit(solution)/shard_map/pallas_call | solution.py:196
  48.6 7.1 %all-to-all-start.1 = ((bf16[16,16,512]{2,1,0:T(8,128)(2,1)}), bf16[16,16,512]{2,1,0:T(8,128)(2,1)S(1)}, u32[]{:S(2)}, u32[]{:S(2)}) async-start(bf16[16,16,512]{2,1,0:T(8,128)(2,1)} %pad_maximum_fusion), calls=%async_computation.1 | async-start | bytes 524288 | tf_op jit(solution)/shard_map/all_to_all | solution.py:233
  60.8 4.6 %all-to-all-done.1 = bf16[16,16,512]{2,1,0:T(8,128)(2,1)S(1)} async-done(((bf16[16,16,512]{2,1,0:T(8,128)(2,1)}), bf16[16,16,512]{2,1,0:T(8,128)(2,1)S(1)}, u32[]{:S(2)}, u32[]{:S(2)}) %all-to-all-start.1) | async-done | bytes 262176 | tf_op jit(solution)/shard_map/all_to_all | solution.py:233
  66.9 3.5 %all-to-all-start.2 = ((bf16[16,8,512]{2,1,0:T(8,128)(2,1)}), bf16[16,8,512]{2,1,0:T(8,128)(2,1)S(1)}, u32[]{:S(2)}, u32[]{:S(2)}) async-start(bf16[16,8,512]{2,1,0:T(8,128)(2,1)} %broadcast_in_dim.15), calls=%async_computation.2 | async-start | bytes 262144 | tf_op jit(solution)/shard_map/all_to_all | solution.py:233
  73.8 5.3 %collective-permute-start.18 = (bf16[4,8,512]{2,1,0:T(8,128)(2,1)S(1)}, bf16[4,8,512]{2,1,0:T(8,128)(2,1)S(1)}, u32[]{:S(2)}, u32[]{:S(2)}) collective-permute-start(bf16[4,8,512]{2,1,0:T(8,128)(2,1)S(1)} %pad_maximum_fusion.4.near_ref), channel_id=1, source_target_pairs={{0,1},{1,0},{2,3},{3,2},{4,5},{5,4},{6,7},{7,6},{8,9},{9,8},{10,11... | collective-permute-start | bytes 98312 | tf_op jit(solution)/shard_map/ppermute | solution.py:246
  79.1 2.6 %collective-permute-start.14 = (bf16[4,8,512]{2,1,0:T(8,128)(2,1)S(1)}, bf16[4,8,512]{2,1,0:T(8,128)(2,1)S(1)}, u32[]{:S(2)}, u32[]{:S(2)}) collective-permute-start(bf16[4,8,512]{2,1,0:T(8,128)(2,1)S(1)} %pad_maximum_fusion.4.near_ref), channel_id=1, source_target_pairs={{0,2},{1,3},{2,0},{3,1},{4,6},{5,7},{6,4},{7,5},{8,10},{9,11},{10,... | collective-permute-start | bytes 98312 | tf_op jit(solution)/shard_map/ppermute | solution.py:246
  81.7 2.0 %collective-permute-done.14.near_y_ref = bf16[4,8,512]{2,1,0:T(8,128)(2,1)S(1)} collective-permute-done((bf16[4,8,512]{2,1,0:T(8,128)(2,1)S(1)}, bf16[4,8,512]{2,1,0:T(8,128)(2,1)S(1)}, u32[]{:S(2)}, u32[]{:S(2)}) %collective-permute-start.14) | collective-permute-done | bytes 32800 | tf_op jit(solution)/shard_map/ppermute | solution.py:246
  85.8 6.4 %shard_map.133 = (bf16[12,8,512]{2,1,0:T(8,128)(2,1)S(1)}, bf16[12,8,512]{2,1,0:T(8,128)(2,1)S(1)}, bf16[128,64,128]{2,1,0:T(8,128)(2,1)S(1)}, bf16[16,8,512]{2,1,0:T(8,128)(2,1)S(1)}, bf16[8,8,512]{2,1,0:T(8,128)(2,1)S(1)}) custom-call(s32[1]{0:T(128)S(6)} %add.102.ids_ref, bf16[128,64,128]{2,1,0:T(8,128)(2,1)} %data_ref.3, ...), custom_call_target="tpu_custom_call" | custom-call | flops 4294967296 | bytes 4194304 | tf_op jit(solution)/shard_map/pallas_call | solution.py:135
  93.9 2.6 %collective-permute-start.22 = (bf16[8,8,512]{2,1,0:T(8,128)(2,1)S(1)}, bf16[8,8,512]{2,1,0:T(8,128)(2,1)S(1)}, u32[]{:S(2)}, u32[]{:S(2)}) collective-permute-start(bf16[8,8,512]{2,1,0:T(8,128)(2,1)S(1)} %slice.87), channel_id=1, source_target_pairs={{0,2},{1,3},{2,0},{3,1},{4,6},{5,7},{6,4},{7,5},{8,10},{9,11},{10,... | collective-permute-start | bytes 196616 | tf_op jit(solution)/shard_map/ppermute | solution.py:246
  96.5 2.6 %collective-permute-done.22.got_ref = bf16[8,8,512]{2,1,0:T(8,128)(2,1)S(1)} collective-permute-done((bf16[8,8,512]{2,1,0:T(8,128)(2,1)S(1)}, bf16[8,8,512]{2,1,0:T(8,128)(2,1)S(1)}, u32[]{:S(2)}, u32[]{:S(2)}) %collective-permute-start.22) | collective-permute-done | bytes 65568 | tf_op jit(solution)/shard_map/ppermute | solution.py:246
  102.4 2.0 %shard_map.135 = bf16[128,512]{1,0:T(8,128)(2,1)S(1)} custom-call(bf16[128,64,128]{2,1,0:T(8,128)(2,1)S(1)} %get-tuple-element.32.slope_ref, bf16[16,8,512]{2,1,0:T(8,128)(2,1)S(1)} %get-tuple-element.33.one_ref, bf16[8,8,512]{2,1,0:T(8,128)(2,1)S(1)} %get-tuple-element.34.three_ref), custom_call_target="tpu_custom_call" | custom-call | flops 2147483648 | bytes 2097152 | tf_op jit(solution)/shard_map/pallas_call | solution.py:196
  105.3 17.0 %all_to_all.20 = bf16[16,16,512]{2,1,0:T(8,128)(2,1)S(1)} all-to-all(bf16[16,16,512]{2,1,0:T(8,128)(2,1)S(1)} %pad_maximum_fusion.1), channel_id=1, replica_groups=mesh['row'=16,'col'=16] {'row'}, dimensions={0} | all-to-all | bytes 524288 | tf_op jit(solution)/shard_map/all_to_all | solution.py:233
  123.2 2.0 %collective-permute-start.28 = (f32[8,512]{1,0:T(8,128)S(1)}, f32[8,512]{1,0:T(8,128)S(1)}, u32[]{:S(2)}, u32[]{:S(2)}) collective-permute-start(f32[8,512]{1,0:T(8,128)S(1)} %get-tuple-element.46), channel_id=1, source_target_pairs={{0,12},{1,13},{2,14},{3,15},{4,8},{5,9},{6,10},{7,11},{8,4},{9,5},... | collective-permute-start | bytes 49160 | tf_op jit(solution)/shard_map/ppermute | solution.py:246
  127.1 2.2 %collective-permute-done.27 = f32[8,512]{1,0:T(8,128)S(1)} collective-permute-done((f32[8,512]{1,0:T(8,128)S(1)}, f32[8,512]{1,0:T(8,128)S(1)}, u32[]{:S(2)}, u32[]{:S(2)}) %collective-permute-start.27) | collective-permute-done | bytes 16416 | tf_op jit(solution)/shard_map/ppermute | solution.py:246
  129.2 5.6 %collective-permute-start.29 = (f32[4,8,512]{2,1,0:T(8,128)S(1)}, f32[4,8,512]{2,1,0:T(8,128)S(1)}, u32[]{:S(2)}, u32[]{:S(2)}) collective-permute-start(f32[4,8,512]{2,1,0:T(8,128)S(1)} %pad_maximum_fusion.2.near_ref), channel_id=1, source_target_pairs={{0,1},{1,0},{2,3},{3,2},{4,5},{5,4},{6,7},{7,6},{8,9},{9,8},{10,11... | collective-permute-start | bytes 196616 | tf_op jit(solution)/shard_map/ppermute | solution.py:246
  (94 shorter events, 34.6 us)
Async XLA Ops:
  1.4 15.9 %collective-permute-start.1 = (bf16[8,512]{1,0:T(8,128)(2,1)S(1)}, bf16[8,512]{1,0:T(8,128)(2,1)S(1)}, u32[]{:S(2)}, u32[]{:S(2)}) collective-permute-start(bf16[8,512]{1,0:T(8,128)(2,1)S(1)} %convert_element_type.74), channel_id=1, source_target_pairs={{0,8},{1,9},{2,10},{3,11},{4,12},{5,13},{6,14},{7,15},{8,0},{9,1},... | collective-permute-start | bytes 24584 | tf_op jit(solution)/shard_map/ppermute | solution.py:246
  4.9 12.3 %collective-permute-start = (bf16[8,512]{1,0:T(8,128)(2,1)S(1)}, bf16[8,512]{1,0:T(8,128)(2,1)S(1)}, u32[]{:S(2)}, u32[]{:S(2)}) collective-permute-start(bf16[8,512]{1,0:T(8,128)(2,1)S(1)} %convert_element_type.74), channel_id=1, source_target_pairs={{0,4},{1,5},{2,6},{3,7},{4,0},{5,1},{6,2},{7,3},{8,12},{9,13},{10,... | collective-permute-start | bytes 24584 | tf_op jit(solution)/shard_map/ppermute | solution.py:246
  5.2 12.0 %collective-permute-start.2 = (bf16[8,512]{1,0:T(8,128)(2,1)S(1)}, bf16[8,512]{1,0:T(8,128)(2,1)S(1)}, u32[]{:S(2)}, u32[]{:S(2)}) collective-permute-start(bf16[8,512]{1,0:T(8,128)(2,1)S(1)} %convert_element_type.74), channel_id=1, source_target_pairs={{0,12},{1,13},{2,14},{3,15},{4,8},{5,9},{6,10},{7,11},{8,4},{9,5},... | collective-permute-start | bytes 24584 | tf_op jit(solution)/shard_map/ppermute | solution.py:246
  7.2 19.0 %all-to-all-start = ((bf16[16,8,512]{2,1,0:T(8,128)(2,1)}), bf16[16,8,512]{2,1,0:T(8,128)(2,1)S(1)}, u32[]{:S(2)}, u32[]{:S(2)}) async-start(bf16[16,8,512]{2,1,0:T(8,128)(2,1)} %broadcast_in_dim.12), calls=%async_computation | async-start | bytes 262144 | tf_op jit(solution)/shard_map/all_to_all | solution.py:233
  17.2 4.5 %collective-permute-start.3 = (bf16[4,8,512]{2,1,0:T(8,128)(2,1)S(1)}, bf16[4,8,512]{2,1,0:T(8,128)(2,1)S(1)}, u32[]{:S(2)}, u32[]{:S(2)}) collective-permute-start(bf16[4,8,512]{2,1,0:T(8,128)(2,1)S(1)} %pad_maximum_fusion.3.near_ref), channel_id=1, source_target_pairs={{0,2},{1,3},{2,0},{3,1},{4,6},{5,7},{6,4},{7,5},{8,10},{9,11},{10,... | collective-permute-start | bytes 98312 | tf_op jit(solution)/shard_map/ppermute | solution.py:246
  20.0 6.2 %collective-permute-start.4 = (bf16[4,8,512]{2,1,0:T(8,128)(2,1)S(1)}, bf16[4,8,512]{2,1,0:T(8,128)(2,1)S(1)}, u32[]{:S(2)}, u32[]{:S(2)}) collective-permute-start(bf16[4,8,512]{2,1,0:T(8,128)(2,1)S(1)} %pad_maximum_fusion.3.near_ref), channel_id=1, source_target_pairs={{0,1},{1,0},{2,3},{3,2},{4,5},{5,4},{6,7},{7,6},{8,9},{9,8},{10,11... | collective-permute-start | bytes 98312 | tf_op jit(solution)/shard_map/ppermute | solution.py:246
  21.8 4.4 %collective-permute-start.5 = (bf16[4,8,512]{2,1,0:T(8,128)(2,1)S(1)}, bf16[4,8,512]{2,1,0:T(8,128)(2,1)S(1)}, u32[]{:S(2)}, u32[]{:S(2)}) collective-permute-start(bf16[4,8,512]{2,1,0:T(8,128)(2,1)S(1)} %collective-permute-done.3.near_y_ref), channel_id=1, source_target_pairs={{0,1},{1,0},{2,3},{3,2},{4,5},{5,4},{6,7},{7,6},{8,9},{9,8},{10,11... | collective-permute-start | bytes 98312 | tf_op jit(solution)/shard_map/ppermute | solution.py:246
  36.0 4.7 %collective-permute-start.7 = (bf16[8,8,512]{2,1,0:T(8,128)(2,1)S(1)}, bf16[8,8,512]{2,1,0:T(8,128)(2,1)S(1)}, u32[]{:S(2)}, u32[]{:S(2)}) collective-permute-start(bf16[8,8,512]{2,1,0:T(8,128)(2,1)S(1)} %slice.78), channel_id=1, source_target_pairs={{0,2},{1,3},{2,0},{3,1},{4,6},{5,7},{6,4},{7,5},{8,10},{9,11},{10,... | collective-permute-start | bytes 196616 | tf_op jit(solution)/shard_map/ppermute | solution.py:246
  40.7 5.8 %collective-permute-start.8 = (bf16[2,8,512]{2,1,0:T(8,128)(2,1)S(1)}, bf16[2,8,512]{2,1,0:T(8,128)(2,1)S(1)}, u32[]{:S(2)}, u32[]{:S(2)}) collective-permute-start(bf16[2,8,512]{2,1,0:T(8,128)(2,1)S(1)} %get-tuple-element.42), channel_id=1, source_target_pairs={{0,4},{1,5},{2,6},{3,7},{4,0},{5,1},{6,2},{7,3},{8,12},{9,13},{10,... | collective-permute-start | bytes 49160 | tf_op jit(solution)/shard_map/ppermute | solution.py:246
  42.0 4.6 %collective-permute-start.10 = (bf16[2,8,512]{2,1,0:T(8,128)(2,1)S(1)}, bf16[2,8,512]{2,1,0:T(8,128)(2,1)S(1)}, u32[]{:S(2)}, u32[]{:S(2)}) collective-permute-start(bf16[2,8,512]{2,1,0:T(8,128)(2,1)S(1)} %get-tuple-element.43), channel_id=1, source_target_pairs={{0,12},{1,13},{2,14},{3,15},{4,8},{5,9},{6,10},{7,11},{8,4},{9,5},... | collective-permute-start | bytes 49160 | tf_op jit(solution)/shard_map/ppermute | solution.py:246
  43.8 4.1 %collective-permute-start.9 = (bf16[2,8,512]{2,1,0:T(8,128)(2,1)S(1)}, bf16[2,8,512]{2,1,0:T(8,128)(2,1)S(1)}, u32[]{:S(2)}, u32[]{:S(2)}) collective-permute-start(bf16[2,8,512]{2,1,0:T(8,128)(2,1)S(1)} %get-tuple-element.44), channel_id=1, source_target_pairs={{0,8},{1,9},{2,10},{3,11},{4,12},{5,13},{6,14},{7,15},{8,0},{9,1},... | collective-permute-start | bytes 49160 | tf_op jit(solution)/shard_map/ppermute | solution.py:246
  48.6 16.7 %all-to-all-start.1 = ((bf16[16,16,512]{2,1,0:T(8,128)(2,1)}), bf16[16,16,512]{2,1,0:T(8,128)(2,1)S(1)}, u32[]{:S(2)}, u32[]{:S(2)}) async-start(bf16[16,16,512]{2,1,0:T(8,128)(2,1)} %pad_maximum_fusion), calls=%async_computation.1 | async-start | bytes 524288 | tf_op jit(solution)/shard_map/all_to_all | solution.py:233
  66.9 16.7 %all-to-all-start.2 = ((bf16[16,8,512]{2,1,0:T(8,128)(2,1)}), bf16[16,8,512]{2,1,0:T(8,128)(2,1)S(1)}, u32[]{:S(2)}, u32[]{:S(2)}) async-start(bf16[16,8,512]{2,1,0:T(8,128)(2,1)} %broadcast_in_dim.15), calls=%async_computation.2 | async-start | bytes 262144 | tf_op jit(solution)/shard_map/all_to_all | solution.py:233
  70.4 11.2 %collective-permute-start.17 = (bf16[8,512]{1,0:T(8,128)(2,1)S(1)}, bf16[8,512]{1,0:T(8,128)(2,1)S(1)}, u32[]{:S(2)}, u32[]{:S(2)}) collective-permute-start(bf16[8,512]{1,0:T(8,128)(2,1)S(1)} %get-tuple-element.37), channel_id=1, source_target_pairs={{0,12},{1,13},{2,14},{3,15},{4,8},{5,9},{6,10},{7,11},{8,4},{9,5},... | collective-permute-start | bytes 24584 | tf_op jit(solution)/shard_map/ppermute | solution.py:246
  72.1 9.6 %collective-permute-start.16 = (bf16[8,512]{1,0:T(8,128)(2,1)S(1)}, bf16[8,512]{1,0:T(8,128)(2,1)S(1)}, u32[]{:S(2)}, u32[]{:S(2)}) collective-permute-start(bf16[8,512]{1,0:T(8,128)(2,1)S(1)} %get-tuple-element.37), channel_id=1, source_target_pairs={{0,8},{1,9},{2,10},{3,11},{4,12},{5,13},{6,14},{7,15},{8,0},{9,1},... | collective-permute-start | bytes 24584 | tf_op jit(solution)/shard_map/ppermute | solution.py:246
  72.9 8.7 %collective-permute-start.15 = (bf16[8,512]{1,0:T(8,128)(2,1)S(1)}, bf16[8,512]{1,0:T(8,128)(2,1)S(1)}, u32[]{:S(2)}, u32[]{:S(2)}) collective-permute-start(bf16[8,512]{1,0:T(8,128)(2,1)S(1)} %get-tuple-element.37), channel_id=1, source_target_pairs={{0,4},{1,5},{2,6},{3,7},{4,0},{5,1},{6,2},{7,3},{8,12},{9,13},{10,... | collective-permute-start | bytes 24584 | tf_op jit(solution)/shard_map/ppermute | solution.py:246
  73.8 10.9 %collective-permute-start.18 = (bf16[4,8,512]{2,1,0:T(8,128)(2,1)S(1)}, bf16[4,8,512]{2,1,0:T(8,128)(2,1)S(1)}, u32[]{:S(2)}, u32[]{:S(2)}) collective-permute-start(bf16[4,8,512]{2,1,0:T(8,128)(2,1)S(1)} %pad_maximum_fusion.4.near_ref), channel_id=1, source_target_pairs={{0,1},{1,0},{2,3},{3,2},{4,5},{5,4},{6,7},{7,6},{8,9},{9,8},{10,11... | collective-permute-start | bytes 98312 | tf_op jit(solution)/shard_map/ppermute | solution.py:246
  79.1 4.6 %collective-permute-start.14 = (bf16[4,8,512]{2,1,0:T(8,128)(2,1)S(1)}, bf16[4,8,512]{2,1,0:T(8,128)(2,1)S(1)}, u32[]{:S(2)}, u32[]{:S(2)}) collective-permute-start(bf16[4,8,512]{2,1,0:T(8,128)(2,1)S(1)} %pad_maximum_fusion.4.near_ref), channel_id=1, source_target_pairs={{0,2},{1,3},{2,0},{3,1},{4,6},{5,7},{6,4},{7,5},{8,10},{9,11},{10,... | collective-permute-start | bytes 98312 | tf_op jit(solution)/shard_map/ppermute | solution.py:246
  93.9 5.1 %collective-permute-start.22 = (bf16[8,8,512]{2,1,0:T(8,128)(2,1)S(1)}, bf16[8,8,512]{2,1,0:T(8,128)(2,1)S(1)}, u32[]{:S(2)}, u32[]{:S(2)}) collective-permute-start(bf16[8,8,512]{2,1,0:T(8,128)(2,1)S(1)} %slice.87), channel_id=1, source_target_pairs={{0,2},{1,3},{2,0},{3,1},{4,6},{5,7},{6,4},{7,5},{8,10},{9,11},{10,... | collective-permute-start | bytes 196616 | tf_op jit(solution)/shard_map/ppermute | solution.py:246
  99.1 5.4 %collective-permute-start.23 = (bf16[2,8,512]{2,1,0:T(8,128)(2,1)S(1)}, bf16[2,8,512]{2,1,0:T(8,128)(2,1)S(1)}, u32[]{:S(2)}, u32[]{:S(2)}) collective-permute-start(bf16[2,8,512]{2,1,0:T(8,128)(2,1)S(1)} %get-tuple-element.39), channel_id=1, source_target_pairs={{0,4},{1,5},{2,6},{3,7},{4,0},{5,1},{6,2},{7,3},{8,12},{9,13},{10,... | collective-permute-start | bytes 49160 | tf_op jit(solution)/shard_map/ppermute | solution.py:246
  100.3 4.2 %collective-permute-start.25 = (bf16[2,8,512]{2,1,0:T(8,128)(2,1)S(1)}, bf16[2,8,512]{2,1,0:T(8,128)(2,1)S(1)}, u32[]{:S(2)}, u32[]{:S(2)}) collective-permute-start(bf16[2,8,512]{2,1,0:T(8,128)(2,1)S(1)} %get-tuple-element.40), channel_id=1, source_target_pairs={{0,12},{1,13},{2,14},{3,15},{4,8},{5,9},{6,10},{7,11},{8,4},{9,5},... | collective-permute-start | bytes 49160 | tf_op jit(solution)/shard_map/ppermute | solution.py:246
  101.1 4.1 %collective-permute-start.24 = (bf16[2,8,512]{2,1,0:T(8,128)(2,1)S(1)}, bf16[2,8,512]{2,1,0:T(8,128)(2,1)S(1)}, u32[]{:S(2)}, u32[]{:S(2)}) collective-permute-start(bf16[2,8,512]{2,1,0:T(8,128)(2,1)S(1)} %get-tuple-element.41), channel_id=1, source_target_pairs={{0,8},{1,9},{2,10},{3,11},{4,12},{5,13},{6,14},{7,15},{8,0},{9,1},... | collective-permute-start | bytes 49160 | tf_op jit(solution)/shard_map/ppermute | solution.py:246
  125.1 4.1 %collective-permute-start.27 = (f32[8,512]{1,0:T(8,128)S(1)}, f32[8,512]{1,0:T(8,128)S(1)}, u32[]{:S(2)}, u32[]{:S(2)}) collective-permute-start(f32[8,512]{1,0:T(8,128)S(1)} %get-tuple-element.46), channel_id=1, source_target_pairs={{0,8},{1,9},{2,10},{3,11},{4,12},{5,13},{6,14},{7,15},{8,0},{9,1},... | collective-permute-start | bytes 49160 | tf_op jit(solution)/shard_map/ppermute | solution.py:246
  129.2 6.5 %collective-permute-start.29 = (f32[4,8,512]{2,1,0:T(8,128)S(1)}, f32[4,8,512]{2,1,0:T(8,128)S(1)}, u32[]{:S(2)}, u32[]{:S(2)}) collective-permute-start(f32[4,8,512]{2,1,0:T(8,128)S(1)} %pad_maximum_fusion.2.near_ref), channel_id=1, source_target_pairs={{0,1},{1,0},{2,3},{3,2},{4,5},{5,4},{6,7},{7,6},{8,9},{9,8},{10,11... | collective-permute-start | bytes 196616 | tf_op jit(solution)/shard_map/ppermute | solution.py:246
  (16 other events, 123.0 us)

commit v6 on v5

--- a/solution.py
+++ b/solution.py
@@ -13,6 +13,8 @@
 BLOCK = 64
 SUB = 4
 VMEM_LIMIT = 50 << 20
+VMEM_ALL = 61 << 20
+VMEM_LATER = 32 << 20
 
 learn_rate = 0.05
 beta_one = 0.8
@@ -62,7 +64,7 @@
                 three_ref[third_slab(col)] = near_three_ref[m]
                 three_ref[third_slab(col ^ CORE)] = far_three_ref[m]
         if not stepped:
-            three_ref[...] = three_in_ref[...].astype(bf16)
+            three_ref[...] = three_in_ref[...]
         gc_acc[...] = jnp.zeros_like(gc_acc)
 
     def run(logistic):
@@ -158,7 +160,7 @@
             pltpu.VMEM((slabs, own, rank), f32),
             pltpu.VMEM(all_threes, f32),
         ],
-        compiler_params=pltpu.CompilerParams(vmem_limit_bytes=VMEM_LIMIT),
+        compiler_params=pltpu.CompilerParams(vmem_limit_bytes=VMEM_LATER if stepped else VMEM_LIMIT),
         cost_estimate=pl.CostEstimate(
             flops=8 * rows * depth * cols * rank, bytes_accessed=4 << 20, transcendentals=rows * depth * cols
         ),
@@ -209,6 +211,38 @@
             flops=4 * rows * depth * cols * rank, bytes_accessed=2 << 20, transcendentals=0
         ),
     )(slope, ones, threes)
+
+
+def prepare_kernel(kind_ref, two_ref, three_ref, ids_ref, twos_ref, half_three_ref):
+    ids_ref[0] = kind_ref[0, 0, 0] + 2 * lax.axis_index("col")
+    two = two_ref[...].astype(bf16)
+    for slab in range(twos_ref.shape[0]):
+        twos_ref[slab] = two
+    half_three_ref[...] = three_ref[...].astype(bf16)
+
+
+def prepare(loss_kind, two, three, copies):
+    whole = lambda shape: pl.BlockSpec(shape, lambda i: (0,) * len(shape))
+    return pl.pallas_call(
+        prepare_kernel,
+        grid=(1,),
+        in_specs=[
+            pl.BlockSpec((1, 8, 128), lambda i: (0, 0, 0), memory_space=pltpu.SMEM),
+            whole(two.shape),
+            whole(three.shape),
+        ],
+        out_specs=[
+            pl.BlockSpec(memory_space=pltpu.SMEM),
+            whole((copies,) + two.shape),
+            whole(three.shape),
+        ],
+        out_shape=[
+            jax.ShapeDtypeStruct((1,), jnp.int32),
+            jax.ShapeDtypeStruct((copies,) + two.shape, bf16),
+            jax.ShapeDtypeStruct(three.shape, bf16),
+        ],
+        compiler_params=pltpu.CompilerParams(vmem_limit_bytes=VMEM_ALL),
+    )(loss_kind, two, three)
 
 
 def place_kernel(ids_ref, near_ref, far_ref, out_ref):
@@ -298,15 +332,16 @@
         1.0 / math.sqrt(full_rows * full_cols),
     )
     here = lax.axis_index("col")
-    ids = loss_kind[0, 0, :1] + 2 * here
     mine = lambda x: lax.dynamic_slice_in_dim(x, third_slab(here) * deep, deep, 0)
     part_three, first_three, second_three = mine(factor_three), mine(first_three), mine(second_three)
     start_one, start_two, start_three = (factor_one, factor_two, part_three)
-    twos = swap_all(to_all(factor_two.astype(bf16), n_row), "row")
+    threes = factor_three.reshape(tile_depth // deep, deep, rank)
+    ids, sent, threes = prepare(loss_kind, factor_two, threes, n_row)
+    twos = swap_all(sent, "row")
     near = gather_x(factor_one.astype(bf16))
     near_y = swap(near, Y_HI)
     ones = (near, near_y, swap(near, CORE), swap(near_y, CORE))
-    threes = (factor_three.reshape(tile_depth // deep, deep, rank),)
+    threes = (threes,)
     for iteration in range(ITERS):
         last = iteration == ITERS - 1
         counter = STEP + iteration + 1
@@ -332,7 +367,7 @@
         if not last:
             near_three = gather_x(part_three.astype(bf16))
             twos = swap_all(to_all(factor_two.astype(bf16), n_row), "row")
-            twos, near_y, near_three = lax.optimization_barrier((twos, near_y, near_three))
+            twos, near, near_y, near_three = lax.optimization_barrier((twos, near, near_y, near_three))
             ones = (near, near_y, swap(near, CORE), swap(near_y, CORE))
             threes = (near_three, swap(near_three, CORE))
     spread = learn_rate * ITERS

time: 137 us -> 137 us (level)
  Pallas kernels: 17.6 us -> 20.1 us
  local copies, waits for them, and re-layouts: 3.51 us -> 1.59 us
  other arithmetic: 5.37 us -> 3.96 us
    all_to_all x3, starting transfers between devices: 19.9 us -> 18 us  [swap_all(): return lax.all_to_all(parts, axis, 0, 0)]
    ppermute x30, starting transfers between devices: 50.3 us -> 52.2 us  [swap(): return lax.ppermute(part, 'col', [(i, i ^ code) for i in range(size)])]
    pallas_call x0 -> x1, Pallas kernels: none -> 1.62 us  [prepare(): pl.pallas_call(prepare_kernel, grid=(1,), in_specs=[pl.BlockSpec((1, 8, 1...]
    all_to_all x3, waiting for transfers between devices: 4.56 us -> 6.01 us  [swap_all(): return lax.all_to_all(parts, axis, 0, 0)]
  transfers between devices with their start and end apart: 33 -> 33, of which waited for: 15 -> 19; matrix products, arithmetic and copies ran while one was open for 3% -> 1% of each run, Pallas kernels for 3% -> 4%
where the time goes in v6:
time: 137 us; the launch traced here: 136 us
  starting transfers between devices  70.2 us (51%)
  waiting for transfers between devices  22.3 us (16%)
  Pallas kernels  20.1 us (15%)
  blocking collectives  17.2 us (13%)
  other arithmetic  3.96 us (3%)
  local copies, waits for them, and re-layouts  1.59 us (1%)
    ppermute x30, starting transfers between devices, swap(): return lax.ppermute(part, 'col', [(i, i ^ code) for i in range(size)])  52.2 us
    all_to_all x3, starting transfers between devices, swap_all(): return lax.all_to_all(parts, axis, 0, 0)  18 us
    all_to_all x1, blocking collectives, swap_all(): return lax.all_to_all(parts, axis, 0, 0)  17.2 us
    ppermute x30, waiting for transfers between devices, swap(): return lax.ppermute(part, 'col', [(i, i ^ code) for i in range(size)])  16.3 us
    pallas_call x2, Pallas kernels, slopes(): pl.pallas_call(functools.partial(slope_kernel, scales, stepped), grid=(ro...  13 us
    all_to_all x3, waiting for transfers between devices, swap_all(): return lax.all_to_all(parts, axis, 0, 0)  6.01 us
    pallas_call x2, Pallas kernels, second_grad(): pl.pallas_call(functools.partial(second_kernel, scale), grid=(rows // blo...  4.08 us
  transfers between devices with their start and end apart: 33, of which 19 were waited for; matrix products, arithmetic and copies ran while one was open for 1% of the time, Pallas kernels for 4%

profile of v6, /device:TPU:1, one launch (start us, length us, event | category | flops | bytes accessed | tf_op | source)
XLA Modules:
  0.0 136.4 jit_solution(8762672399161950740)
XLA Ops:
  1.4 3.6 %collective-permute-start.1 = (bf16[8,512]{1,0:T(8,128)(2,1)S(1)}, bf16[8,512]{1,0:T(8,128)(2,1)S(1)}, u32[]{:S(2)}, u32[]{:S(2)}) collective-permute-start(bf16[8,512]{1,0:T(8,128)(2,1)S(1)} %convert_element_type.70), channel_id=1, source_target_pairs={{0,8},{1,9},{2,10},{3,11},{4,12},{5,13},{6,14},{7,15},{8,0},{9,1},... | collective-permute-start | bytes 24584 | tf_op jit(solution)/shard_map/ppermute | solution.py:280
  7.4 9.3 %all-to-all-start = ((bf16[16,8,512]{2,1,0:T(8,128)(2,1)}), bf16[16,8,512]{2,1,0:T(8,128)(2,1)S(1)}, u32[]{:S(2)}, u32[]{:S(2)}) async-start(bf16[16,8,512]{2,1,0:T(8,128)(2,1)} %get-tuple-element.25), calls=%async_computation | async-start | bytes 262144 | tf_op jit(solution)/shard_map/all_to_all | solution.py:267
  16.8 2.7 %collective-permute-start.3 = (bf16[4,8,512]{2,1,0:T(8,128)(2,1)S(1)}, bf16[4,8,512]{2,1,0:T(8,128)(2,1)S(1)}, u32[]{:S(2)}, u32[]{:S(2)}) collective-permute-start(bf16[4,8,512]{2,1,0:T(8,128)(2,1)S(1)} %pad_maximum_fusion.3.near_ref), channel_id=1, source_target_pairs={{0,2},{1,3},{2,0},{3,1},{4,6},{5,7},{6,4},{7,5},{8,10},{9,11},{10,... | collective-permute-start | bytes 98312 | tf_op jit(solution)/shard_map/ppermute | solution.py:280
  21.3 2.7 %collective-permute-start.5 = (bf16[4,8,512]{2,1,0:T(8,128)(2,1)S(1)}, bf16[4,8,512]{2,1,0:T(8,128)(2,1)S(1)}, u32[]{:S(2)}, u32[]{:S(2)}) collective-permute-start(bf16[4,8,512]{2,1,0:T(8,128)(2,1)S(1)} %collective-permute-done.3.near_y_ref), channel_id=1, source_target_pairs={{0,1},{1,0},{2,3},{3,2},{4,5},{5,4},{6,7},{7,6},{8,9},{9,8},{10,11... | collective-permute-start | bytes 98312 | tf_op jit(solution)/shard_map/ppermute | solution.py:280
  26.1 7.1 %shard_map.131 = (bf16[12,8,512]{2,1,0:T(8,128)(2,1)S(1)}, bf16[12,8,512]{2,1,0:T(8,128)(2,1)S(1)}, bf16[128,64,128]{2,1,0:T(8,128)(2,1)S(1)}, bf16[16,8,512]{2,1,0:T(8,128)(2,1)S(1)}, bf16[8,8,512]{2,1,0:T(8,128)(2,1)S(1)}) custom-call(s32[1]{0:T(128)} %get-tuple-element.24.ids_ref, bf16[128,64,128]{2,1,0:T(8,128)(2,1)} %data_ref.3, ...), custom_call_target="tpu_custom_call" | custom-call | flops 4294967296 | bytes 4194304 | tf_op jit(solution)/shard_map/pallas_call | solution.py:137
  33.1 2.7 %collective-permute-start.6 = (bf16[12,8,512]{2,1,0:T(8,128)(2,1)S(1)}, bf16[12,8,512]{2,1,0:T(8,128)(2,1)S(1)}, u32[]{:S(2)}, u32[]{:S(2)}) collective-permute-start(bf16[12,8,512]{2,1,0:T(8,128)(2,1)S(1)} %get-tuple-element.28), channel_id=1, source_target_pairs={{0,1},{1,0},{2,3},{3,2},{4,5},{5,4},{6,7},{7,6},{8,9},{9,8},{10,11... | collective-permute-start | bytes 294920 | tf_op jit(solution)/shard_map/ppermute | solution.py:280
  36.9 2.7 %collective-permute-start.7 = (bf16[8,8,512]{2,1,0:T(8,128)(2,1)S(1)}, bf16[8,8,512]{2,1,0:T(8,128)(2,1)S(1)}, u32[]{:S(2)}, u32[]{:S(2)}) collective-permute-start(bf16[8,8,512]{2,1,0:T(8,128)(2,1)S(1)} %slice.74), channel_id=1, source_target_pairs={{0,2},{1,3},{2,0},{3,1},{4,6},{5,7},{6,4},{7,5},{8,10},{9,11},{10,... | collective-permute-start | bytes 196616 | tf_op jit(solution)/shard_map/ppermute | solution.py:280
  39.6 2.0 %collective-permute-done.7.got_ref = bf16[8,8,512]{2,1,0:T(8,128)(2,1)S(1)} collective-permute-done((bf16[8,8,512]{2,1,0:T(8,128)(2,1)S(1)}, bf16[8,8,512]{2,1,0:T(8,128)(2,1)S(1)}, u32[]{:S(2)}, u32[]{:S(2)}) %collective-permute-start.7) | collective-permute-done | bytes 65568 | tf_op jit(solution)/shard_map/ppermute | solution.py:280
  42.8 1.8 %collective-permute-start.10 = (bf16[2,8,512]{2,1,0:T(8,128)(2,1)S(1)}, bf16[2,8,512]{2,1,0:T(8,128)(2,1)S(1)}, u32[]{:S(2)}, u32[]{:S(2)}) collective-permute-start(bf16[2,8,512]{2,1,0:T(8,128)(2,1)S(1)} %get-tuple-element.51), channel_id=1, source_target_pairs={{0,12},{1,13},{2,14},{3,15},{4,8},{5,9},{6,10},{7,11},{8,4},{9,5},... | collective-permute-start | bytes 49160 | tf_op jit(solution)/shard_map/ppermute | solution.py:280
  45.4 2.0 %shard_map.133 = bf16[128,512]{1,0:T(8,128)(2,1)S(1)} custom-call(bf16[128,64,128]{2,1,0:T(8,128)(2,1)S(1)} %get-tuple-element.29.slope_ref, bf16[16,8,512]{2,1,0:T(8,128)(2,1)S(1)} %get-tuple-element.30.one_ref, bf16[8,8,512]{2,1,0:T(8,128)(2,1)S(1)} %get-tuple-element.31.three_ref), custom_call_target="tpu_custom_call" | custom-call | flops 2147483648 | bytes 2097152 | tf_op jit(solution)/shard_map/pallas_call | solution.py:198
  49.6 5.2 %all-to-all-start.1 = ((bf16[16,16,512]{2,1,0:T(8,128)(2,1)}), bf16[16,16,512]{2,1,0:T(8,128)(2,1)S(1)}, u32[]{:S(2)}, u32[]{:S(2)}) async-start(bf16[16,16,512]{2,1,0:T(8,128)(2,1)} %pad_maximum_fusion), calls=%async_computation.1 | async-start | bytes 524288 | tf_op jit(solution)/shard_map/all_to_all | solution.py:267
  59.8 4.8 %all-to-all-done.1 = bf16[16,16,512]{2,1,0:T(8,128)(2,1)S(1)} async-done(((bf16[16,16,512]{2,1,0:T(8,128)(2,1)}), bf16[16,16,512]{2,1,0:T(8,128)(2,1)S(1)}, u32[]{:S(2)}, u32[]{:S(2)}) %all-to-all-start.1) | async-done | bytes 262176 | tf_op jit(solution)/shard_map/all_to_all | solution.py:267
  66.1 3.5 %all-to-all-start.2 = ((bf16[16,8,512]{2,1,0:T(8,128)(2,1)}), bf16[16,8,512]{2,1,0:T(8,128)(2,1)S(1)}, u32[]{:S(2)}, u32[]{:S(2)}) async-start(bf16[16,8,512]{2,1,0:T(8,128)(2,1)} %broadcast_in_dim.24), calls=%async_computation.2 | async-start | bytes 262144 | tf_op jit(solution)/shard_map/all_to_all | solution.py:267
  72.9 2.4 %collective-permute-start.14 = (bf16[4,8,512]{2,1,0:T(8,128)(2,1)S(1)}, bf16[4,8,512]{2,1,0:T(8,128)(2,1)S(1)}, u32[]{:S(2)}, u32[]{:S(2)}) collective-permute-start(bf16[4,8,512]{2,1,0:T(8,128)(2,1)S(1)} %pad_maximum_fusion.4.near_ref), channel_id=1, source_target_pairs={{0,2},{1,3},{2,0},{3,1},{4,6},{5,7},{6,4},{7,5},{8,10},{9,11},{10,... | collective-permute-start | bytes 98312 | tf_op jit(solution)/shard_map/ppermute | solution.py:280
  75.4 1.8 %collective-permute-done.14.near_y_ref = bf16[4,8,512]{2,1,0:T(8,128)(2,1)S(1)} collective-permute-done((bf16[4,8,512]{2,1,0:T(8,128)(2,1)S(1)}, bf16[4,8,512]{2,1,0:T(8,128)(2,1)S(1)}, u32[]{:S(2)}, u32[]{:S(2)}) %collective-permute-start.14) | collective-permute-done | bytes 32800 | tf_op jit(solution)/shard_map/ppermute | solution.py:280
  78.1 5.9 %collective-permute-start.18 = (bf16[4,8,512]{2,1,0:T(8,128)(2,1)S(1)}, bf16[4,8,512]{2,1,0:T(8,128)(2,1)S(1)}, u32[]{:S(2)}, u32[]{:S(2)}) collective-permute-start(bf16[4,8,512]{2,1,0:T(8,128)(2,1)S(1)} %pad_maximum_fusion.4.near_ref), channel_id=1, source_target_pairs={{0,1},{1,0},{2,3},{3,2},{4,5},{5,4},{6,7},{7,6},{8,9},{9,8},{10,11... | collective-permute-start | bytes 98312 | tf_op jit(solution)/shard_map/ppermute | solution.py:280
  85.4 5.9 %shard_map.134 = (bf16[12,8,512]{2,1,0:T(8,128)(2,1)S(1)}, bf16[12,8,512]{2,1,0:T(8,128)(2,1)S(1)}, bf16[128,64,128]{2,1,0:T(8,128)(2,1)S(1)}, bf16[16,8,512]{2,1,0:T(8,128)(2,1)S(1)}, bf16[8,8,512]{2,1,0:T(8,128)(2,1)S(1)}) custom-call(s32[1]{0:T(128)} %get-tuple-element.24.ids_ref, bf16[128,64,128]{2,1,0:T(8,128)(2,1)S(1)} %copy-done, ...), custom_call_target="tpu_custom_call" | custom-call | flops 4294967296 | bytes 4194304 | tf_op jit(solution)/shard_map/pallas_call | solution.py:137
  93.0 2.5 %collective-permute-start.22 = (bf16[8,8,512]{2,1,0:T(8,128)(2,1)S(1)}, bf16[8,8,512]{2,1,0:T(8,128)(2,1)S(1)}, u32[]{:S(2)}, u32[]{:S(2)}) collective-permute-start(bf16[8,8,512]{2,1,0:T(8,128)(2,1)S(1)} %slice.83), channel_id=1, source_target_pairs={{0,2},{1,3},{2,0},{3,1},{4,6},{5,7},{6,4},{7,5},{8,10},{9,11},{10,... | collective-permute-start | bytes 196616 | tf_op jit(solution)/shard_map/ppermute | solution.py:280
  95.5 2.2 %collective-permute-done.22.got_ref = bf16[8,8,512]{2,1,0:T(8,128)(2,1)S(1)} collective-permute-done((bf16[8,8,512]{2,1,0:T(8,128)(2,1)S(1)}, bf16[8,8,512]{2,1,0:T(8,128)(2,1)S(1)}, u32[]{:S(2)}, u32[]{:S(2)}) %collective-permute-start.22) | collective-permute-done | bytes 65568 | tf_op jit(solution)/shard_map/ppermute | solution.py:280
  101.0 2.0 %shard_map.136 = bf16[128,512]{1,0:T(8,128)(2,1)S(1)} custom-call(bf16[128,64,128]{2,1,0:T(8,128)(2,1)S(1)} %get-tuple-element.40.slope_ref, bf16[16,8,512]{2,1,0:T(8,128)(2,1)S(1)} %get-tuple-element.41.one_ref, bf16[8,8,512]{2,1,0:T(8,128)(2,1)S(1)} %get-tuple-element.42.three_ref), custom_call_target="tpu_custom_call" | custom-call | flops 2147483648 | bytes 2097152 | tf_op jit(solution)/shard_map/pallas_call | solution.py:198
  104.1 17.2 %all_to_all.20 = bf16[16,16,512]{2,1,0:T(8,128)(2,1)S(1)} all-to-all(bf16[16,16,512]{2,1,0:T(8,128)(2,1)S(1)} %pad_maximum_fusion.1), channel_id=1, replica_groups=mesh['row'=16,'col'=16] {'row'}, dimensions={0} | all-to-all | bytes 524288 | tf_op jit(solution)/shard_map/all_to_all | solution.py:267
  122.1 1.9 %collective-permute-start.28 = (f32[8,512]{1,0:T(8,128)S(1)}, f32[8,512]{1,0:T(8,128)S(1)}, u32[]{:S(2)}, u32[]{:S(2)}) collective-permute-start(f32[8,512]{1,0:T(8,128)S(1)} %get-tuple-element.54), channel_id=1, source_target_pairs={{0,12},{1,13},{2,14},{3,15},{4,8},{5,9},{6,10},{7,11},{8,4},{9,5},... | collective-permute-start | bytes 49160 | tf_op jit(solution)/shard_map/ppermute | solution.py:280
  126.0 2.1 %collective-permute-done.27 = f32[8,512]{1,0:T(8,128)S(1)} collective-permute-done((f32[8,512]{1,0:T(8,128)S(1)}, f32[8,512]{1,0:T(8,128)S(1)}, u32[]{:S(2)}, u32[]{:S(2)}) %collective-permute-start.27) | collective-permute-done | bytes 16416 | tf_op jit(solution)/shard_map/ppermute | solution.py:280
  128.1 6.0 %collective-permute-start.29 = (f32[4,8,512]{2,1,0:T(8,128)S(1)}, f32[4,8,512]{2,1,0:T(8,128)S(1)}, u32[]{:S(2)}, u32[]{:S(2)}) collective-permute-start(f32[4,8,512]{2,1,0:T(8,128)S(1)} %pad_maximum_fusion.2.near_ref), channel_id=1, source_target_pairs={{0,1},{1,0},{2,3},{3,2},{4,5},{5,4},{6,7},{7,6},{8,9},{9,8},{10,11... | collective-permute-start | bytes 196616 | tf_op jit(solution)/shard_map/ppermute | solution.py:280
  (94 shorter events, 35.3 us)
Async XLA Ops:
  1.4 15.4 %collective-permute-start.1 = (bf16[8,512]{1,0:T(8,128)(2,1)S(1)}, bf16[8,512]{1,0:T(8,128)(2,1)S(1)}, u32[]{:S(2)}, u32[]{:S(2)}) collective-permute-start(bf16[8,512]{1,0:T(8,128)(2,1)S(1)} %convert_element_type.70), channel_id=1, source_target_pairs={{0,8},{1,9},{2,10},{3,11},{4,12},{5,13},{6,14},{7,15},{8,0},{9,1},... | collective-permute-start | bytes 24584 | tf_op jit(solution)/shard_map/ppermute | solution.py:280
  4.9 11.8 %collective-permute-start = (bf16[8,512]{1,0:T(8,128)(2,1)S(1)}, bf16[8,512]{1,0:T(8,128)(2,1)S(1)}, u32[]{:S(2)}, u32[]{:S(2)}) collective-permute-start(bf16[8,512]{1,0:T(8,128)(2,1)S(1)} %convert_element_type.70), channel_id=1, source_target_pairs={{0,4},{1,5},{2,6},{3,7},{4,0},{5,1},{6,2},{7,3},{8,12},{9,13},{10,... | collective-permute-start | bytes 24584 | tf_op jit(solution)/shard_map/ppermute | solution.py:280
  5.2 11.5 %collective-permute-start.2 = (bf16[8,512]{1,0:T(8,128)(2,1)S(1)}, bf16[8,512]{1,0:T(8,128)(2,1)S(1)}, u32[]{:S(2)}, u32[]{:S(2)}) collective-permute-start(bf16[8,512]{1,0:T(8,128)(2,1)S(1)} %convert_element_type.70), channel_id=1, source_target_pairs={{0,12},{1,13},{2,14},{3,15},{4,8},{5,9},{6,10},{7,11},{8,4},{9,5},... | collective-permute-start | bytes 24584 | tf_op jit(solution)/shard_map/ppermute | solution.py:280
  7.4 17.8 %all-to-all-start = ((bf16[16,8,512]{2,1,0:T(8,128)(2,1)}), bf16[16,8,512]{2,1,0:T(8,128)(2,1)S(1)}, u32[]{:S(2)}, u32[]{:S(2)}) async-start(bf16[16,8,512]{2,1,0:T(8,128)(2,1)} %get-tuple-element.25), calls=%async_computation | async-start | bytes 262144 | tf_op jit(solution)/shard_map/all_to_all | solution.py:267
  16.8 4.5 %collective-permute-start.3 = (bf16[4,8,512]{2,1,0:T(8,128)(2,1)S(1)}, bf16[4,8,512]{2,1,0:T(8,128)(2,1)S(1)}, u32[]{:S(2)}, u32[]{:S(2)}) collective-permute-start(bf16[4,8,512]{2,1,0:T(8,128)(2,1)S(1)} %pad_maximum_fusion.3.near_ref), channel_id=1, source_target_pairs={{0,2},{1,3},{2,0},{3,1},{4,6},{5,7},{6,4},{7,5},{8,10},{9,11},{10,... | collective-permute-start | bytes 98312 | tf_op jit(solution)/shard_map/ppermute | solution.py:280
  19.5 4.5 %collective-permute-start.4 = (bf16[4,8,512]{2,1,0:T(8,128)(2,1)S(1)}, bf16[4,8,512]{2,1,0:T(8,128)(2,1)S(1)}, u32[]{:S(2)}, u32[]{:S(2)}) collective-permute-start(bf16[4,8,512]{2,1,0:T(8,128)(2,1)S(1)} %pad_maximum_fusion.3.near_ref), channel_id=1, source_target_pairs={{0,1},{1,0},{2,3},{3,2},{4,5},{5,4},{6,7},{7,6},{8,9},{9,8},{10,11... | collective-permute-start | bytes 98312 | tf_op jit(solution)/shard_map/ppermute | solution.py:280
  36.9 4.7 %collective-permute-start.7 = (bf16[8,8,512]{2,1,0:T(8,128)(2,1)S(1)}, bf16[8,8,512]{2,1,0:T(8,128)(2,1)S(1)}, u32[]{:S(2)}, u32[]{:S(2)}) collective-permute-start(bf16[8,8,512]{2,1,0:T(8,128)(2,1)S(1)} %slice.74), channel_id=1, source_target_pairs={{0,2},{1,3},{2,0},{3,1},{4,6},{5,7},{6,4},{7,5},{8,10},{9,11},{10,... | collective-permute-start | bytes 196616 | tf_op jit(solution)/shard_map/ppermute | solution.py:280
  41.6 5.8 %collective-permute-start.8 = (bf16[2,8,512]{2,1,0:T(8,128)(2,1)S(1)}, bf16[2,8,512]{2,1,0:T(8,128)(2,1)S(1)}, u32[]{:S(2)}, u32[]{:S(2)}) collective-permute-start(bf16[2,8,512]{2,1,0:T(8,128)(2,1)S(1)} %get-tuple-element.50), channel_id=1, source_target_pairs={{0,4},{1,5},{2,6},{3,7},{4,0},{5,1},{6,2},{7,3},{8,12},{9,13},{10,... | collective-permute-start | bytes 49160 | tf_op jit(solution)/shard_map/ppermute | solution.py:280
  42.8 4.6 %collective-permute-start.10 = (bf16[2,8,512]{2,1,0:T(8,128)(2,1)S(1)}, bf16[2,8,512]{2,1,0:T(8,128)(2,1)S(1)}, u32[]{:S(2)}, u32[]{:S(2)}) collective-permute-start(bf16[2,8,512]{2,1,0:T(8,128)(2,1)S(1)} %get-tuple-element.51), channel_id=1, source_target_pairs={{0,12},{1,13},{2,14},{3,15},{4,8},{5,9},{6,10},{7,11},{8,4},{9,5},... | collective-permute-start | bytes 49160 | tf_op jit(solution)/shard_map/ppermute | solution.py:280
  44.7 4.1 %collective-permute-start.9 = (bf16[2,8,512]{2,1,0:T(8,128)(2,1)S(1)}, bf16[2,8,512]{2,1,0:T(8,128)(2,1)S(1)}, u32[]{:S(2)}, u32[]{:S(2)}) collective-permute-start(bf16[2,8,512]{2,1,0:T(8,128)(2,1)S(1)} %get-tuple-element.52), channel_id=1, source_target_pairs={{0,8},{1,9},{2,10},{3,11},{4,12},{5,13},{6,14},{7,15},{8,0},{9,1},... | collective-permute-start | bytes 49160 | tf_op jit(solution)/shard_map/ppermute | solution.py:280
  49.6 15.0 %all-to-all-start.1 = ((bf16[16,16,512]{2,1,0:T(8,128)(2,1)}), bf16[16,16,512]{2,1,0:T(8,128)(2,1)S(1)}, u32[]{:S(2)}, u32[]{:S(2)}) async-start(bf16[16,16,512]{2,1,0:T(8,128)(2,1)} %pad_maximum_fusion), calls=%async_computation.1 | async-start | bytes 524288 | tf_op jit(solution)/shard_map/all_to_all | solution.py:267
  55.7 4.0 %collective-permute-start.12 = (bf16[8,512]{1,0:T(8,128)(2,1)S(1)}, bf16[8,512]{1,0:T(8,128)(2,1)S(1)}, u32[]{:S(2)}, u32[]{:S(2)}) collective-permute-start(bf16[8,512]{1,0:T(8,128)(2,1)S(1)} %fusion.31), channel_id=1, source_target_pairs={{0,8},{1,9},{2,10},{3,11},{4,12},{5,13},{6,14},{7,15},{8,0},{9,1},... | collective-permute-start | bytes 24584 | tf_op jit(solution)/shard_map/ppermute | solution.py:280
  66.1 12.0 %all-to-all-start.2 = ((bf16[16,8,512]{2,1,0:T(8,128)(2,1)}), bf16[16,8,512]{2,1,0:T(8,128)(2,1)S(1)}, u32[]{:S(2)}, u32[]{:S(2)}) async-start(bf16[16,8,512]{2,1,0:T(8,128)(2,1)} %broadcast_in_dim.24), calls=%async_computation.2 | async-start | bytes 262144 | tf_op jit(solution)/shard_map/all_to_all | solution.py:267
  69.6 5.8 %collective-permute-start.17 = (bf16[8,512]{1,0:T(8,128)(2,1)S(1)}, bf16[8,512]{1,0:T(8,128)(2,1)S(1)}, u32[]{:S(2)}, u32[]{:S(2)}) collective-permute-start(bf16[8,512]{1,0:T(8,128)(2,1)S(1)} %get-tuple-element.45), channel_id=1, source_target_pairs={{0,12},{1,13},{2,14},{3,15},{4,8},{5,9},{6,10},{7,11},{8,4},{9,5},... | collective-permute-start | bytes 24584 | tf_op jit(solution)/shard_map/ppermute | solution.py:280
  71.1 4.3 %collective-permute-start.16 = (bf16[8,512]{1,0:T(8,128)(2,1)S(1)}, bf16[8,512]{1,0:T(8,128)(2,1)S(1)}, u32[]{:S(2)}, u32[]{:S(2)}) collective-permute-start(bf16[8,512]{1,0:T(8,128)(2,1)S(1)} %get-tuple-element.45), channel_id=1, source_target_pairs={{0,8},{1,9},{2,10},{3,11},{4,12},{5,13},{6,14},{7,15},{8,0},{9,1},... | collective-permute-start | bytes 24584 | tf_op jit(solution)/shard_map/ppermute | solution.py:280
  72.9 4.3 %collective-permute-start.14 = (bf16[4,8,512]{2,1,0:T(8,128)(2,1)S(1)}, bf16[4,8,512]{2,1,0:T(8,128)(2,1)S(1)}, u32[]{:S(2)}, u32[]{:S(2)}) collective-permute-start(bf16[4,8,512]{2,1,0:T(8,128)(2,1)S(1)} %pad_maximum_fusion.4.near_ref), channel_id=1, source_target_pairs={{0,2},{1,3},{2,0},{3,1},{4,6},{5,7},{6,4},{7,5},{8,10},{9,11},{10,... | collective-permute-start | bytes 98312 | tf_op jit(solution)/shard_map/ppermute | solution.py:280
  78.1 6.8 %collective-permute-start.18 = (bf16[4,8,512]{2,1,0:T(8,128)(2,1)S(1)}, bf16[4,8,512]{2,1,0:T(8,128)(2,1)S(1)}, u32[]{:S(2)}, u32[]{:S(2)}) collective-permute-start(bf16[4,8,512]{2,1,0:T(8,128)(2,1)S(1)} %pad_maximum_fusion.4.near_ref), channel_id=1, source_target_pairs={{0,1},{1,0},{2,3},{3,2},{4,5},{5,4},{6,7},{7,6},{8,9},{9,8},{10,11... | collective-permute-start | bytes 98312 | tf_op jit(solution)/shard_map/ppermute | solution.py:280
  93.0 4.7 %collective-permute-start.22 = (bf16[8,8,512]{2,1,0:T(8,128)(2,1)S(1)}, bf16[8,8,512]{2,1,0:T(8,128)(2,1)S(1)}, u32[]{:S(2)}, u32[]{:S(2)}) collective-permute-start(bf16[8,8,512]{2,1,0:T(8,128)(2,1)S(1)} %slice.83), channel_id=1, source_target_pairs={{0,2},{1,3},{2,0},{3,1},{4,6},{5,7},{6,4},{7,5},{8,10},{9,11},{10,... | collective-permute-start | bytes 196616 | tf_op jit(solution)/shard_map/ppermute | solution.py:280
  97.7 5.4 %collective-permute-start.23 = (bf16[2,8,512]{2,1,0:T(8,128)(2,1)S(1)}, bf16[2,8,512]{2,1,0:T(8,128)(2,1)S(1)}, u32[]{:S(2)}, u32[]{:S(2)}) collective-permute-start(bf16[2,8,512]{2,1,0:T(8,128)(2,1)S(1)} %get-tuple-element.47), channel_id=1, source_target_pairs={{0,4},{1,5},{2,6},{3,7},{4,0},{5,1},{6,2},{7,3},{8,12},{9,13},{10,... | collective-permute-start | bytes 49160 | tf_op jit(solution)/shard_map/ppermute | solution.py:280
  98.9 4.2 %collective-permute-start.25 = (bf16[2,8,512]{2,1,0:T(8,128)(2,1)S(1)}, bf16[2,8,512]{2,1,0:T(8,128)(2,1)S(1)}, u32[]{:S(2)}, u32[]{:S(2)}) collective-permute-start(bf16[2,8,512]{2,1,0:T(8,128)(2,1)S(1)} %get-tuple-element.48), channel_id=1, source_target_pairs={{0,12},{1,13},{2,14},{3,15},{4,8},{5,9},{6,10},{7,11},{8,4},{9,5},... | collective-permute-start | bytes 49160 | tf_op jit(solution)/shard_map/ppermute | solution.py:280
  99.8 4.2 %collective-permute-start.24 = (bf16[2,8,512]{2,1,0:T(8,128)(2,1)S(1)}, bf16[2,8,512]{2,1,0:T(8,128)(2,1)S(1)}, u32[]{:S(2)}, u32[]{:S(2)}) collective-permute-start(bf16[2,8,512]{2,1,0:T(8,128)(2,1)S(1)} %get-tuple-element.49), channel_id=1, source_target_pairs={{0,8},{1,9},{2,10},{3,11},{4,12},{5,13},{6,14},{7,15},{8,0},{9,1},... | collective-permute-start | bytes 49160 | tf_op jit(solution)/shard_map/ppermute | solution.py:280
  122.1 3.9 %collective-permute-start.28 = (f32[8,512]{1,0:T(8,128)S(1)}, f32[8,512]{1,0:T(8,128)S(1)}, u32[]{:S(2)}, u32[]{:S(2)}) collective-permute-start(f32[8,512]{1,0:T(8,128)S(1)} %get-tuple-element.54), channel_id=1, source_target_pairs={{0,12},{1,13},{2,14},{3,15},{4,8},{5,9},{6,10},{7,11},{8,4},{9,5},... | collective-permute-start | bytes 49160 | tf_op jit(solution)/shard_map/ppermute | solution.py:280
  124.0 4.1 %collective-permute-start.27 = (f32[8,512]{1,0:T(8,128)S(1)}, f32[8,512]{1,0:T(8,128)S(1)}, u32[]{:S(2)}, u32[]{:S(2)}) collective-permute-start(f32[8,512]{1,0:T(8,128)S(1)} %get-tuple-element.54), channel_id=1, source_target_pairs={{0,8},{1,9},{2,10},{3,11},{4,12},{5,13},{6,14},{7,15},{8,0},{9,1},... | collective-permute-start | bytes 49160 | tf_op jit(solution)/shard_map/ppermute | solution.py:280
  128.1 6.9 %collective-permute-start.29 = (f32[4,8,512]{2,1,0:T(8,128)S(1)}, f32[4,8,512]{2,1,0:T(8,128)S(1)}, u32[]{:S(2)}, u32[]{:S(2)}) collective-permute-start(f32[4,8,512]{2,1,0:T(8,128)S(1)} %pad_maximum_fusion.2.near_ref), channel_id=1, source_target_pairs={{0,1},{1,0},{2,3},{3,2},{4,5},{5,4},{6,7},{7,6},{8,9},{9,8},{10,11... | collective-permute-start | bytes 196616 | tf_op jit(solution)/shard_map/ppermute | solution.py:280
  (17 other events, 151.1 us)

commit v7 on v5

--- a/solution.py
+++ b/solution.py
@@ -13,6 +13,8 @@
 BLOCK = 64
 SUB = 4
 VMEM_LIMIT = 50 << 20
+VMEM_ALL = 61 << 20
+VMEM_LATER = 49 << 20
 
 learn_rate = 0.05
 beta_one = 0.8
@@ -38,20 +40,25 @@
     return col // X_ONE * 2 + col % 2
 
 
-def slope_kernel(scales, stepped, ids_ref, data_ref, two_ref, near_ref, near_y_ref, far_ref, far_y_ref, *refs):
+def slope_kernel(scales, stepped, kind_hbm, data_ref, two_ref, near_ref, near_y_ref, far_ref, far_y_ref, *refs):
     if stepped:
         near_three_ref, far_three_ref, *refs = refs
     else:
-        three_in_ref, *refs = refs
-    sent_ref, kept_ref, slope_ref, one_ref, three_ref, ga_acc, gc_acc = refs
+        three_hbm, *refs = refs
+    sent_ref, kept_ref, slope_ref, one_ref, three_ref, ga_acc, gc_acc, kind_ref, kind_sem, three_sem = refs
     step = pl.program_id(0)
     n_slab, own, rank = one_ref.shape
     depth = three_ref.shape[0] * three_ref.shape[1]
     cols = two_ref.shape[0] * two_ref.shape[1]
-    here = ids_ref[0] // 2
+    here = lax.axis_index("col")
 
     @pl.when(step == 0)
     def _():
+        kind_copy = pltpu.make_async_copy(kind_hbm.at[0, pl.ds(0, 8)], kind_ref, kind_sem)
+        kind_copy.start()
+        if not stepped:
+            three_copy = pltpu.make_async_copy(three_hbm, gc_acc, three_sem)
+            three_copy.start()
         for m in range(4):
             col = here ^ (m * X_ONE)
             one_ref[col] = near_ref[m]
@@ -61,8 +68,10 @@
             if stepped:
                 three_ref[third_slab(col)] = near_three_ref[m]
                 three_ref[third_slab(col ^ CORE)] = far_three_ref[m]
+        kind_copy.wait()
         if not stepped:
-            three_ref[...] = three_in_ref[...].astype(bf16)
+            three_copy.wait()
+            three_ref[...] = gc_acc[...].astype(bf16)
         gc_acc[...] = jnp.zeros_like(gc_acc)
 
     def run(logistic):
@@ -111,8 +120,8 @@
         ga_acc[pl.ds(step * slabs, slabs)] = jnp.concatenate(grad_one).reshape(slabs, own, rank)
         gc_acc[...] += grad_three.reshape(gc_acc.shape)
 
-    pl.when(ids_ref[0] % 2 == 1)(lambda: run(True))
-    pl.when(ids_ref[0] % 2 != 1)(lambda: run(False))
+    pl.when(kind_ref[0, 0] == 1)(lambda: run(True))
+    pl.when(kind_ref[0, 0] != 1)(lambda: run(False))
 
     @pl.when(step == pl.num_programs(0) - 1)
     def _():
@@ -124,7 +133,7 @@
                 out_ref[8 + m] = (ga_acc[col ^ Y_HI] * scales[0]).astype(bf16)
 
 
-def slopes(ids, tensor, twos, ones, threes, scales):
+def slopes(loss_kind, tensor, twos, ones, threes, scales):
     rows, depth, cols = tensor.shape
     own, rank = ones[0].shape[1:]
     slabs = rows // own
@@ -136,9 +145,10 @@
         functools.partial(slope_kernel, scales, stepped),
         grid=(rows // BLOCK,),
         in_specs=[
-            pl.BlockSpec(memory_space=pltpu.SMEM),
+            pl.BlockSpec(memory_space=pltpu.HBM),
             pl.BlockSpec((BLOCK, depth, cols), lambda i: (i, 0, 0)),
-            *[whole(x.shape) for x in (twos, *ones, *threes)],
+            *[whole(x.shape) for x in (twos, *ones)],
+            *([whole(x.shape) for x in threes] if stepped else [pl.BlockSpec(memory_space=pltpu.HBM)]),
         ],
         out_specs=[
             whole(swapped),
@@ -157,12 +167,15 @@
         scratch_shapes=[
             pltpu.VMEM((slabs, own, rank), f32),
             pltpu.VMEM(all_threes, f32),
+            pltpu.SMEM((8, cols), jnp.int32),
+            pltpu.SemaphoreType.DMA,
+            pltpu.SemaphoreType.DMA,
         ],
-        compiler_params=pltpu.CompilerParams(vmem_limit_bytes=VMEM_LIMIT),
+        compiler_params=pltpu.CompilerParams(vmem_limit_bytes=VMEM_LATER if stepped else VMEM_LIMIT),
         cost_estimate=pl.CostEstimate(
             flops=8 * rows * depth * cols * rank, bytes_accessed=4 << 20, transcendentals=rows * depth * cols
         ),
-    )(ids, tensor, twos, *ones, *threes)
+    )(loss_kind, tensor, twos, *ones, *threes)
 
 
 def second_kernel(scale, slope_ref, one_ref, three_ref, out_ref, acc):
@@ -211,22 +224,69 @@
     )(slope, ones, threes)
 
 
-def place_kernel(ids_ref, near_ref, far_ref, out_ref):
+def copies_kernel(part_ref, out_ref):
+    part = part_ref[...].astype(bf16)
+    for slab in range(out_ref.shape[0]):
+        out_ref[slab] = part
+
+
+def copies(part, size):
+    whole = lambda shape: pl.BlockSpec(shape, lambda i: (0,) * len(shape))
+    out = (size,) + part.shape
+    return pl.pallas_call(
+        copies_kernel,
+        grid=(1,),
+        in_specs=[whole(part.shape)],
+        out_specs=whole(out),
+        out_shape=jax.ShapeDtypeStruct(out, bf16),
+        compiler_params=pltpu.CompilerParams(vmem_limit_bytes=VMEM_ALL),
+    )(part)
+
+
+def place_kernel(near_ref, far_ref, out_ref):
     for m in range(4):
-        col = ids_ref[0] // 2 ^ (m * X_ONE)
+        col = lax.axis_index("col") ^ (m * X_ONE)
         out_ref[third_slab(col)] = near_ref[m]
         out_ref[third_slab(col ^ CORE)] = far_ref[m]
 
 
-def place_third(ids, near, far):
+def place_third(near, far):
     slabs, own, rank = near.shape
     return pl.pallas_call(
         place_kernel,
-        in_specs=[pl.BlockSpec(memory_space=pltpu.SMEM)] + [pl.BlockSpec(memory_space=pltpu.VMEM)] * 2,
+        in_specs=[pl.BlockSpec(memory_space=pltpu.VMEM)] * 2,
         out_specs=pl.BlockSpec(memory_space=pltpu.VMEM),
         out_shape=jax.ShapeDtypeStruct((2 * slabs, own, rank), near.dtype),
         compiler_params=pltpu.CompilerParams(vmem_limit_bytes=8 << 20),
-    )(ids, near, far)
+    )(near, far)
+
+
+def update_kernel(counter, got_ref, *refs):
+    two_in, three_in, two_out, three_out = refs[:3], refs[3:6], refs[6:9], refs[9:12]
+    twos_ref, half_ref = refs[12:]
+    own = two_in[0].shape[0]
+    got = jnp.sum(got_ref[...].astype(f32), axis=0)
+    for grad, old, new in ((got[:own], two_in, two_out), (got[own:], three_in, three_out)):
+        for ref, value in zip(new, adam_step(*[x[...] for x in old], grad, counter)):
+            ref[...] = value
+    two = two_out[0][...].astype(bf16)
+    for slab in range(twos_ref.shape[0]):
+        twos_ref[slab] = two
+    half_ref[...] = three_out[0][...].astype(bf16)
+
+
+def update(got, two, three, counter):
+    shapes = [jax.ShapeDtypeStruct(x.shape, f32) for x in (*two, *three)]
+    twos = jax.ShapeDtypeStruct((got.shape[0],) + two[0].shape, bf16)
+    vmem = pl.BlockSpec(memory_space=pltpu.VMEM)
+    out = pl.pallas_call(
+        functools.partial(update_kernel, counter),
+        in_specs=[vmem] * 7,
+        out_specs=[vmem] * 8,
+        out_shape=[*shapes, twos, jax.ShapeDtypeStruct(three[0].shape, bf16)],
+        compiler_params=pltpu.CompilerParams(vmem_limit_bytes=8 << 20),
+    )(got, *two, *three)
+    return out[:3], out[3:6], out[6], out[7]
 
 
 def swap_all(parts, axis):
@@ -298,11 +358,10 @@
         1.0 / math.sqrt(full_rows * full_cols),
     )
     here = lax.axis_index("col")
-    ids = loss_kind[0, 0, :1] + 2 * here
     mine = lambda x: lax.dynamic_slice_in_dim(x, third_slab(here) * deep, deep, 0)
     part_three, first_three, second_three = mine(factor_three), mine(first_three), mine(second_three)
     start_one, start_two, start_three = (factor_one, factor_two, part_three)
-    twos = swap_all(to_all(factor_two.astype(bf16), n_row), "row")
+    twos = swap_all(copies(factor_two, n_row), "row")
     near = gather_x(factor_one.astype(bf16))
     near_y = swap(near, Y_HI)
     ones = (near, near_y, swap(near, CORE), swap(near_y, CORE))
@@ -310,33 +369,39 @@
     for iteration in range(ITERS):
         last = iteration == ITERS - 1
         counter = STEP + iteration + 1
-        sent, kept, slope, all_ones, all_threes = slopes(ids, tensor, twos, ones, threes, scales)
+        sent, kept, slope, all_ones, all_threes = slopes(loss_kind, tensor, twos, ones, threes, scales)
         grad_two = second_grad(slope, all_ones, all_threes, scales[1]).reshape(n_row, own_two, rank)
         grad_one, grad_three = reduce_col(plus(kept, swap(sent, CORE)))
         sent = jnp.concatenate([grad_two, to_all(grad_three.astype(bf16), n_row)], axis=1)
         factor_one, first_one, second_one = adam_step(factor_one, first_one, second_one, grad_one, counter)
         got = swap_all(sent, "row")
-        if not last:
+        if last:
+            got = total(got)
+            grad_two, grad_three = got[:own_two], got[own_two:]
+            part_three, first_three, second_three = adam_step(
+                part_three, first_three, second_three, grad_three, counter
+            )
+            near_three = gather_x((start_three - part_three) / (learn_rate * ITERS))
+            near_three, grad_two = lax.optimization_barrier((near_three, grad_two))
+            factor_two, first_two, second_two = adam_step(
+                factor_two, first_two, second_two, grad_two, counter
+            )
+        else:
             near = gather_x(factor_one.astype(bf16))
             got, near = lax.optimization_barrier((got, near))
             near_y = swap(near, Y_HI)
-        got = total(got)
-        grad_two, grad_three = got[:own_two], got[own_two:]
-        part_three, first_three, second_three = adam_step(
-            part_three, first_three, second_three, grad_three, counter
-        )
-        if last:
-            near = gather_x((start_three - part_three) / (learn_rate * ITERS))
-            near, grad_two = lax.optimization_barrier((near, grad_two))
-        factor_two, first_two, second_two = adam_step(factor_two, first_two, second_two, grad_two, counter)
-        if not last:
-            near_three = gather_x(part_three.astype(bf16))
-            twos = swap_all(to_all(factor_two.astype(bf16), n_row), "row")
-            twos, near_y, near_three = lax.optimization_barrier((twos, near_y, near_three))
-            ones = (near, near_y, swap(near, CORE), swap(near_y, CORE))
-            threes = (near_three, swap(near_three, CORE))
+            two, three, sent, half_three = update(
+                got, (factor_two, first_two, second_two), (part_three, first_three, second_three), counter
+            )
+            factor_two, first_two, second_two = two
+            part_three, first_three, second_three = three
+            near_three = gather_x(half_three)
+            twos = swap_all(sent, "row")
+            far = swap(jnp.concatenate([near, near_y, near_three]), CORE)
+            ones = (near, near_y, far[:4], far[4:8])
+            threes = (near_three, far[8:])
     spread = learn_rate * ITERS
-    new_three = place_third(ids, near, swap(near, CORE)).reshape(tile_depth, rank)
+    new_three = place_third(near_three, swap(near_three, CORE)).reshape(tile_depth, rank)
     return ((start_one - factor_one) / spread, (start_two - factor_two) / spread, new_three)
 
 

time: 137 us -> 136 us (level)
  starting transfers between devices: 70.2 us -> 75.9 us
  blocking collectives: 17 us -> 12.2 us
  Pallas kernels: 17.6 us -> 19.9 us
  waiting for transfers between devices: 21.1 us -> 19.4 us
    ppermute x30 -> x28, starting transfers between devices: 50.3 us -> 57.4 us  [swap(): return lax.ppermute(part, 'col', [(i, i ^ code) for i in range(size)])]
    all_to_all x1, blocking collectives: 17 us -> 12.2 us  [swap_all(): return lax.all_to_all(parts, axis, 0, 0)]
    ppermute x30 -> x28, waiting for transfers between devices: 16.5 us -> 14.1 us  [swap(): return lax.ppermute(part, 'col', [(i, i ^ code) for i in range(size)])]
    pallas_call x1 -> x3, Pallas kernels: 0.68 us -> 2.8 us  [the longest x1 1.38 us: copies(): pl.pallas_call(copies_kernel, grid=(1,), in_specs=[whole(part.shape)], ou...]
    convert_element_type x2 -> x0, other arithmetic: 1.51 us -> none  [the longest x1 0.79 us: shards(): near_three = gather_x(part_three.astype(bf16))]
    dynamic_slice x0 -> x2, local copies, waits for them, and re-layouts: none -> 1.46 us  [shards(): lax.dynamic_slice_in_dim(x, third_slab(here) * deep, deep, 0)]
    all_to_all x3, starting transfers between devices: 19.9 us -> 18.5 us  [swap_all(): return lax.all_to_all(parts, axis, 0, 0)]
  transfers between devices with their start and end apart: 33 -> 31, of which waited for: 15 -> 13; matrix products, arithmetic and copies ran while one was open for 3% -> 3% of each run, Pallas kernels for 3% -> 4%
where the time goes in v7:
time: 136 us; the launch traced here: 135 us
  starting transfers between devices  75.9 us (56%)
  Pallas kernels  19.9 us (15%)
  waiting for transfers between devices  19.4 us (14%)
  blocking collectives  12.2 us (9%)
  other arithmetic  4.4 us (3%)
  local copies, waits for them, and re-layouts  2.48 us (2%)
    ppermute x28, starting transfers between devices, swap(): return lax.ppermute(part, 'col', [(i, i ^ code) for i in range(size)])  57.4 us
    all_to_all x3, starting transfers between devices, swap_all(): return lax.all_to_all(parts, axis, 0, 0)  18.5 us
    ppermute x28, waiting for transfers between devices, swap(): return lax.ppermute(part, 'col', [(i, i ^ code) for i in range(size)])  14.1 us
    pallas_call x2, Pallas kernels, slopes(): pl.pallas_call(functools.partial(slope_kernel, scales, stepped), grid=(ro...  13 us
    all_to_all x1, blocking collectives, swap_all(): return lax.all_to_all(parts, axis, 0, 0)  12.2 us
    all_to_all x3, waiting for transfers between devices, swap_all(): return lax.all_to_all(parts, axis, 0, 0)  5.32 us
    pallas_call x2, Pallas kernels, second_grad(): pl.pallas_call(functools.partial(second_kernel, scale), grid=(rows // blo...  4.08 us
  transfers between devices with their start and end apart: 31, of which 13 were waited for; matrix products, arithmetic and copies ran while one was open for 3% of the time, Pallas kernels for 4%

profile of v7, /device:TPU:1, one launch (start us, length us, event | category | flops | bytes accessed | tf_op | source)
XLA Modules:
  0.0 135.3 jit_solution(10347041601575145247)
XLA Ops:
  1.4 3.6 %collective-permute-start.1 = (bf16[8,512]{1,0:T(8,128)(2,1)S(1)}, bf16[8,512]{1,0:T(8,128)(2,1)S(1)}, u32[]{:S(2)}, u32[]{:S(2)}) collective-permute-start(bf16[8,512]{1,0:T(8,128)(2,1)S(1)} %convert_element_type.61), channel_id=1, source_target_pairs={{0,8},{1,9},{2,10},{3,11},{4,12},{5,13},{6,14},{7,15},{8,0},{9,1},... | collective-permute-start | bytes 24584 | tf_op jit(solution)/shard_map/ppermute | solution.py:306
  7.2 9.3 %all-to-all-start = ((bf16[16,8,512]{2,1,0:T(8,128)(2,1)}), bf16[16,8,512]{2,1,0:T(8,128)(2,1)S(1)}, u32[]{:S(2)}, u32[]{:S(2)}) async-start(bf16[16,8,512]{2,1,0:T(8,128)(2,1)} %shard_map.130), calls=%async_computation | async-start | bytes 262144 | tf_op jit(solution)/shard_map/all_to_all | solution.py:293
  17.2 2.7 %collective-permute-start.3 = (bf16[4,8,512]{2,1,0:T(8,128)(2,1)S(1)}, bf16[4,8,512]{2,1,0:T(8,128)(2,1)S(1)}, u32[]{:S(2)}, u32[]{:S(2)}) collective-permute-start(bf16[4,8,512]{2,1,0:T(8,128)(2,1)S(1)} %pad_maximum_fusion.3.near_ref), channel_id=1, source_target_pairs={{0,2},{1,3},{2,0},{3,1},{4,6},{5,7},{6,4},{7,5},{8,10},{9,11},{10,... | collective-permute-start | bytes 98312 | tf_op jit(solution)/shard_map/ppermute | solution.py:306
  19.9 1.8 %collective-permute-start.4 = (bf16[4,8,512]{2,1,0:T(8,128)(2,1)S(1)}, bf16[4,8,512]{2,1,0:T(8,128)(2,1)S(1)}, u32[]{:S(2)}, u32[]{:S(2)}) collective-permute-start(bf16[4,8,512]{2,1,0:T(8,128)(2,1)S(1)} %pad_maximum_fusion.3.near_ref), channel_id=1, source_target_pairs={{0,1},{1,0},{2,3},{3,2},{4,5},{5,4},{6,7},{7,6},{8,9},{9,8},{10,11... | collective-permute-start | bytes 98312 | tf_op jit(solution)/shard_map/ppermute | solution.py:306
  21.7 2.5 %collective-permute-start.5 = (bf16[4,8,512]{2,1,0:T(8,128)(2,1)S(1)}, bf16[4,8,512]{2,1,0:T(8,128)(2,1)S(1)}, u32[]{:S(2)}, u32[]{:S(2)}) collective-permute-start(bf16[4,8,512]{2,1,0:T(8,128)(2,1)S(1)} %collective-permute-done.3.near_y_ref), channel_id=1, source_target_pairs={{0,1},{1,0},{2,3},{3,2},{4,5},{5,4},{6,7},{7,6},{8,9},{9,8},{10,11... | collective-permute-start | bytes 98312 | tf_op jit(solution)/shard_map/ppermute | solution.py:306
  26.0 7.1 %shard_map.131 = (bf16[12,8,512]{2,1,0:T(8,128)(2,1)S(1)}, bf16[12,8,512]{2,1,0:T(8,128)(2,1)S(1)}, bf16[128,64,128]{2,1,0:T(8,128)(2,1)S(1)}, bf16[16,8,512]{2,1,0:T(8,128)(2,1)S(1)}, bf16[8,8,512]{2,1,0:T(8,128)(2,1)S(1)}) custom-call(s32[128,64,128]{2,1,0:T(8,128)} %kind_hbm.3, bf16[128,64,128]{2,1,0:T(8,128)(2,1)} %data_ref.3, ...), custom_call_target="tpu_custom_call" | custom-call | flops 4294967296 | bytes 4194304 | tf_op jit(solution)/shard_map/pallas_call | solution.py:144
  33.1 2.6 %collective-permute-start.6 = (bf16[12,8,512]{2,1,0:T(8,128)(2,1)S(1)}, bf16[12,8,512]{2,1,0:T(8,128)(2,1)S(1)}, u32[]{:S(2)}, u32[]{:S(2)}) collective-permute-start(bf16[12,8,512]{2,1,0:T(8,128)(2,1)S(1)} %get-tuple-element.26), channel_id=1, source_target_pairs={{0,1},{1,0},{2,3},{3,2},{4,5},{5,4},{6,7},{7,6},{8,9},{9,8},{10,11... | collective-permute-start | bytes 294920 | tf_op jit(solution)/shard_map/ppermute | solution.py:306
  36.7 2.7 %collective-permute-start.7 = (bf16[8,8,512]{2,1,0:T(8,128)(2,1)S(1)}, bf16[8,8,512]{2,1,0:T(8,128)(2,1)S(1)}, u32[]{:S(2)}, u32[]{:S(2)}) collective-permute-start(bf16[8,8,512]{2,1,0:T(8,128)(2,1)S(1)} %slice.78), channel_id=1, source_target_pairs={{0,2},{1,3},{2,0},{3,1},{4,6},{5,7},{6,4},{7,5},{8,10},{9,11},{10,... | collective-permute-start | bytes 196616 | tf_op jit(solution)/shard_map/ppermute | solution.py:306
  39.4 2.0 %collective-permute-done.7.got_ref = bf16[8,8,512]{2,1,0:T(8,128)(2,1)S(1)} collective-permute-done((bf16[8,8,512]{2,1,0:T(8,128)(2,1)S(1)}, bf16[8,8,512]{2,1,0:T(8,128)(2,1)S(1)}, u32[]{:S(2)}, u32[]{:S(2)}) %collective-permute-start.7) | collective-permute-done | bytes 65568 | tf_op jit(solution)/shard_map/ppermute | solution.py:306
  42.7 1.9 %collective-permute-start.10 = (bf16[2,8,512]{2,1,0:T(8,128)(2,1)S(1)}, bf16[2,8,512]{2,1,0:T(8,128)(2,1)S(1)}, u32[]{:S(2)}, u32[]{:S(2)}) collective-permute-start(bf16[2,8,512]{2,1,0:T(8,128)(2,1)S(1)} %get-tuple-element.54), channel_id=1, source_target_pairs={{0,12},{1,13},{2,14},{3,15},{4,8},{5,9},{6,10},{7,11},{8,4},{9,5},... | collective-permute-start | bytes 49160 | tf_op jit(solution)/shard_map/ppermute | solution.py:306
  45.2 2.0 %shard_map.133 = bf16[128,512]{1,0:T(8,128)(2,1)S(1)} custom-call(bf16[128,64,128]{2,1,0:T(8,128)(2,1)S(1)} %get-tuple-element.27.slope_ref, bf16[16,8,512]{2,1,0:T(8,128)(2,1)S(1)} %get-tuple-element.28.one_ref, bf16[8,8,512]{2,1,0:T(8,128)(2,1)S(1)} %get-tuple-element.29.three_ref), custom_call_target="tpu_custom_call" | custom-call | flops 2147483648 | bytes 2097152 | tf_op jit(solution)/shard_map/pallas_call | solution.py:209
  49.4 5.7 %all-to-all-start.1 = ((bf16[16,16,512]{2,1,0:T(8,128)(2,1)}), bf16[16,16,512]{2,1,0:T(8,128)(2,1)S(1)}, u32[]{:S(2)}, u32[]{:S(2)}) async-start(bf16[16,16,512]{2,1,0:T(8,128)(2,1)} %pad_maximum_fusion), calls=%async_computation.1 | async-start | bytes 524288 | tf_op jit(solution)/shard_map/all_to_all | solution.py:293
  60.8 4.0 %all-to-all-done.1.got_ref = bf16[16,16,512]{2,1,0:T(8,128)(2,1)S(1)} async-done(((bf16[16,16,512]{2,1,0:T(8,128)(2,1)}), bf16[16,16,512]{2,1,0:T(8,128)(2,1)S(1)}, u32[]{:S(2)}, u32[]{:S(2)}) %all-to-all-start.1) | async-done | bytes 262176 | tf_op jit(solution)/shard_map/all_to_all | solution.py:293
  68.8 2.6 %collective-permute-start.14 = (bf16[4,8,512]{2,1,0:T(8,128)(2,1)S(1)}, bf16[4,8,512]{2,1,0:T(8,128)(2,1)S(1)}, u32[]{:S(2)}, u32[]{:S(2)}) collective-permute-start(bf16[4,8,512]{2,1,0:T(8,128)(2,1)S(1)} %pad_maximum_fusion.4.near_ref), channel_id=1, source_target_pairs={{0,2},{1,3},{2,0},{3,1},{4,6},{5,7},{6,4},{7,5},{8,10},{9,11},{10,... | collective-permute-start | bytes 98312 | tf_op jit(solution)/shard_map/ppermute | solution.py:306
  71.4 3.5 %all-to-all-start.2 = ((bf16[16,8,512]{2,1,0:T(8,128)(2,1)}), bf16[16,8,512]{2,1,0:T(8,128)(2,1)S(1)}, u32[]{:S(2)}, u32[]{:S(2)}) async-start(bf16[16,8,512]{2,1,0:T(8,128)(2,1)} %get-tuple-element.31), calls=%async_computation.2 | async-start | bytes 262144 | tf_op jit(solution)/shard_map/all_to_all | solution.py:293
  75.1 6.2 %collective-permute-start.18 = (bf16[12,8,512]{2,1,0:T(8,128)(2,1)S(1)}, bf16[12,8,512]{2,1,0:T(8,128)(2,1)S(1)}, u32[]{:S(2)}, u32[]{:S(2)}) collective-permute-start(bf16[12,8,512]{2,1,0:T(8,128)(2,1)S(1)} %constant_dynamic-update-slice_fusion), channel_id=1, source_target_pairs={{0,1},{1,0},{2,3},{3,2},{4,5},{5,4},{6,7},{7,6},{8,9},{9,8},{10,11... | collective-permute-start | bytes 294920 | tf_op jit(solution)/shard_map/ppermute | solution.py:306
  83.5 5.9 %shard_map.135 = (bf16[12,8,512]{2,1,0:T(8,128)(2,1)S(1)}, bf16[12,8,512]{2,1,0:T(8,128)(2,1)S(1)}, bf16[128,64,128]{2,1,0:T(8,128)(2,1)S(1)}, bf16[16,8,512]{2,1,0:T(8,128)(2,1)S(1)}, bf16[8,8,512]{2,1,0:T(8,128)(2,1)S(1)}) custom-call(s32[128,64,128]{2,1,0:T(8,128)} %kind_hbm.3, bf16[128,64,128]{2,1,0:T(8,128)(2,1)S(1)} %copy-done.4, ...), custom_call_target="tpu_custom_call" | custom-call | flops 4294967296 | bytes 4194304 | tf_op jit(solution)/shard_map/pallas_call | solution.py:144
  89.4 7.3 %collective-permute-start.19 = (bf16[12,8,512]{2,1,0:T(8,128)(2,1)S(1)}, bf16[12,8,512]{2,1,0:T(8,128)(2,1)S(1)}, u32[]{:S(2)}, u32[]{:S(2)}) collective-permute-start(bf16[12,8,512]{2,1,0:T(8,128)(2,1)S(1)} %get-tuple-element.35), channel_id=1, source_target_pairs={{0,1},{1,0},{2,3},{3,2},{4,5},{5,4},{6,7},{7,6},{8,9},{9,8},{10,11... | collective-permute-start | bytes 294920 | tf_op jit(solution)/shard_map/ppermute | solution.py:306
  99.3 3.1 %collective-permute-done.20.got_ref = bf16[8,8,512]{2,1,0:T(8,128)(2,1)S(1)} collective-permute-done((bf16[8,8,512]{2,1,0:T(8,128)(2,1)S(1)}, bf16[8,8,512]{2,1,0:T(8,128)(2,1)S(1)}, u32[]{:S(2)}, u32[]{:S(2)}) %collective-permute-start.20) | collective-permute-done | bytes 65568 | tf_op jit(solution)/shard_map/ppermute | solution.py:306
  106.0 2.0 %shard_map.137 = bf16[128,512]{1,0:T(8,128)(2,1)S(1)} custom-call(bf16[128,64,128]{2,1,0:T(8,128)(2,1)S(1)} %get-tuple-element.40.slope_ref, bf16[16,8,512]{2,1,0:T(8,128)(2,1)S(1)} %get-tuple-element.41.one_ref, bf16[8,8,512]{2,1,0:T(8,128)(2,1)S(1)} %get-tuple-element.42.three_ref), custom_call_target="tpu_custom_call" | custom-call | flops 2147483648 | bytes 2097152 | tf_op jit(solution)/shard_map/pallas_call | solution.py:209
  109.0 12.2 %all_to_all.20 = bf16[16,16,512]{2,1,0:T(8,128)(2,1)S(1)} all-to-all(bf16[16,16,512]{2,1,0:T(8,128)(2,1)S(1)} %pad_maximum_fusion.1), channel_id=1, replica_groups=mesh['row'=16,'col'=16] {'row'}, dimensions={0} | all-to-all | bytes 524288 | tf_op jit(solution)/shard_map/all_to_all | solution.py:293
  122.0 1.7 %collective-permute-start.26 = (f32[8,512]{1,0:T(8,128)S(1)}, f32[8,512]{1,0:T(8,128)S(1)}, u32[]{:S(2)}, u32[]{:S(2)}) collective-permute-start(f32[8,512]{1,0:T(8,128)S(1)} %get-tuple-element.57), channel_id=1, source_target_pairs={{0,12},{1,13},{2,14},{3,15},{4,8},{5,9},{6,10},{7,11},{8,4},{9,5},... | collective-permute-start | bytes 49160 | tf_op jit(solution)/shard_map/ppermute | solution.py:306
  126.0 1.8 %collective-permute-done.25 = f32[8,512]{1,0:T(8,128)S(1)} collective-permute-done((f32[8,512]{1,0:T(8,128)S(1)}, f32[8,512]{1,0:T(8,128)S(1)}, u32[]{:S(2)}, u32[]{:S(2)}) %collective-permute-start.25) | collective-permute-done | bytes 16416 | tf_op jit(solution)/shard_map/ppermute | solution.py:306
  127.9 5.8 %collective-permute-start.27 = (f32[4,8,512]{2,1,0:T(8,128)S(1)}, f32[4,8,512]{2,1,0:T(8,128)S(1)}, u32[]{:S(2)}, u32[]{:S(2)}) collective-permute-start(f32[4,8,512]{2,1,0:T(8,128)S(1)} %pad_maximum_fusion.2.near_ref), channel_id=1, source_target_pairs={{0,1},{1,0},{2,3},{3,2},{4,5},{5,4},{6,7},{7,6},{8,9},{9,8},{10,11... | collective-permute-start | bytes 196616 | tf_op jit(solution)/shard_map/ppermute | solution.py:306
  (98 shorter events, 34.3 us)
Async XLA Ops:
  1.4 15.9 %collective-permute-start.1 = (bf16[8,512]{1,0:T(8,128)(2,1)S(1)}, bf16[8,512]{1,0:T(8,128)(2,1)S(1)}, u32[]{:S(2)}, u32[]{:S(2)}) collective-permute-start(bf16[8,512]{1,0:T(8,128)(2,1)S(1)} %convert_element_type.61), channel_id=1, source_target_pairs={{0,8},{1,9},{2,10},{3,11},{4,12},{5,13},{6,14},{7,15},{8,0},{9,1},... | collective-permute-start | bytes 24584 | tf_op jit(solution)/shard_map/ppermute | solution.py:306
  4.9 12.3 %collective-permute-start = (bf16[8,512]{1,0:T(8,128)(2,1)S(1)}, bf16[8,512]{1,0:T(8,128)(2,1)S(1)}, u32[]{:S(2)}, u32[]{:S(2)}) collective-permute-start(bf16[8,512]{1,0:T(8,128)(2,1)S(1)} %convert_element_type.61), channel_id=1, source_target_pairs={{0,4},{1,5},{2,6},{3,7},{4,0},{5,1},{6,2},{7,3},{8,12},{9,13},{10,... | collective-permute-start | bytes 24584 | tf_op jit(solution)/shard_map/ppermute | solution.py:306
  5.2 12.0 %collective-permute-start.2 = (bf16[8,512]{1,0:T(8,128)(2,1)S(1)}, bf16[8,512]{1,0:T(8,128)(2,1)S(1)}, u32[]{:S(2)}, u32[]{:S(2)}) collective-permute-start(bf16[8,512]{1,0:T(8,128)(2,1)S(1)} %convert_element_type.61), channel_id=1, source_target_pairs={{0,12},{1,13},{2,14},{3,15},{4,8},{5,9},{6,10},{7,11},{8,4},{9,5},... | collective-permute-start | bytes 24584 | tf_op jit(solution)/shard_map/ppermute | solution.py:306
  7.2 18.0 %all-to-all-start = ((bf16[16,8,512]{2,1,0:T(8,128)(2,1)}), bf16[16,8,512]{2,1,0:T(8,128)(2,1)S(1)}, u32[]{:S(2)}, u32[]{:S(2)}) async-start(bf16[16,8,512]{2,1,0:T(8,128)(2,1)} %shard_map.130), calls=%async_computation | async-start | bytes 262144 | tf_op jit(solution)/shard_map/all_to_all | solution.py:293
  17.2 4.5 %collective-permute-start.3 = (bf16[4,8,512]{2,1,0:T(8,128)(2,1)S(1)}, bf16[4,8,512]{2,1,0:T(8,128)(2,1)S(1)}, u32[]{:S(2)}, u32[]{:S(2)}) collective-permute-start(bf16[4,8,512]{2,1,0:T(8,128)(2,1)S(1)} %pad_maximum_fusion.3.near_ref), channel_id=1, source_target_pairs={{0,2},{1,3},{2,0},{3,1},{4,6},{5,7},{6,4},{7,5},{8,10},{9,11},{10,... | collective-permute-start | bytes 98312 | tf_op jit(solution)/shard_map/ppermute | solution.py:306
  19.9 4.3 %collective-permute-start.4 = (bf16[4,8,512]{2,1,0:T(8,128)(2,1)S(1)}, bf16[4,8,512]{2,1,0:T(8,128)(2,1)S(1)}, u32[]{:S(2)}, u32[]{:S(2)}) collective-permute-start(bf16[4,8,512]{2,1,0:T(8,128)(2,1)S(1)} %pad_maximum_fusion.3.near_ref), channel_id=1, source_target_pairs={{0,1},{1,0},{2,3},{3,2},{4,5},{5,4},{6,7},{7,6},{8,9},{9,8},{10,11... | collective-permute-start | bytes 98312 | tf_op jit(solution)/shard_map/ppermute | solution.py:306
  36.7 4.7 %collective-permute-start.7 = (bf16[8,8,512]{2,1,0:T(8,128)(2,1)S(1)}, bf16[8,8,512]{2,1,0:T(8,128)(2,1)S(1)}, u32[]{:S(2)}, u32[]{:S(2)}) collective-permute-start(bf16[8,8,512]{2,1,0:T(8,128)(2,1)S(1)} %slice.78), channel_id=1, source_target_pairs={{0,2},{1,3},{2,0},{3,1},{4,6},{5,7},{6,4},{7,5},{8,10},{9,11},{10,... | collective-permute-start | bytes 196616 | tf_op jit(solution)/shard_map/ppermute | solution.py:306
  41.4 5.8 %collective-permute-start.8 = (bf16[2,8,512]{2,1,0:T(8,128)(2,1)S(1)}, bf16[2,8,512]{2,1,0:T(8,128)(2,1)S(1)}, u32[]{:S(2)}, u32[]{:S(2)}) collective-permute-start(bf16[2,8,512]{2,1,0:T(8,128)(2,1)S(1)} %get-tuple-element.53), channel_id=1, source_target_pairs={{0,4},{1,5},{2,6},{3,7},{4,0},{5,1},{6,2},{7,3},{8,12},{9,13},{10,... | collective-permute-start | bytes 49160 | tf_op jit(solution)/shard_map/ppermute | solution.py:306
  42.7 4.6 %collective-permute-start.10 = (bf16[2,8,512]{2,1,0:T(8,128)(2,1)S(1)}, bf16[2,8,512]{2,1,0:T(8,128)(2,1)S(1)}, u32[]{:S(2)}, u32[]{:S(2)}) collective-permute-start(bf16[2,8,512]{2,1,0:T(8,128)(2,1)S(1)} %get-tuple-element.54), channel_id=1, source_target_pairs={{0,12},{1,13},{2,14},{3,15},{4,8},{5,9},{6,10},{7,11},{8,4},{9,5},... | collective-permute-start | bytes 49160 | tf_op jit(solution)/shard_map/ppermute | solution.py:306
  44.5 4.1 %collective-permute-start.9 = (bf16[2,8,512]{2,1,0:T(8,128)(2,1)S(1)}, bf16[2,8,512]{2,1,0:T(8,128)(2,1)S(1)}, u32[]{:S(2)}, u32[]{:S(2)}) collective-permute-start(bf16[2,8,512]{2,1,0:T(8,128)(2,1)S(1)} %get-tuple-element.55), channel_id=1, source_target_pairs={{0,8},{1,9},{2,10},{3,11},{4,12},{5,13},{6,14},{7,15},{8,0},{9,1},... | collective-permute-start | bytes 49160 | tf_op jit(solution)/shard_map/ppermute | solution.py:306
  49.4 15.4 %all-to-all-start.1 = ((bf16[16,16,512]{2,1,0:T(8,128)(2,1)}), bf16[16,16,512]{2,1,0:T(8,128)(2,1)S(1)}, u32[]{:S(2)}, u32[]{:S(2)}) async-start(bf16[16,16,512]{2,1,0:T(8,128)(2,1)} %pad_maximum_fusion), calls=%async_computation.1 | async-start | bytes 524288 | tf_op jit(solution)/shard_map/all_to_all | solution.py:293
  65.6 9.5 %collective-permute-start.17 = (bf16[8,512]{1,0:T(8,128)(2,1)S(1)}, bf16[8,512]{1,0:T(8,128)(2,1)S(1)}, u32[]{:S(2)}, u32[]{:S(2)}) collective-permute-start(bf16[8,512]{1,0:T(8,128)(2,1)S(1)} %get-tuple-element.33), channel_id=1, source_target_pairs={{0,12},{1,13},{2,14},{3,15},{4,8},{5,9},{6,10},{7,11},{8,4},{9,5},... | collective-permute-start | bytes 24584 | tf_op jit(solution)/shard_map/ppermute | solution.py:306
  66.5 8.6 %collective-permute-start.16 = (bf16[8,512]{1,0:T(8,128)(2,1)S(1)}, bf16[8,512]{1,0:T(8,128)(2,1)S(1)}, u32[]{:S(2)}, u32[]{:S(2)}) collective-permute-start(bf16[8,512]{1,0:T(8,128)(2,1)S(1)} %get-tuple-element.33), channel_id=1, source_target_pairs={{0,8},{1,9},{2,10},{3,11},{4,12},{5,13},{6,14},{7,15},{8,0},{9,1},... | collective-permute-start | bytes 24584 | tf_op jit(solution)/shard_map/ppermute | solution.py:306
  67.7 7.3 %collective-permute-start.15 = (bf16[8,512]{1,0:T(8,128)(2,1)S(1)}, bf16[8,512]{1,0:T(8,128)(2,1)S(1)}, u32[]{:S(2)}, u32[]{:S(2)}) collective-permute-start(bf16[8,512]{1,0:T(8,128)(2,1)S(1)} %get-tuple-element.33), channel_id=1, source_target_pairs={{0,4},{1,5},{2,6},{3,7},{4,0},{5,1},{6,2},{7,3},{8,12},{9,13},{10,... | collective-permute-start | bytes 24584 | tf_op jit(solution)/shard_map/ppermute | solution.py:306
  68.8 6.1 %collective-permute-start.14 = (bf16[4,8,512]{2,1,0:T(8,128)(2,1)S(1)}, bf16[4,8,512]{2,1,0:T(8,128)(2,1)S(1)}, u32[]{:S(2)}, u32[]{:S(2)}) collective-permute-start(bf16[4,8,512]{2,1,0:T(8,128)(2,1)S(1)} %pad_maximum_fusion.4.near_ref), channel_id=1, source_target_pairs={{0,2},{1,3},{2,0},{3,1},{4,6},{5,7},{6,4},{7,5},{8,10},{9,11},{10,... | collective-permute-start | bytes 98312 | tf_op jit(solution)/shard_map/ppermute | solution.py:306
  71.4 12.0 %all-to-all-start.2 = ((bf16[16,8,512]{2,1,0:T(8,128)(2,1)}), bf16[16,8,512]{2,1,0:T(8,128)(2,1)S(1)}, u32[]{:S(2)}, u32[]{:S(2)}) async-start(bf16[16,8,512]{2,1,0:T(8,128)(2,1)} %get-tuple-element.31), calls=%async_computation.2 | async-start | bytes 262144 | tf_op jit(solution)/shard_map/all_to_all | solution.py:293
  75.1 7.1 %collective-permute-start.18 = (bf16[12,8,512]{2,1,0:T(8,128)(2,1)S(1)}, bf16[12,8,512]{2,1,0:T(8,128)(2,1)S(1)}, u32[]{:S(2)}, u32[]{:S(2)}) collective-permute-start(bf16[12,8,512]{2,1,0:T(8,128)(2,1)S(1)} %constant_dynamic-update-slice_fusion), channel_id=1, source_target_pairs={{0,1},{1,0},{2,3},{3,2},{4,5},{5,4},{6,7},{7,6},{8,9},{9,8},{10,11... | collective-permute-start | bytes 294920 | tf_op jit(solution)/shard_map/ppermute | solution.py:306
  89.4 8.2 %collective-permute-start.19 = (bf16[12,8,512]{2,1,0:T(8,128)(2,1)S(1)}, bf16[12,8,512]{2,1,0:T(8,128)(2,1)S(1)}, u32[]{:S(2)}, u32[]{:S(2)}) collective-permute-start(bf16[12,8,512]{2,1,0:T(8,128)(2,1)S(1)} %get-tuple-element.35), channel_id=1, source_target_pairs={{0,1},{1,0},{2,3},{3,2},{4,5},{5,4},{6,7},{7,6},{8,9},{9,8},{10,11... | collective-permute-start | bytes 294920 | tf_op jit(solution)/shard_map/ppermute | solution.py:306
  97.7 4.7 %collective-permute-start.20 = (bf16[8,8,512]{2,1,0:T(8,128)(2,1)S(1)}, bf16[8,8,512]{2,1,0:T(8,128)(2,1)S(1)}, u32[]{:S(2)}, u32[]{:S(2)}) collective-permute-start(bf16[8,8,512]{2,1,0:T(8,128)(2,1)S(1)} %slice.88), channel_id=1, source_target_pairs={{0,2},{1,3},{2,0},{3,1},{4,6},{5,7},{6,4},{7,5},{8,10},{9,11},{10,... | collective-permute-start | bytes 196616 | tf_op jit(solution)/shard_map/ppermute | solution.py:306
  102.4 5.6 %collective-permute-start.21 = (bf16[2,8,512]{2,1,0:T(8,128)(2,1)S(1)}, bf16[2,8,512]{2,1,0:T(8,128)(2,1)S(1)}, u32[]{:S(2)}, u32[]{:S(2)}) collective-permute-start(bf16[2,8,512]{2,1,0:T(8,128)(2,1)S(1)} %get-tuple-element.50), channel_id=1, source_target_pairs={{0,4},{1,5},{2,6},{3,7},{4,0},{5,1},{6,2},{7,3},{8,12},{9,13},{10,... | collective-permute-start | bytes 49160 | tf_op jit(solution)/shard_map/ppermute | solution.py:306
  103.8 4.2 %collective-permute-start.23 = (bf16[2,8,512]{2,1,0:T(8,128)(2,1)S(1)}, bf16[2,8,512]{2,1,0:T(8,128)(2,1)S(1)}, u32[]{:S(2)}, u32[]{:S(2)}) collective-permute-start(bf16[2,8,512]{2,1,0:T(8,128)(2,1)S(1)} %get-tuple-element.51), channel_id=1, source_target_pairs={{0,12},{1,13},{2,14},{3,15},{4,8},{5,9},{6,10},{7,11},{8,4},{9,5},... | collective-permute-start | bytes 49160 | tf_op jit(solution)/shard_map/ppermute | solution.py:306
  104.7 4.2 %collective-permute-start.22 = (bf16[2,8,512]{2,1,0:T(8,128)(2,1)S(1)}, bf16[2,8,512]{2,1,0:T(8,128)(2,1)S(1)}, u32[]{:S(2)}, u32[]{:S(2)}) collective-permute-start(bf16[2,8,512]{2,1,0:T(8,128)(2,1)S(1)} %get-tuple-element.52), channel_id=1, source_target_pairs={{0,8},{1,9},{2,10},{3,11},{4,12},{5,13},{6,14},{7,15},{8,0},{9,1},... | collective-permute-start | bytes 49160 | tf_op jit(solution)/shard_map/ppermute | solution.py:306
  123.8 4.1 %collective-permute-start.25 = (f32[8,512]{1,0:T(8,128)S(1)}, f32[8,512]{1,0:T(8,128)S(1)}, u32[]{:S(2)}, u32[]{:S(2)}) collective-permute-start(f32[8,512]{1,0:T(8,128)S(1)} %get-tuple-element.57), channel_id=1, source_target_pairs={{0,8},{1,9},{2,10},{3,11},{4,12},{5,13},{6,14},{7,15},{8,0},{9,1},... | collective-permute-start | bytes 49160 | tf_op jit(solution)/shard_map/ppermute | solution.py:306
  127.9 6.7 %collective-permute-start.27 = (f32[4,8,512]{2,1,0:T(8,128)S(1)}, f32[4,8,512]{2,1,0:T(8,128)S(1)}, u32[]{:S(2)}, u32[]{:S(2)}) collective-permute-start(f32[4,8,512]{2,1,0:T(8,128)S(1)} %pad_maximum_fusion.2.near_ref), channel_id=1, source_target_pairs={{0,1},{1,0},{2,3},{3,2},{4,5},{5,4},{6,7},{7,6},{8,9},{9,8},{10,11... | collective-permute-start | bytes 196616 | tf_op jit(solution)/shard_map/ppermute | solution.py:306
  (15 other events, 153.3 us)

commit v8 on v7

--- a/solution.py
+++ b/solution.py
@@ -40,12 +40,12 @@
     return col // X_ONE * 2 + col % 2
 
 
-def slope_kernel(scales, stepped, kind_hbm, data_ref, two_ref, near_ref, near_y_ref, far_ref, far_y_ref, *refs):
+def slope_kernel(scales, stepped, kind_ref, data_ref, two_ref, near_ref, near_y_ref, far_ref, far_y_ref, *refs):
     if stepped:
         near_three_ref, far_three_ref, *refs = refs
     else:
-        three_hbm, *refs = refs
-    sent_ref, kept_ref, slope_ref, one_ref, three_ref, ga_acc, gc_acc, kind_ref, kind_sem, three_sem = refs
+        three_in_ref, *refs = refs
+    sent_ref, kept_ref, slope_ref, one_ref, three_ref, ga_acc, gc_acc = refs
     step = pl.program_id(0)
     n_slab, own, rank = one_ref.shape
     depth = three_ref.shape[0] * three_ref.shape[1]
@@ -54,11 +54,6 @@
 
     @pl.when(step == 0)
     def _():
-        kind_copy = pltpu.make_async_copy(kind_hbm.at[0, pl.ds(0, 8)], kind_ref, kind_sem)
-        kind_copy.start()
-        if not stepped:
-            three_copy = pltpu.make_async_copy(three_hbm, gc_acc, three_sem)
-            three_copy.start()
         for m in range(4):
             col = here ^ (m * X_ONE)
             one_ref[col] = near_ref[m]
@@ -68,10 +63,8 @@
             if stepped:
                 three_ref[third_slab(col)] = near_three_ref[m]
                 three_ref[third_slab(col ^ CORE)] = far_three_ref[m]
-        kind_copy.wait()
         if not stepped:
-            three_copy.wait()
-            three_ref[...] = gc_acc[...].astype(bf16)
+            three_ref[...] = three_in_ref[...].astype(bf16)
         gc_acc[...] = jnp.zeros_like(gc_acc)
 
     def run(logistic):
@@ -120,8 +113,8 @@
         ga_acc[pl.ds(step * slabs, slabs)] = jnp.concatenate(grad_one).reshape(slabs, own, rank)
         gc_acc[...] += grad_three.reshape(gc_acc.shape)
 
-    pl.when(kind_ref[0, 0] == 1)(lambda: run(True))
-    pl.when(kind_ref[0, 0] != 1)(lambda: run(False))
+    pl.when(kind_ref[0] == 1)(lambda: run(True))
+    pl.when(kind_ref[0] != 1)(lambda: run(False))
 
     @pl.when(step == pl.num_programs(0) - 1)
     def _():
@@ -133,7 +126,7 @@
                 out_ref[8 + m] = (ga_acc[col ^ Y_HI] * scales[0]).astype(bf16)
 
 
-def slopes(loss_kind, tensor, twos, ones, threes, scales):
+def slopes(kind, tensor, twos, ones, threes, scales):
     rows, depth, cols = tensor.shape
     own, rank = ones[0].shape[1:]
     slabs = rows // own
@@ -145,10 +138,9 @@
         functools.partial(slope_kernel, scales, stepped),
         grid=(rows // BLOCK,),
         in_specs=[
-            pl.BlockSpec(memory_space=pltpu.HBM),
+            pl.BlockSpec(memory_space=pltpu.SMEM),
             pl.BlockSpec((BLOCK, depth, cols), lambda i: (i, 0, 0)),
-            *[whole(x.shape) for x in (twos, *ones)],
-            *([whole(x.shape) for x in threes] if stepped else [pl.BlockSpec(memory_space=pltpu.HBM)]),
+            *[whole(x.shape) for x in (twos, *ones, *threes)],
         ],
         out_specs=[
             whole(swapped),
@@ -167,15 +159,12 @@
         scratch_shapes=[
             pltpu.VMEM((slabs, own, rank), f32),
             pltpu.VMEM(all_threes, f32),
-            pltpu.SMEM((8, cols), jnp.int32),
-            pltpu.SemaphoreType.DMA,
-            pltpu.SemaphoreType.DMA,
         ],
         compiler_params=pltpu.CompilerParams(vmem_limit_bytes=VMEM_LATER if stepped else VMEM_LIMIT),
         cost_estimate=pl.CostEstimate(
             flops=8 * rows * depth * cols * rank, bytes_accessed=4 << 20, transcendentals=rows * depth * cols
         ),
-    )(loss_kind, tensor, twos, *ones, *threes)
+    )(kind, tensor, twos, *ones, *threes)
 
 
 def second_kernel(scale, slope_ref, one_ref, three_ref, out_ref, acc):
@@ -263,30 +252,34 @@
 
 def update_kernel(counter, got_ref, *refs):
     two_in, three_in, two_out, three_out = refs[:3], refs[3:6], refs[6:9], refs[9:12]
-    twos_ref, half_ref = refs[12:]
+    start_ref, twos_ref, half_ref = refs[12:]
     own = two_in[0].shape[0]
+    slab = third_slab(lax.axis_index("col"))
     got = jnp.sum(got_ref[...].astype(f32), axis=0)
-    for grad, old, new in ((got[:own], two_in, two_out), (got[own:], three_in, three_out)):
-        for ref, value in zip(new, adam_step(*[x[...] for x in old], grad, counter)):
-            ref[...] = value
-    two = two_out[0][...].astype(bf16)
-    for slab in range(twos_ref.shape[0]):
-        twos_ref[slab] = two
-    half_ref[...] = three_out[0][...].astype(bf16)
+    two = adam_step(*[x[...] for x in two_in], got[:own], counter)
+    three = adam_step(*[x[slab] for x in three_in], got[own:], counter)
+    for ref, value in zip((*two_out, *three_out), (*two, *three)):
+        ref[...] = value
+    start_ref[...] = three_in[0][slab]
+    half = two[0].astype(bf16)
+    for place in range(twos_ref.shape[0]):
+        twos_ref[place] = half
+    half_ref[...] = three[0].astype(bf16)
 
 
 def update(got, two, three, counter):
-    shapes = [jax.ShapeDtypeStruct(x.shape, f32) for x in (*two, *three)]
+    rows = jax.ShapeDtypeStruct(two[0].shape, f32)
+    third = jax.ShapeDtypeStruct(three[0].shape[1:], f32)
     twos = jax.ShapeDtypeStruct((got.shape[0],) + two[0].shape, bf16)
     vmem = pl.BlockSpec(memory_space=pltpu.VMEM)
     out = pl.pallas_call(
         functools.partial(update_kernel, counter),
         in_specs=[vmem] * 7,
-        out_specs=[vmem] * 8,
-        out_shape=[*shapes, twos, jax.ShapeDtypeStruct(three[0].shape, bf16)],
+        out_specs=[vmem] * 9,
+        out_shape=[rows] * 3 + [third] * 4 + [twos, jax.ShapeDtypeStruct(third.shape, bf16)],
         compiler_params=pltpu.CompilerParams(vmem_limit_bytes=8 << 20),
     )(got, *two, *three)
-    return out[:3], out[3:6], out[6], out[7]
+    return out[:3], out[3:6], out[6], out[7], out[8]
 
 
 def swap_all(parts, axis):
@@ -357,19 +350,18 @@
         1.0 / math.sqrt(full_rows * tile_depth),
         1.0 / math.sqrt(full_rows * full_cols),
     )
-    here = lax.axis_index("col")
-    mine = lambda x: lax.dynamic_slice_in_dim(x, third_slab(here) * deep, deep, 0)
-    part_three, first_three, second_three = mine(factor_three), mine(first_three), mine(second_three)
-    start_one, start_two, start_three = (factor_one, factor_two, part_three)
+    start_one, start_two = factor_one, factor_two
+    slabs = lambda x: x.reshape(tile_depth // deep, deep, rank)
     twos = swap_all(copies(factor_two, n_row), "row")
     near = gather_x(factor_one.astype(bf16))
     near_y = swap(near, Y_HI)
     ones = (near, near_y, swap(near, CORE), swap(near_y, CORE))
-    threes = (factor_three.reshape(tile_depth // deep, deep, rank),)
+    threes = (slabs(factor_three),)
+    kind = loss_kind[0, 0, :1]
     for iteration in range(ITERS):
         last = iteration == ITERS - 1
         counter = STEP + iteration + 1
-        sent, kept, slope, all_ones, all_threes = slopes(loss_kind, tensor, twos, ones, threes, scales)
+        sent, kept, slope, all_ones, all_threes = slopes(kind, tensor, twos, ones, threes, scales)
         grad_two = second_grad(slope, all_ones, all_threes, scales[1]).reshape(n_row, own_two, rank)
         grad_one, grad_three = reduce_col(plus(kept, swap(sent, CORE)))
         sent = jnp.concatenate([grad_two, to_all(grad_three.astype(bf16), n_row)], axis=1)
@@ -390,8 +382,9 @@
             near = gather_x(factor_one.astype(bf16))
             got, near = lax.optimization_barrier((got, near))
             near_y = swap(near, Y_HI)
-            two, three, sent, half_three = update(
-                got, (factor_two, first_two, second_two), (part_three, first_three, second_three), counter
+            third = [slabs(x) for x in (factor_three, first_three, second_three)]
+            two, three, start_three, sent, half_three = update(
+                got, (factor_two, first_two, second_two), third, counter
             )
             factor_two, first_two, second_two = two
             part_three, first_three, second_three = three

time: 136 us -> 135 us (level)
  waiting for transfers between devices: 19.4 us -> 21.2 us
  starting transfers between devices: 75.9 us -> 74.5 us
    ppermute x28, starting transfers between devices: 57.4 us -> 55.2 us  [swap(): return lax.ppermute(part, 'col', [(i, i ^ code) for i in range(size)])]
    dynamic_slice x2 -> x0, local copies, waits for them, and re-layouts: 1.46 us -> none  [shards(): lax.dynamic_slice_in_dim(x, third_slab(here) * deep, deep, 0)]
    all_to_all x3, waiting for transfers between devices: 5.32 us -> 6.73 us  [swap_all(): return lax.all_to_all(parts, axis, 0, 0)]
  transfers between devices with their start and end apart: 31 -> 31, of which waited for: 13 -> 14; matrix products, arithmetic and copies ran while one was open for 3% -> 2% of each run, Pallas kernels for 4% -> 4%
where the time goes in v8:
time: 135 us; the launch traced here: 134 us
  starting transfers between devices  74.5 us (55%)
  waiting for transfers between devices  21.2 us (16%)
  Pallas kernels  19.7 us (15%)
  blocking collectives  12.2 us (9%)
  other arithmetic  3.05 us (2%)
  local copies, waits for them, and re-layouts  2.23 us (2%)
    ppermute x28, starting transfers between devices, swap(): return lax.ppermute(part, 'col', [(i, i ^ code) for i in range(size)])  55.2 us
    all_to_all x3, starting transfers between devices, swap_all(): return lax.all_to_all(parts, axis, 0, 0)  19.2 us
    ppermute x28, waiting for transfers between devices, swap(): return lax.ppermute(part, 'col', [(i, i ^ code) for i in range(size)])  14.5 us
    pallas_call x2, Pallas kernels, slopes(): pl.pallas_call(functools.partial(slope_kernel, scales, stepped), grid=(ro...  12.8 us
    all_to_all x1, blocking collectives, swap_all(): return lax.all_to_all(parts, axis, 0, 0)  12.2 us
    all_to_all x3, waiting for transfers between devices, swap_all(): return lax.all_to_all(parts, axis, 0, 0)  6.73 us
    pallas_call x2, Pallas kernels, second_grad(): pl.pallas_call(functools.partial(second_kernel, scale), grid=(rows // blo...  4.08 us
  transfers between devices with their start and end apart: 31, of which 14 were waited for; matrix products, arithmetic and copies ran while one was open for 2% of the time, Pallas kernels for 4%

profile of v8, /device:TPU:1, one launch (start us, length us, event | category | flops | bytes accessed | tf_op | source)
XLA Modules:
  0.0 133.9 jit_solution(15111453605350675869)
XLA Ops:
  1.4 3.6 %collective-permute-start.1 = (bf16[8,512]{1,0:T(8,128)(2,1)S(1)}, bf16[8,512]{1,0:T(8,128)(2,1)S(1)}, u32[]{:S(2)}, u32[]{:S(2)}) collective-permute-start(bf16[8,512]{1,0:T(8,128)(2,1)S(1)} %convert_element_type.61), channel_id=1, source_target_pairs={{0,8},{1,9},{2,10},{3,11},{4,12},{5,13},{6,14},{7,15},{8,0},{9,1},... | collective-permute-start | bytes 24584 | tf_op jit(solution)/shard_map/ppermute | solution.py:299
  7.2 9.3 %all-to-all-start = ((bf16[16,8,512]{2,1,0:T(8,128)(2,1)}), bf16[16,8,512]{2,1,0:T(8,128)(2,1)S(1)}, u32[]{:S(2)}, u32[]{:S(2)}) async-start(bf16[16,8,512]{2,1,0:T(8,128)(2,1)} %shard_map.130), calls=%async_computation | async-start | bytes 262144 | tf_op jit(solution)/shard_map/all_to_all | solution.py:286
  17.2 2.7 %collective-permute-start.3 = (bf16[4,8,512]{2,1,0:T(8,128)(2,1)S(1)}, bf16[4,8,512]{2,1,0:T(8,128)(2,1)S(1)}, u32[]{:S(2)}, u32[]{:S(2)}) collective-permute-start(bf16[4,8,512]{2,1,0:T(8,128)(2,1)S(1)} %pad_maximum_fusion.3.near_ref), channel_id=1, source_target_pairs={{0,2},{1,3},{2,0},{3,1},{4,6},{5,7},{6,4},{7,5},{8,10},{9,11},{10,... | collective-permute-start | bytes 98312 | tf_op jit(solution)/shard_map/ppermute | solution.py:299
  19.9 1.8 %collective-permute-start.4 = (bf16[4,8,512]{2,1,0:T(8,128)(2,1)S(1)}, bf16[4,8,512]{2,1,0:T(8,128)(2,1)S(1)}, u32[]{:S(2)}, u32[]{:S(2)}) collective-permute-start(bf16[4,8,512]{2,1,0:T(8,128)(2,1)S(1)} %pad_maximum_fusion.3.near_ref), channel_id=1, source_target_pairs={{0,1},{1,0},{2,3},{3,2},{4,5},{5,4},{6,7},{7,6},{8,9},{9,8},{10,11... | collective-permute-start | bytes 98312 | tf_op jit(solution)/shard_map/ppermute | solution.py:299
  21.7 2.5 %collective-permute-start.5 = (bf16[4,8,512]{2,1,0:T(8,128)(2,1)S(1)}, bf16[4,8,512]{2,1,0:T(8,128)(2,1)S(1)}, u32[]{:S(2)}, u32[]{:S(2)}) collective-permute-start(bf16[4,8,512]{2,1,0:T(8,128)(2,1)S(1)} %collective-permute-done.3.near_y_ref), channel_id=1, source_target_pairs={{0,1},{1,0},{2,3},{3,2},{4,5},{5,4},{6,7},{7,6},{8,9},{9,8},{10,11... | collective-permute-start | bytes 98312 | tf_op jit(solution)/shard_map/ppermute | solution.py:299
  26.4 7.0 %shard_map.131 = (bf16[12,8,512]{2,1,0:T(8,128)(2,1)S(1)}, bf16[12,8,512]{2,1,0:T(8,128)(2,1)S(1)}, bf16[128,64,128]{2,1,0:T(8,128)(2,1)S(1)}, bf16[16,8,512]{2,1,0:T(8,128)(2,1)S(1)}, bf16[8,8,512]{2,1,0:T(8,128)(2,1)S(1)}) custom-call(s32[1]{0:T(128)} %bitcast.kind_ref, bf16[128,64,128]{2,1,0:T(8,128)(2,1)} %data_ref.3, ...), custom_call_target="tpu_custom_call" | custom-call | flops 4294967296 | bytes 4194304 | tf_op jit(solution)/shard_map/pallas_call | solution.py:137
  33.4 2.3 %collective-permute-start.6 = (bf16[12,8,512]{2,1,0:T(8,128)(2,1)S(1)}, bf16[12,8,512]{2,1,0:T(8,128)(2,1)S(1)}, u32[]{:S(2)}, u32[]{:S(2)}) collective-permute-start(bf16[12,8,512]{2,1,0:T(8,128)(2,1)S(1)} %get-tuple-element.27), channel_id=1, source_target_pairs={{0,1},{1,0},{2,3},{3,2},{4,5},{5,4},{6,7},{7,6},{8,9},{9,8},{10,11... | collective-permute-start | bytes 294920 | tf_op jit(solution)/shard_map/ppermute | solution.py:299
  36.6 2.7 %collective-permute-start.7 = (bf16[8,8,512]{2,1,0:T(8,128)(2,1)S(1)}, bf16[8,8,512]{2,1,0:T(8,128)(2,1)S(1)}, u32[]{:S(2)}, u32[]{:S(2)}) collective-permute-start(bf16[8,8,512]{2,1,0:T(8,128)(2,1)S(1)} %slice.82), channel_id=1, source_target_pairs={{0,2},{1,3},{2,0},{3,1},{4,6},{5,7},{6,4},{7,5},{8,10},{9,11},{10,... | collective-permute-start | bytes 196616 | tf_op jit(solution)/shard_map/ppermute | solution.py:299
  39.3 2.0 %collective-permute-done.7.got_ref = bf16[8,8,512]{2,1,0:T(8,128)(2,1)S(1)} collective-permute-done((bf16[8,8,512]{2,1,0:T(8,128)(2,1)S(1)}, bf16[8,8,512]{2,1,0:T(8,128)(2,1)S(1)}, u32[]{:S(2)}, u32[]{:S(2)}) %collective-permute-start.7) | collective-permute-done | bytes 65568 | tf_op jit(solution)/shard_map/ppermute | solution.py:299
  42.6 1.8 %collective-permute-start.10 = (bf16[2,8,512]{2,1,0:T(8,128)(2,1)S(1)}, bf16[2,8,512]{2,1,0:T(8,128)(2,1)S(1)}, u32[]{:S(2)}, u32[]{:S(2)}) collective-permute-start(bf16[2,8,512]{2,1,0:T(8,128)(2,1)S(1)} %get-tuple-element.56), channel_id=1, source_target_pairs={{0,12},{1,13},{2,14},{3,15},{4,8},{5,9},{6,10},{7,11},{8,4},{9,5},... | collective-permute-start | bytes 49160 | tf_op jit(solution)/shard_map/ppermute | solution.py:299
  45.2 2.0 %shard_map.133 = bf16[128,512]{1,0:T(8,128)(2,1)S(1)} custom-call(bf16[128,64,128]{2,1,0:T(8,128)(2,1)S(1)} %get-tuple-element.28.slope_ref, bf16[16,8,512]{2,1,0:T(8,128)(2,1)S(1)} %get-tuple-element.29.one_ref, bf16[8,8,512]{2,1,0:T(8,128)(2,1)S(1)} %get-tuple-element.30.three_ref), custom_call_target="tpu_custom_call" | custom-call | flops 2147483648 | bytes 2097152 | tf_op jit(solution)/shard_map/pallas_call | solution.py:198
  49.3 6.4 %all-to-all-start.1 = ((bf16[16,16,512]{2,1,0:T(8,128)(2,1)}), bf16[16,16,512]{2,1,0:T(8,128)(2,1)S(1)}, u32[]{:S(2)}, u32[]{:S(2)}) async-start(bf16[16,16,512]{2,1,0:T(8,128)(2,1)} %pad_maximum_fusion), calls=%async_computation.1 | async-start | bytes 524288 | tf_op jit(solution)/shard_map/all_to_all | solution.py:286
  60.8 4.6 %all-to-all-done.1.got_ref = bf16[16,16,512]{2,1,0:T(8,128)(2,1)S(1)} async-done(((bf16[16,16,512]{2,1,0:T(8,128)(2,1)}), bf16[16,16,512]{2,1,0:T(8,128)(2,1)S(1)}, u32[]{:S(2)}, u32[]{:S(2)}) %all-to-all-start.1) | async-done | bytes 262176 | tf_op jit(solution)/shard_map/all_to_all | solution.py:286
  69.3 2.6 %collective-permute-start.14 = (bf16[4,8,512]{2,1,0:T(8,128)(2,1)S(1)}, bf16[4,8,512]{2,1,0:T(8,128)(2,1)S(1)}, u32[]{:S(2)}, u32[]{:S(2)}) collective-permute-start(bf16[4,8,512]{2,1,0:T(8,128)(2,1)S(1)} %pad_maximum_fusion.4.near_ref), channel_id=1, source_target_pairs={{0,2},{1,3},{2,0},{3,1},{4,6},{5,7},{6,4},{7,5},{8,10},{9,11},{10,... | collective-permute-start | bytes 98312 | tf_op jit(solution)/shard_map/ppermute | solution.py:299
  72.0 3.5 %all-to-all-start.2 = ((bf16[16,8,512]{2,1,0:T(8,128)(2,1)}), bf16[16,8,512]{2,1,0:T(8,128)(2,1)S(1)}, u32[]{:S(2)}, u32[]{:S(2)}) async-start(bf16[16,8,512]{2,1,0:T(8,128)(2,1)} %get-tuple-element.32), calls=%async_computation.2 | async-start | bytes 262144 | tf_op jit(solution)/shard_map/all_to_all | solution.py:286
  75.6 5.3 %collective-permute-start.18 = (bf16[12,8,512]{2,1,0:T(8,128)(2,1)S(1)}, bf16[12,8,512]{2,1,0:T(8,128)(2,1)S(1)}, u32[]{:S(2)}, u32[]{:S(2)}) collective-permute-start(bf16[12,8,512]{2,1,0:T(8,128)(2,1)S(1)} %constant_dynamic-update-slice_fusion), channel_id=1, source_target_pairs={{0,1},{1,0},{2,3},{3,2},{4,5},{5,4},{6,7},{7,6},{8,9},{9,8},{10,11... | collective-permute-start | bytes 294920 | tf_op jit(solution)/shard_map/ppermute | solution.py:299
  81.8 2.1 %all-to-all-done.2.two_ref = bf16[16,8,512]{2,1,0:T(8,128)(2,1)S(1)} async-done(((bf16[16,8,512]{2,1,0:T(8,128)(2,1)}), bf16[16,8,512]{2,1,0:T(8,128)(2,1)S(1)}, u32[]{:S(2)}, u32[]{:S(2)}) %all-to-all-start.2) | async-done | bytes 131104 | tf_op jit(solution)/shard_map/all_to_all | solution.py:286
  84.0 5.8 %shard_map.135 = (bf16[12,8,512]{2,1,0:T(8,128)(2,1)S(1)}, bf16[12,8,512]{2,1,0:T(8,128)(2,1)S(1)}, bf16[128,64,128]{2,1,0:T(8,128)(2,1)S(1)}, bf16[16,8,512]{2,1,0:T(8,128)(2,1)S(1)}, bf16[8,8,512]{2,1,0:T(8,128)(2,1)S(1)}) custom-call(s32[1]{0:T(128)} %bitcast.kind_ref, bf16[128,64,128]{2,1,0:T(8,128)(2,1)S(1)} %copy-done.7, ...), custom_call_target="tpu_custom_call" | custom-call | flops 4294967296 | bytes 4194304 | tf_op jit(solution)/shard_map/pallas_call | solution.py:137
  89.8 6.5 %collective-permute-start.19 = (bf16[12,8,512]{2,1,0:T(8,128)(2,1)S(1)}, bf16[12,8,512]{2,1,0:T(8,128)(2,1)S(1)}, u32[]{:S(2)}, u32[]{:S(2)}) collective-permute-start(bf16[12,8,512]{2,1,0:T(8,128)(2,1)S(1)} %get-tuple-element.36), channel_id=1, source_target_pairs={{0,1},{1,0},{2,3},{3,2},{4,5},{5,4},{6,7},{7,6},{8,9},{9,8},{10,11... | collective-permute-start | bytes 294920 | tf_op jit(solution)/shard_map/ppermute | solution.py:299
  98.7 3.4 %collective-permute-done.20.got_ref = bf16[8,8,512]{2,1,0:T(8,128)(2,1)S(1)} collective-permute-done((bf16[8,8,512]{2,1,0:T(8,128)(2,1)S(1)}, bf16[8,8,512]{2,1,0:T(8,128)(2,1)S(1)}, u32[]{:S(2)}, u32[]{:S(2)}) %collective-permute-start.20) | collective-permute-done | bytes 65568 | tf_op jit(solution)/shard_map/ppermute | solution.py:299
  105.6 2.0 %shard_map.137 = bf16[128,512]{1,0:T(8,128)(2,1)S(1)} custom-call(bf16[128,64,128]{2,1,0:T(8,128)(2,1)S(1)} %get-tuple-element.42.slope_ref, bf16[16,8,512]{2,1,0:T(8,128)(2,1)S(1)} %get-tuple-element.43.one_ref, bf16[8,8,512]{2,1,0:T(8,128)(2,1)S(1)} %get-tuple-element.44.three_ref), custom_call_target="tpu_custom_call" | custom-call | flops 2147483648 | bytes 2097152 | tf_op jit(solution)/shard_map/pallas_call | solution.py:198
  108.4 12.2 %all_to_all.20 = bf16[16,16,512]{2,1,0:T(8,128)(2,1)S(1)} all-to-all(bf16[16,16,512]{2,1,0:T(8,128)(2,1)S(1)} %pad_maximum_fusion.1), channel_id=1, replica_groups=mesh['row'=16,'col'=16] {'row'}, dimensions={0} | all-to-all | bytes 524288 | tf_op jit(solution)/shard_map/all_to_all | solution.py:286
  124.7 1.8 %collective-permute-done.25 = f32[8,512]{1,0:T(8,128)S(1)} collective-permute-done((f32[8,512]{1,0:T(8,128)S(1)}, f32[8,512]{1,0:T(8,128)S(1)}, u32[]{:S(2)}, u32[]{:S(2)}) %collective-permute-start.25) | collective-permute-done | bytes 16416 | tf_op jit(solution)/shard_map/ppermute | solution.py:299
  126.5 5.8 %collective-permute-start.27 = (f32[4,8,512]{2,1,0:T(8,128)S(1)}, f32[4,8,512]{2,1,0:T(8,128)S(1)}, u32[]{:S(2)}, u32[]{:S(2)}) collective-permute-start(f32[4,8,512]{2,1,0:T(8,128)S(1)} %pad_maximum_fusion.2.near_ref), channel_id=1, source_target_pairs={{0,1},{1,0},{2,3},{3,2},{4,5},{5,4},{6,7},{7,6},{8,9},{9,8},{10,11... | collective-permute-start | bytes 196616 | tf_op jit(solution)/shard_map/ppermute | solution.py:299
  (102 shorter events, 33.0 us)
Async XLA Ops:
  1.4 15.9 %collective-permute-start.1 = (bf16[8,512]{1,0:T(8,128)(2,1)S(1)}, bf16[8,512]{1,0:T(8,128)(2,1)S(1)}, u32[]{:S(2)}, u32[]{:S(2)}) collective-permute-start(bf16[8,512]{1,0:T(8,128)(2,1)S(1)} %convert_element_type.61), channel_id=1, source_target_pairs={{0,8},{1,9},{2,10},{3,11},{4,12},{5,13},{6,14},{7,15},{8,0},{9,1},... | collective-permute-start | bytes 24584 | tf_op jit(solution)/shard_map/ppermute | solution.py:299
  4.9 12.3 %collective-permute-start = (bf16[8,512]{1,0:T(8,128)(2,1)S(1)}, bf16[8,512]{1,0:T(8,128)(2,1)S(1)}, u32[]{:S(2)}, u32[]{:S(2)}) collective-permute-start(bf16[8,512]{1,0:T(8,128)(2,1)S(1)} %convert_element_type.61), channel_id=1, source_target_pairs={{0,4},{1,5},{2,6},{3,7},{4,0},{5,1},{6,2},{7,3},{8,12},{9,13},{10,... | collective-permute-start | bytes 24584 | tf_op jit(solution)/shard_map/ppermute | solution.py:299
  5.2 12.0 %collective-permute-start.2 = (bf16[8,512]{1,0:T(8,128)(2,1)S(1)}, bf16[8,512]{1,0:T(8,128)(2,1)S(1)}, u32[]{:S(2)}, u32[]{:S(2)}) collective-permute-start(bf16[8,512]{1,0:T(8,128)(2,1)S(1)} %convert_element_type.61), channel_id=1, source_target_pairs={{0,12},{1,13},{2,14},{3,15},{4,8},{5,9},{6,10},{7,11},{8,4},{9,5},... | collective-permute-start | bytes 24584 | tf_op jit(solution)/shard_map/ppermute | solution.py:299
  7.2 18.3 %all-to-all-start = ((bf16[16,8,512]{2,1,0:T(8,128)(2,1)}), bf16[16,8,512]{2,1,0:T(8,128)(2,1)S(1)}, u32[]{:S(2)}, u32[]{:S(2)}) async-start(bf16[16,8,512]{2,1,0:T(8,128)(2,1)} %shard_map.130), calls=%async_computation | async-start | bytes 262144 | tf_op jit(solution)/shard_map/all_to_all | solution.py:286
  17.2 4.5 %collective-permute-start.3 = (bf16[4,8,512]{2,1,0:T(8,128)(2,1)S(1)}, bf16[4,8,512]{2,1,0:T(8,128)(2,1)S(1)}, u32[]{:S(2)}, u32[]{:S(2)}) collective-permute-start(bf16[4,8,512]{2,1,0:T(8,128)(2,1)S(1)} %pad_maximum_fusion.3.near_ref), channel_id=1, source_target_pairs={{0,2},{1,3},{2,0},{3,1},{4,6},{5,7},{6,4},{7,5},{8,10},{9,11},{10,... | collective-permute-start | bytes 98312 | tf_op jit(solution)/shard_map/ppermute | solution.py:299
  19.9 5.5 %collective-permute-start.4 = (bf16[4,8,512]{2,1,0:T(8,128)(2,1)S(1)}, bf16[4,8,512]{2,1,0:T(8,128)(2,1)S(1)}, u32[]{:S(2)}, u32[]{:S(2)}) collective-permute-start(bf16[4,8,512]{2,1,0:T(8,128)(2,1)S(1)} %pad_maximum_fusion.3.near_ref), channel_id=1, source_target_pairs={{0,1},{1,0},{2,3},{3,2},{4,5},{5,4},{6,7},{7,6},{8,9},{9,8},{10,11... | collective-permute-start | bytes 98312 | tf_op jit(solution)/shard_map/ppermute | solution.py:299
  36.6 4.7 %collective-permute-start.7 = (bf16[8,8,512]{2,1,0:T(8,128)(2,1)S(1)}, bf16[8,8,512]{2,1,0:T(8,128)(2,1)S(1)}, u32[]{:S(2)}, u32[]{:S(2)}) collective-permute-start(bf16[8,8,512]{2,1,0:T(8,128)(2,1)S(1)} %slice.82), channel_id=1, source_target_pairs={{0,2},{1,3},{2,0},{3,1},{4,6},{5,7},{6,4},{7,5},{8,10},{9,11},{10,... | collective-permute-start | bytes 196616 | tf_op jit(solution)/shard_map/ppermute | solution.py:299
  41.4 5.9 %collective-permute-start.8 = (bf16[2,8,512]{2,1,0:T(8,128)(2,1)S(1)}, bf16[2,8,512]{2,1,0:T(8,128)(2,1)S(1)}, u32[]{:S(2)}, u32[]{:S(2)}) collective-permute-start(bf16[2,8,512]{2,1,0:T(8,128)(2,1)S(1)} %get-tuple-element.55), channel_id=1, source_target_pairs={{0,4},{1,5},{2,6},{3,7},{4,0},{5,1},{6,2},{7,3},{8,12},{9,13},{10,... | collective-permute-start | bytes 49160 | tf_op jit(solution)/shard_map/ppermute | solution.py:299
  42.6 4.6 %collective-permute-start.10 = (bf16[2,8,512]{2,1,0:T(8,128)(2,1)S(1)}, bf16[2,8,512]{2,1,0:T(8,128)(2,1)S(1)}, u32[]{:S(2)}, u32[]{:S(2)}) collective-permute-start(bf16[2,8,512]{2,1,0:T(8,128)(2,1)S(1)} %get-tuple-element.56), channel_id=1, source_target_pairs={{0,12},{1,13},{2,14},{3,15},{4,8},{5,9},{6,10},{7,11},{8,4},{9,5},... | collective-permute-start | bytes 49160 | tf_op jit(solution)/shard_map/ppermute | solution.py:299
  44.4 4.1 %collective-permute-start.9 = (bf16[2,8,512]{2,1,0:T(8,128)(2,1)S(1)}, bf16[2,8,512]{2,1,0:T(8,128)(2,1)S(1)}, u32[]{:S(2)}, u32[]{:S(2)}) collective-permute-start(bf16[2,8,512]{2,1,0:T(8,128)(2,1)S(1)} %get-tuple-element.57), channel_id=1, source_target_pairs={{0,8},{1,9},{2,10},{3,11},{4,12},{5,13},{6,14},{7,15},{8,0},{9,1},... | collective-permute-start | bytes 49160 | tf_op jit(solution)/shard_map/ppermute | solution.py:299
  49.3 16.1 %all-to-all-start.1 = ((bf16[16,16,512]{2,1,0:T(8,128)(2,1)}), bf16[16,16,512]{2,1,0:T(8,128)(2,1)S(1)}, u32[]{:S(2)}, u32[]{:S(2)}) async-start(bf16[16,16,512]{2,1,0:T(8,128)(2,1)} %pad_maximum_fusion), calls=%async_computation.1 | async-start | bytes 524288 | tf_op jit(solution)/shard_map/all_to_all | solution.py:286
  66.1 9.5 %collective-permute-start.17 = (bf16[8,512]{1,0:T(8,128)(2,1)S(1)}, bf16[8,512]{1,0:T(8,128)(2,1)S(1)}, u32[]{:S(2)}, u32[]{:S(2)}) collective-permute-start(bf16[8,512]{1,0:T(8,128)(2,1)S(1)} %get-tuple-element.34), channel_id=1, source_target_pairs={{0,12},{1,13},{2,14},{3,15},{4,8},{5,9},{6,10},{7,11},{8,4},{9,5},... | collective-permute-start | bytes 24584 | tf_op jit(solution)/shard_map/ppermute | solution.py:299
  67.0 8.6 %collective-permute-start.16 = (bf16[8,512]{1,0:T(8,128)(2,1)S(1)}, bf16[8,512]{1,0:T(8,128)(2,1)S(1)}, u32[]{:S(2)}, u32[]{:S(2)}) collective-permute-start(bf16[8,512]{1,0:T(8,128)(2,1)S(1)} %get-tuple-element.34), channel_id=1, source_target_pairs={{0,8},{1,9},{2,10},{3,11},{4,12},{5,13},{6,14},{7,15},{8,0},{9,1},... | collective-permute-start | bytes 24584 | tf_op jit(solution)/shard_map/ppermute | solution.py:299
  68.2 7.3 %collective-permute-start.15 = (bf16[8,512]{1,0:T(8,128)(2,1)S(1)}, bf16[8,512]{1,0:T(8,128)(2,1)S(1)}, u32[]{:S(2)}, u32[]{:S(2)}) collective-permute-start(bf16[8,512]{1,0:T(8,128)(2,1)S(1)} %get-tuple-element.34), channel_id=1, source_target_pairs={{0,4},{1,5},{2,6},{3,7},{4,0},{5,1},{6,2},{7,3},{8,12},{9,13},{10,... | collective-permute-start | bytes 24584 | tf_op jit(solution)/shard_map/ppermute | solution.py:299
  69.3 6.1 %collective-permute-start.14 = (bf16[4,8,512]{2,1,0:T(8,128)(2,1)S(1)}, bf16[4,8,512]{2,1,0:T(8,128)(2,1)S(1)}, u32[]{:S(2)}, u32[]{:S(2)}) collective-permute-start(bf16[4,8,512]{2,1,0:T(8,128)(2,1)S(1)} %pad_maximum_fusion.4.near_ref), channel_id=1, source_target_pairs={{0,2},{1,3},{2,0},{3,1},{4,6},{5,7},{6,4},{7,5},{8,10},{9,11},{10,... | collective-permute-start | bytes 98312 | tf_op jit(solution)/shard_map/ppermute | solution.py:299
  72.0 12.0 %all-to-all-start.2 = ((bf16[16,8,512]{2,1,0:T(8,128)(2,1)}), bf16[16,8,512]{2,1,0:T(8,128)(2,1)S(1)}, u32[]{:S(2)}, u32[]{:S(2)}) async-start(bf16[16,8,512]{2,1,0:T(8,128)(2,1)} %get-tuple-element.32), calls=%async_computation.2 | async-start | bytes 262144 | tf_op jit(solution)/shard_map/all_to_all | solution.py:286
  75.6 6.3 %collective-permute-start.18 = (bf16[12,8,512]{2,1,0:T(8,128)(2,1)S(1)}, bf16[12,8,512]{2,1,0:T(8,128)(2,1)S(1)}, u32[]{:S(2)}, u32[]{:S(2)}) collective-permute-start(bf16[12,8,512]{2,1,0:T(8,128)(2,1)S(1)} %constant_dynamic-update-slice_fusion), channel_id=1, source_target_pairs={{0,1},{1,0},{2,3},{3,2},{4,5},{5,4},{6,7},{7,6},{8,9},{9,8},{10,11... | collective-permute-start | bytes 294920 | tf_op jit(solution)/shard_map/ppermute | solution.py:299
  89.8 7.4 %collective-permute-start.19 = (bf16[12,8,512]{2,1,0:T(8,128)(2,1)S(1)}, bf16[12,8,512]{2,1,0:T(8,128)(2,1)S(1)}, u32[]{:S(2)}, u32[]{:S(2)}) collective-permute-start(bf16[12,8,512]{2,1,0:T(8,128)(2,1)S(1)} %get-tuple-element.36), channel_id=1, source_target_pairs={{0,1},{1,0},{2,3},{3,2},{4,5},{5,4},{6,7},{7,6},{8,9},{9,8},{10,11... | collective-permute-start | bytes 294920 | tf_op jit(solution)/shard_map/ppermute | solution.py:299
  97.3 4.7 %collective-permute-start.20 = (bf16[8,8,512]{2,1,0:T(8,128)(2,1)S(1)}, bf16[8,8,512]{2,1,0:T(8,128)(2,1)S(1)}, u32[]{:S(2)}, u32[]{:S(2)}) collective-permute-start(bf16[8,8,512]{2,1,0:T(8,128)(2,1)S(1)} %slice.92), channel_id=1, source_target_pairs={{0,2},{1,3},{2,0},{3,1},{4,6},{5,7},{6,4},{7,5},{8,10},{9,11},{10,... | collective-permute-start | bytes 196616 | tf_op jit(solution)/shard_map/ppermute | solution.py:299
  102.0 5.6 %collective-permute-start.21 = (bf16[2,8,512]{2,1,0:T(8,128)(2,1)S(1)}, bf16[2,8,512]{2,1,0:T(8,128)(2,1)S(1)}, u32[]{:S(2)}, u32[]{:S(2)}) collective-permute-start(bf16[2,8,512]{2,1,0:T(8,128)(2,1)S(1)} %get-tuple-element.52), channel_id=1, source_target_pairs={{0,4},{1,5},{2,6},{3,7},{4,0},{5,1},{6,2},{7,3},{8,12},{9,13},{10,... | collective-permute-start | bytes 49160 | tf_op jit(solution)/shard_map/ppermute | solution.py:299
  103.2 4.5 %collective-permute-start.23 = (bf16[2,8,512]{2,1,0:T(8,128)(2,1)S(1)}, bf16[2,8,512]{2,1,0:T(8,128)(2,1)S(1)}, u32[]{:S(2)}, u32[]{:S(2)}) collective-permute-start(bf16[2,8,512]{2,1,0:T(8,128)(2,1)S(1)} %get-tuple-element.53), channel_id=1, source_target_pairs={{0,12},{1,13},{2,14},{3,15},{4,8},{5,9},{6,10},{7,11},{8,4},{9,5},... | collective-permute-start | bytes 49160 | tf_op jit(solution)/shard_map/ppermute | solution.py:299
  104.0 4.3 %collective-permute-start.22 = (bf16[2,8,512]{2,1,0:T(8,128)(2,1)S(1)}, bf16[2,8,512]{2,1,0:T(8,128)(2,1)S(1)}, u32[]{:S(2)}, u32[]{:S(2)}) collective-permute-start(bf16[2,8,512]{2,1,0:T(8,128)(2,1)S(1)} %get-tuple-element.54), channel_id=1, source_target_pairs={{0,8},{1,9},{2,10},{3,11},{4,12},{5,13},{6,14},{7,15},{8,0},{9,1},... | collective-permute-start | bytes 49160 | tf_op jit(solution)/shard_map/ppermute | solution.py:299
  122.4 4.1 %collective-permute-start.25 = (f32[8,512]{1,0:T(8,128)S(1)}, f32[8,512]{1,0:T(8,128)S(1)}, u32[]{:S(2)}, u32[]{:S(2)}) collective-permute-start(f32[8,512]{1,0:T(8,128)S(1)} %get-tuple-element.59), channel_id=1, source_target_pairs={{0,8},{1,9},{2,10},{3,11},{4,12},{5,13},{6,14},{7,15},{8,0},{9,1},... | collective-permute-start | bytes 49160 | tf_op jit(solution)/shard_map/ppermute | solution.py:299
  126.5 6.7 %collective-permute-start.27 = (f32[4,8,512]{2,1,0:T(8,128)S(1)}, f32[4,8,512]{2,1,0:T(8,128)S(1)}, u32[]{:S(2)}, u32[]{:S(2)}) collective-permute-start(f32[4,8,512]{2,1,0:T(8,128)S(1)} %pad_maximum_fusion.2.near_ref), channel_id=1, source_target_pairs={{0,1},{1,0},{2,3},{3,2},{4,5},{5,4},{6,7},{7,6},{8,9},{9,8},{10,11... | collective-permute-start | bytes 196616 | tf_op jit(solution)/shard_map/ppermute | solution.py:299
  (18 other events, 216.0 us)

commit v9 on v8

--- a/solution.py
+++ b/solution.py
@@ -113,8 +113,8 @@
         ga_acc[pl.ds(step * slabs, slabs)] = jnp.concatenate(grad_one).reshape(slabs, own, rank)
         gc_acc[...] += grad_three.reshape(gc_acc.shape)
 
-    pl.when(kind_ref[0] == 1)(lambda: run(True))
-    pl.when(kind_ref[0] != 1)(lambda: run(False))
+    pl.when(kind_ref[0] % 2 == 1)(lambda: run(True))
+    pl.when(kind_ref[0] % 2 != 1)(lambda: run(False))
 
     @pl.when(step == pl.num_programs(0) - 1)
     def _():
@@ -250,36 +250,39 @@
     )(near, far)
 
 
-def update_kernel(counter, got_ref, *refs):
-    two_in, three_in, two_out, three_out = refs[:3], refs[3:6], refs[6:9], refs[9:12]
-    start_ref, twos_ref, half_ref = refs[12:]
+def update_kernel(counter, grad_ref, got_ref, *refs):
+    one_in, two_in, three_in = refs[:3], refs[3:6], refs[6:9]
+    new_refs = refs[9:18]
+    start_ref, twos_ref, pair_ref = refs[18:]
     own = two_in[0].shape[0]
     slab = third_slab(lax.axis_index("col"))
     got = jnp.sum(got_ref[...].astype(f32), axis=0)
+    one = adam_step(*[x[...] for x in one_in], grad_ref[0], counter)
     two = adam_step(*[x[...] for x in two_in], got[:own], counter)
     three = adam_step(*[x[slab] for x in three_in], got[own:], counter)
-    for ref, value in zip((*two_out, *three_out), (*two, *three)):
+    for ref, value in zip(new_refs, (*one, *two, *three)):
         ref[...] = value
     start_ref[...] = three_in[0][slab]
     half = two[0].astype(bf16)
     for place in range(twos_ref.shape[0]):
         twos_ref[place] = half
-    half_ref[...] = three[0].astype(bf16)
-
-
-def update(got, two, three, counter):
+    pair_ref[0] = one[0].astype(bf16)
+    pair_ref[1] = three[0].astype(bf16)
+
+
+def update(grads, got, one, two, three, counter):
     rows = jax.ShapeDtypeStruct(two[0].shape, f32)
     third = jax.ShapeDtypeStruct(three[0].shape[1:], f32)
     twos = jax.ShapeDtypeStruct((got.shape[0],) + two[0].shape, bf16)
     vmem = pl.BlockSpec(memory_space=pltpu.VMEM)
     out = pl.pallas_call(
         functools.partial(update_kernel, counter),
-        in_specs=[vmem] * 7,
-        out_specs=[vmem] * 9,
-        out_shape=[rows] * 3 + [third] * 4 + [twos, jax.ShapeDtypeStruct(third.shape, bf16)],
+        in_specs=[vmem] * 11,
+        out_specs=[vmem] * 12,
+        out_shape=[rows] * 6 + [third] * 4 + [twos, jax.ShapeDtypeStruct((2,) + third.shape, bf16)],
         compiler_params=pltpu.CompilerParams(vmem_limit_bytes=8 << 20),
-    )(got, *two, *three)
-    return out[:3], out[3:6], out[6], out[7], out[8]
+    )(grads, got, *one, *two, *three)
+    return out[:3], out[3:6], out[6:9], out[9], out[10], out[11]
 
 
 def swap_all(parts, axis):
@@ -332,7 +335,7 @@
     out = pairs[0].astype(f32)
     for part in got:
         out = out + part.astype(f32)
-    return out[0], out[1]
+    return out
 
 
 def shards(
@@ -357,17 +360,19 @@
     near_y = swap(near, Y_HI)
     ones = (near, near_y, swap(near, CORE), swap(near_y, CORE))
     threes = (slabs(factor_three),)
-    kind = loss_kind[0, 0, :1]
+    kind = loss_kind[0, 0, :1] + 2 * lax.axis_index("col")
     for iteration in range(ITERS):
         last = iteration == ITERS - 1
         counter = STEP + iteration + 1
         sent, kept, slope, all_ones, all_threes = slopes(kind, tensor, twos, ones, threes, scales)
         grad_two = second_grad(slope, all_ones, all_threes, scales[1]).reshape(n_row, own_two, rank)
-        grad_one, grad_three = reduce_col(plus(kept, swap(sent, CORE)))
-        sent = jnp.concatenate([grad_two, to_all(grad_three.astype(bf16), n_row)], axis=1)
-        factor_one, first_one, second_one = adam_step(factor_one, first_one, second_one, grad_one, counter)
+        grads = reduce_col(plus(kept, swap(sent, CORE)))
+        sent = jnp.concatenate([grad_two, to_all(grads[1].astype(bf16), n_row)], axis=1)
         got = swap_all(sent, "row")
         if last:
+            factor_one, first_one, second_one = adam_step(
+                factor_one, first_one, second_one, grads[0], counter
+            )
             got = total(got)
             grad_two, grad_three = got[:own_two], got[own_two:]
             part_three, first_three, second_three = adam_step(
@@ -379,20 +384,19 @@
                 factor_two, first_two, second_two, grad_two, counter
             )
         else:
-            near = gather_x(factor_one.astype(bf16))
-            got, near = lax.optimization_barrier((got, near))
-            near_y = swap(near, Y_HI)
             third = [slabs(x) for x in (factor_three, first_three, second_three)]
-            two, three, start_three, sent, half_three = update(
-                got, (factor_two, first_two, second_two), third, counter
+            one, two, three, start_three, sent, pair = update(
+                grads, got, (factor_one, first_one, second_one), (factor_two, first_two, second_two), third, counter
             )
+            factor_one, first_one, second_one = one
             factor_two, first_two, second_two = two
             part_three, first_three, second_three = three
-            near_three = gather_x(half_three)
             twos = swap_all(sent, "row")
-            far = swap(jnp.concatenate([near, near_y, near_three]), CORE)
-            ones = (near, near_y, far[:4], far[4:8])
-            threes = (near_three, far[8:])
+            half = gather_x(pair)
+            near, near_three = half[:, 0], half[:, 1]
+            near_y = swap(near, Y_HI)
+            ones = (near, near_y, swap(near, CORE), swap(near_y, CORE))
+            threes = (near_three, swap(near_three, CORE))
     spread = learn_rate * ITERS
     new_three = place_third(near_three, swap(near_three, CORE)).reshape(tile_depth, rank)
     return ((start_one - factor_one) / spread, (start_two - factor_two) / spread, new_three)

time: 135 us -> 132 us (0.978)
  blocking collectives: 12.2 us -> 31 us
  waiting for transfers between devices: 21.2 us -> 11.1 us
  starting transfers between devices: 74.5 us -> 64.6 us
    all_to_all x1 -> x2, blocking collectives: 12.2 us -> 31 us  [swap_all(): return lax.all_to_all(parts, axis, 0, 0)]
    all_to_all x3 -> x2, waiting for transfers between devices: 6.73 us -> 0.01 us  [swap_all(): return lax.all_to_all(parts, axis, 0, 0)]
    all_to_all x3 -> x2, starting transfers between devices: 19.2 us -> 12.8 us  [swap_all(): return lax.all_to_all(parts, axis, 0, 0)]
    ppermute x28 -> x27, starting transfers between devices: 55.2 us -> 51.8 us  [swap(): return lax.ppermute(part, 'col', [(i, i ^ code) for i in range(size)])]
    ppermute x28 -> x27, waiting for transfers between devices: 14.5 us -> 11.1 us  [swap(): return lax.ppermute(part, 'col', [(i, i ^ code) for i in range(size)])]
  transfers between devices with their start and end apart: 31 -> 29, of which waited for: 14 -> 9; matrix products, arithmetic and copies ran while one was open for 2% -> 2% of each run, Pallas kernels for 4% -> 4%
where the time goes in v9:
time: 132 us; the launch traced here: 131 us
  starting transfers between devices  64.6 us (49%)
  blocking collectives  31 us (23%)
  Pallas kernels  18.5 us (14%)
  waiting for transfers between devices  11.1 us (8%)
  other arithmetic  2.31 us (2%)
  local copies, waits for them, and re-layouts  2.21 us (2%)
  between operations  1.7 us (1%)
    ppermute x27, starting transfers between devices, swap(): return lax.ppermute(part, 'col', [(i, i ^ code) for i in range(size)])  51.8 us
    all_to_all x2, blocking collectives, swap_all(): return lax.all_to_all(parts, axis, 0, 0)  31 us
    all_to_all x2, starting transfers between devices, swap_all(): return lax.all_to_all(parts, axis, 0, 0)  12.8 us
    pallas_call x2, Pallas kernels, slopes(): pl.pallas_call(functools.partial(slope_kernel, scales, stepped), grid=(ro...  11.6 us
    ppermute x27, waiting for transfers between devices, swap(): return lax.ppermute(part, 'col', [(i, i ^ code) for i in range(size)])  11.1 us
    pallas_call x2, Pallas kernels, second_grad(): pl.pallas_call(functools.partial(second_kernel, scale), grid=(rows // blo...  4.09 us
  transfers between devices with their start and end apart: 29, of which 9 were waited for; matrix products, arithmetic and copies ran while one was open for 2% of the time, Pallas kernels for 4%

profile of v9, /device:TPU:1, one launch (start us, length us, event | category | flops | bytes accessed | tf_op | source)
XLA Modules:
  0.0 131.4 jit_solution(1286613455636111298)
XLA Ops:
  1.4 3.6 %collective-permute-start.1 = (bf16[8,512]{1,0:T(8,128)(2,1)S(1)}, bf16[8,512]{1,0:T(8,128)(2,1)S(1)}, u32[]{:S(2)}, u32[]{:S(2)}) collective-permute-start(bf16[8,512]{1,0:T(8,128)(2,1)S(1)} %convert_element_type.58), channel_id=1, source_target_pairs={{0,8},{1,9},{2,10},{3,11},{4,12},{5,13},{6,14},{7,15},{8,0},{9,1},... | collective-permute-start | bytes 24584 | tf_op jit(solution)/shard_map/ppermute | solution.py:302
  7.2 9.3 %all-to-all-start = ((bf16[16,8,512]{2,1,0:T(8,128)(2,1)}), bf16[16,8,512]{2,1,0:T(8,128)(2,1)S(1)}, u32[]{:S(2)}, u32[]{:S(2)}) async-start(bf16[16,8,512]{2,1,0:T(8,128)(2,1)} %shard_map.130), calls=%async_computation | async-start | bytes 262144 | tf_op jit(solution)/shard_map/all_to_all | solution.py:289
  17.2 2.7 %collective-permute-start.3 = (bf16[4,8,512]{2,1,0:T(8,128)(2,1)S(1)}, bf16[4,8,512]{2,1,0:T(8,128)(2,1)S(1)}, u32[]{:S(2)}, u32[]{:S(2)}) collective-permute-start(bf16[4,8,512]{2,1,0:T(8,128)(2,1)S(1)} %pad_maximum_fusion.4.near_ref), channel_id=1, source_target_pairs={{0,2},{1,3},{2,0},{3,1},{4,6},{5,7},{6,4},{7,5},{8,10},{9,11},{10,... | collective-permute-start | bytes 98312 | tf_op jit(solution)/shard_map/ppermute | solution.py:302
  21.7 2.5 %collective-permute-start.5 = (bf16[4,8,512]{2,1,0:T(8,128)(2,1)S(1)}, bf16[4,8,512]{2,1,0:T(8,128)(2,1)S(1)}, u32[]{:S(2)}, u32[]{:S(2)}) collective-permute-start(bf16[4,8,512]{2,1,0:T(8,128)(2,1)S(1)} %collective-permute-done.3.near_y_ref), channel_id=1, source_target_pairs={{0,1},{1,0},{2,3},{3,2},{4,5},{5,4},{6,7},{7,6},{8,9},{9,8},{10,11... | collective-permute-start | bytes 98312 | tf_op jit(solution)/shard_map/ppermute | solution.py:302
  27.1 6.4 %shard_map.131 = (bf16[12,8,512]{2,1,0:T(8,128)(2,1)S(1)}, bf16[12,8,512]{2,1,0:T(8,128)(2,1)S(1)}, bf16[128,64,128]{2,1,0:T(8,128)(2,1)S(1)}, bf16[16,8,512]{2,1,0:T(8,128)(2,1)S(1)}, bf16[8,8,512]{2,1,0:T(8,128)(2,1)S(1)}) custom-call(s32[1]{0:T(128)S(6)} %add.58.kind_ref, bf16[128,64,128]{2,1,0:T(8,128)(2,1)} %data_ref.3, ...), custom_call_target="tpu_custom_call" | custom-call | flops 4294967296 | bytes 4194304 | tf_op jit(solution)/shard_map/pallas_call | solution.py:137
  36.0 2.7 %collective-permute-start.7 = (bf16[8,8,512]{2,1,0:T(8,128)(2,1)S(1)}, bf16[8,8,512]{2,1,0:T(8,128)(2,1)S(1)}, u32[]{:S(2)}, u32[]{:S(2)}) collective-permute-start(bf16[8,8,512]{2,1,0:T(8,128)(2,1)S(1)} %slice.74), channel_id=1, source_target_pairs={{0,2},{1,3},{2,0},{3,1},{4,6},{5,7},{6,4},{7,5},{8,10},{9,11},{10,... | collective-permute-start | bytes 196616 | tf_op jit(solution)/shard_map/ppermute | solution.py:302
  38.7 2.0 %collective-permute-done.7.got_ref = bf16[8,8,512]{2,1,0:T(8,128)(2,1)S(1)} collective-permute-done((bf16[8,8,512]{2,1,0:T(8,128)(2,1)S(1)}, bf16[8,8,512]{2,1,0:T(8,128)(2,1)S(1)}, u32[]{:S(2)}, u32[]{:S(2)}) %collective-permute-start.7) | collective-permute-done | bytes 65568 | tf_op jit(solution)/shard_map/ppermute | solution.py:302
  42.0 1.8 %collective-permute-start.10 = (bf16[2,8,512]{2,1,0:T(8,128)(2,1)S(1)}, bf16[2,8,512]{2,1,0:T(8,128)(2,1)S(1)}, u32[]{:S(2)}, u32[]{:S(2)}) collective-permute-start(bf16[2,8,512]{2,1,0:T(8,128)(2,1)S(1)} %get-tuple-element.57), channel_id=1, source_target_pairs={{0,12},{1,13},{2,14},{3,15},{4,8},{5,9},{6,10},{7,11},{8,4},{9,5},... | collective-permute-start | bytes 49160 | tf_op jit(solution)/shard_map/ppermute | solution.py:302
  44.5 2.1 %shard_map.133 = bf16[128,512]{1,0:T(8,128)(2,1)S(1)} custom-call(bf16[128,64,128]{2,1,0:T(8,128)(2,1)S(1)} %get-tuple-element.29.slope_ref, bf16[16,8,512]{2,1,0:T(8,128)(2,1)S(1)} %get-tuple-element.30.one_ref, bf16[8,8,512]{2,1,0:T(8,128)(2,1)S(1)} %get-tuple-element.31.three_ref), custom_call_target="tpu_custom_call" | custom-call | flops 2147483648 | bytes 2097152 | tf_op jit(solution)/shard_map/pallas_call | solution.py:198
  47.9 16.5 %all_to_all.20.got_ref = bf16[16,16,512]{2,1,0:T(8,128)(2,1)S(1)} all-to-all(bf16[16,16,512]{2,1,0:T(8,128)(2,1)S(1)} %pad_maximum_fusion), channel_id=1, replica_groups=mesh['row'=16,'col'=16] {'row'}, dimensions={0} | all-to-all | bytes 524288 | tf_op jit(solution)/shard_map/all_to_all | solution.py:289
  68.5 3.5 %all-to-all-start.2 = ((bf16[16,8,512]{2,1,0:T(8,128)(2,1)}), bf16[16,8,512]{2,1,0:T(8,128)(2,1)S(1)}, u32[]{:S(2)}, u32[]{:S(2)}) async-start(bf16[16,8,512]{2,1,0:T(8,128)(2,1)} %get-tuple-element.34), calls=%async_computation.2 | async-start | bytes 262144 | tf_op jit(solution)/shard_map/all_to_all | solution.py:289
  72.1 2.8 %collective-permute-start.14 = (bf16[4,8,512]{2,1,0:T(8,128)(2,1)S(1)}, bf16[4,8,512]{2,1,0:T(8,128)(2,1)S(1)}, u32[]{:S(2)}, u32[]{:S(2)}) collective-permute-start(bf16[4,8,512]{2,1,0:T(8,128)(2,1)S(1)} %get-tuple-element.55.near_ref), channel_id=1, source_target_pairs={{0,2},{1,3},{2,0},{3,1},{4,6},{5,7},{6,4},{7,5},{8,10},{9,11},{10,... | collective-permute-start | bytes 98312 | tf_op jit(solution)/shard_map/ppermute | solution.py:302
  74.8 5.2 %collective-permute-start.15 = (bf16[4,8,512]{2,1,0:T(8,128)(2,1)S(1)}, bf16[4,8,512]{2,1,0:T(8,128)(2,1)S(1)}, u32[]{:S(2)}, u32[]{:S(2)}) collective-permute-start(bf16[4,8,512]{2,1,0:T(8,128)(2,1)S(1)} %get-tuple-element.55.near_ref), channel_id=1, source_target_pairs={{0,1},{1,0},{2,3},{3,2},{4,5},{5,4},{6,7},{7,6},{8,9},{9,8},{10,11... | collective-permute-start | bytes 98312 | tf_op jit(solution)/shard_map/ppermute | solution.py:302
  80.1 2.5 %collective-permute-start.16 = (bf16[4,8,512]{2,1,0:T(8,128)(2,1)S(1)}, bf16[4,8,512]{2,1,0:T(8,128)(2,1)S(1)}, u32[]{:S(2)}, u32[]{:S(2)}) collective-permute-start(bf16[4,8,512]{2,1,0:T(8,128)(2,1)S(1)} %collective-permute-done.14.near_y_ref), channel_id=1, source_target_pairs={{0,1},{1,0},{2,3},{3,2},{4,5},{5,4},{6,7},{7,6},{8,9},{9,8},{10,11... | collective-permute-start | bytes 98312 | tf_op jit(solution)/shard_map/ppermute | solution.py:302
  83.5 5.2 %shard_map.135 = (bf16[12,8,512]{2,1,0:T(8,128)(2,1)S(1)}, bf16[12,8,512]{2,1,0:T(8,128)(2,1)S(1)}, bf16[128,64,128]{2,1,0:T(8,128)(2,1)S(1)}, bf16[16,8,512]{2,1,0:T(8,128)(2,1)S(1)}, bf16[8,8,512]{2,1,0:T(8,128)(2,1)S(1)}) custom-call(s32[1]{0:T(128)S(6)} %add.58.kind_ref, bf16[128,64,128]{2,1,0:T(8,128)(2,1)S(1)} %copy-done.10, ...), custom_call_target="tpu_custom_call" | custom-call | flops 4294967296 | bytes 4194304 | tf_op jit(solution)/shard_map/pallas_call | solution.py:137
  88.7 3.3 %collective-permute-start.18 = (bf16[12,8,512]{2,1,0:T(8,128)(2,1)S(1)}, bf16[12,8,512]{2,1,0:T(8,128)(2,1)S(1)}, u32[]{:S(2)}, u32[]{:S(2)}) collective-permute-start(bf16[12,8,512]{2,1,0:T(8,128)(2,1)S(1)} %get-tuple-element.37), channel_id=1, source_target_pairs={{0,1},{1,0},{2,3},{3,2},{4,5},{5,4},{6,7},{7,6},{8,9},{9,8},{10,11... | collective-permute-start | bytes 294920 | tf_op jit(solution)/shard_map/ppermute | solution.py:302
  92.9 2.7 %collective-permute-start.19 = (bf16[8,8,512]{2,1,0:T(8,128)(2,1)S(1)}, bf16[8,8,512]{2,1,0:T(8,128)(2,1)S(1)}, u32[]{:S(2)}, u32[]{:S(2)}) collective-permute-start(bf16[8,8,512]{2,1,0:T(8,128)(2,1)S(1)} %slice.82), channel_id=1, source_target_pairs={{0,2},{1,3},{2,0},{3,1},{4,6},{5,7},{6,4},{7,5},{8,10},{9,11},{10,... | collective-permute-start | bytes 196616 | tf_op jit(solution)/shard_map/ppermute | solution.py:302
  95.6 2.0 %collective-permute-done.19.got_ref = bf16[8,8,512]{2,1,0:T(8,128)(2,1)S(1)} collective-permute-done((bf16[8,8,512]{2,1,0:T(8,128)(2,1)S(1)}, bf16[8,8,512]{2,1,0:T(8,128)(2,1)S(1)}, u32[]{:S(2)}, u32[]{:S(2)}) %collective-permute-start.19) | collective-permute-done | bytes 65568 | tf_op jit(solution)/shard_map/ppermute | solution.py:302
  98.9 2.1 %collective-permute-start.21 = (bf16[2,8,512]{2,1,0:T(8,128)(2,1)S(1)}, bf16[2,8,512]{2,1,0:T(8,128)(2,1)S(1)}, u32[]{:S(2)}, u32[]{:S(2)}) collective-permute-start(bf16[2,8,512]{2,1,0:T(8,128)(2,1)S(1)} %get-tuple-element.53), channel_id=1, source_target_pairs={{0,8},{1,9},{2,10},{3,11},{4,12},{5,13},{6,14},{7,15},{8,0},{9,1},... | collective-permute-start | bytes 49160 | tf_op jit(solution)/shard_map/ppermute | solution.py:302
  101.0 2.0 %shard_map.137 = bf16[128,512]{1,0:T(8,128)(2,1)S(1)} custom-call(bf16[128,64,128]{2,1,0:T(8,128)(2,1)S(1)} %get-tuple-element.44.slope_ref, bf16[16,8,512]{2,1,0:T(8,128)(2,1)S(1)} %get-tuple-element.45.one_ref, bf16[8,8,512]{2,1,0:T(8,128)(2,1)S(1)} %get-tuple-element.46.three_ref), custom_call_target="tpu_custom_call" | custom-call | flops 2147483648 | bytes 2097152 | tf_op jit(solution)/shard_map/pallas_call | solution.py:198
  103.2 14.5 %all_to_all.21 = bf16[16,16,512]{2,1,0:T(8,128)(2,1)S(1)} all-to-all(bf16[16,16,512]{2,1,0:T(8,128)(2,1)S(1)} %pad_maximum_fusion.1), channel_id=1, replica_groups=mesh['row'=16,'col'=16] {'row'}, dimensions={0} | all-to-all | bytes 524288 | tf_op jit(solution)/shard_map/all_to_all | solution.py:289
  117.7 2.0 %collective-permute-start.25 = (f32[8,512]{1,0:T(8,128)S(1)}, f32[8,512]{1,0:T(8,128)S(1)}, u32[]{:S(2)}, u32[]{:S(2)}) collective-permute-start(f32[8,512]{1,0:T(8,128)S(1)} %get-tuple-element.60), channel_id=1, source_target_pairs={{0,12},{1,13},{2,14},{3,15},{4,8},{5,9},{6,10},{7,11},{8,4},{9,5},... | collective-permute-start | bytes 49160 | tf_op jit(solution)/shard_map/ppermute | solution.py:302
  121.6 2.2 %collective-permute-done.24 = f32[8,512]{1,0:T(8,128)S(1)} collective-permute-done((f32[8,512]{1,0:T(8,128)S(1)}, f32[8,512]{1,0:T(8,128)S(1)}, u32[]{:S(2)}, u32[]{:S(2)}) %collective-permute-start.24) | collective-permute-done | bytes 16416 | tf_op jit(solution)/shard_map/ppermute | solution.py:302
  123.8 6.0 %collective-permute-start.26 = (f32[4,8,512]{2,1,0:T(8,128)S(1)}, f32[4,8,512]{2,1,0:T(8,128)S(1)}, u32[]{:S(2)}, u32[]{:S(2)}) collective-permute-start(f32[4,8,512]{2,1,0:T(8,128)S(1)} %pad_maximum_fusion.3.near_ref), channel_id=1, source_target_pairs={{0,1},{1,0},{2,3},{3,2},{4,5},{5,4},{6,7},{7,6},{8,9},{9,8},{10,11... | collective-permute-start | bytes 196616 | tf_op jit(solution)/shard_map/ppermute | solution.py:302
  (91 shorter events, 24.2 us)
Async XLA Ops:
  1.4 15.9 %collective-permute-start.1 = (bf16[8,512]{1,0:T(8,128)(2,1)S(1)}, bf16[8,512]{1,0:T(8,128)(2,1)S(1)}, u32[]{:S(2)}, u32[]{:S(2)}) collective-permute-start(bf16[8,512]{1,0:T(8,128)(2,1)S(1)} %convert_element_type.58), channel_id=1, source_target_pairs={{0,8},{1,9},{2,10},{3,11},{4,12},{5,13},{6,14},{7,15},{8,0},{9,1},... | collective-permute-start | bytes 24584 | tf_op jit(solution)/shard_map/ppermute | solution.py:302
  4.9 12.3 %collective-permute-start = (bf16[8,512]{1,0:T(8,128)(2,1)S(1)}, bf16[8,512]{1,0:T(8,128)(2,1)S(1)}, u32[]{:S(2)}, u32[]{:S(2)}) collective-permute-start(bf16[8,512]{1,0:T(8,128)(2,1)S(1)} %convert_element_type.58), channel_id=1, source_target_pairs={{0,4},{1,5},{2,6},{3,7},{4,0},{5,1},{6,2},{7,3},{8,12},{9,13},{10,... | collective-permute-start | bytes 24584 | tf_op jit(solution)/shard_map/ppermute | solution.py:302
  5.2 12.0 %collective-permute-start.2 = (bf16[8,512]{1,0:T(8,128)(2,1)S(1)}, bf16[8,512]{1,0:T(8,128)(2,1)S(1)}, u32[]{:S(2)}, u32[]{:S(2)}) collective-permute-start(bf16[8,512]{1,0:T(8,128)(2,1)S(1)} %convert_element_type.58), channel_id=1, source_target_pairs={{0,12},{1,13},{2,14},{3,15},{4,8},{5,9},{6,10},{7,11},{8,4},{9,5},... | collective-permute-start | bytes 24584 | tf_op jit(solution)/shard_map/ppermute | solution.py:302
  7.2 19.0 %all-to-all-start = ((bf16[16,8,512]{2,1,0:T(8,128)(2,1)}), bf16[16,8,512]{2,1,0:T(8,128)(2,1)S(1)}, u32[]{:S(2)}, u32[]{:S(2)}) async-start(bf16[16,8,512]{2,1,0:T(8,128)(2,1)} %shard_map.130), calls=%async_computation | async-start | bytes 262144 | tf_op jit(solution)/shard_map/all_to_all | solution.py:289
  17.2 4.5 %collective-permute-start.3 = (bf16[4,8,512]{2,1,0:T(8,128)(2,1)S(1)}, bf16[4,8,512]{2,1,0:T(8,128)(2,1)S(1)}, u32[]{:S(2)}, u32[]{:S(2)}) collective-permute-start(bf16[4,8,512]{2,1,0:T(8,128)(2,1)S(1)} %pad_maximum_fusion.4.near_ref), channel_id=1, source_target_pairs={{0,2},{1,3},{2,0},{3,1},{4,6},{5,7},{6,4},{7,5},{8,10},{9,11},{10,... | collective-permute-start | bytes 98312 | tf_op jit(solution)/shard_map/ppermute | solution.py:302
  19.9 6.2 %collective-permute-start.4 = (bf16[4,8,512]{2,1,0:T(8,128)(2,1)S(1)}, bf16[4,8,512]{2,1,0:T(8,128)(2,1)S(1)}, u32[]{:S(2)}, u32[]{:S(2)}) collective-permute-start(bf16[4,8,512]{2,1,0:T(8,128)(2,1)S(1)} %pad_maximum_fusion.4.near_ref), channel_id=1, source_target_pairs={{0,1},{1,0},{2,3},{3,2},{4,5},{5,4},{6,7},{7,6},{8,9},{9,8},{10,11... | collective-permute-start | bytes 98312 | tf_op jit(solution)/shard_map/ppermute | solution.py:302
  21.7 4.4 %collective-permute-start.5 = (bf16[4,8,512]{2,1,0:T(8,128)(2,1)S(1)}, bf16[4,8,512]{2,1,0:T(8,128)(2,1)S(1)}, u32[]{:S(2)}, u32[]{:S(2)}) collective-permute-start(bf16[4,8,512]{2,1,0:T(8,128)(2,1)S(1)} %collective-permute-done.3.near_y_ref), channel_id=1, source_target_pairs={{0,1},{1,0},{2,3},{3,2},{4,5},{5,4},{6,7},{7,6},{8,9},{9,8},{10,11... | collective-permute-start | bytes 98312 | tf_op jit(solution)/shard_map/ppermute | solution.py:302
  36.0 4.7 %collective-permute-start.7 = (bf16[8,8,512]{2,1,0:T(8,128)(2,1)S(1)}, bf16[8,8,512]{2,1,0:T(8,128)(2,1)S(1)}, u32[]{:S(2)}, u32[]{:S(2)}) collective-permute-start(bf16[8,8,512]{2,1,0:T(8,128)(2,1)S(1)} %slice.74), channel_id=1, source_target_pairs={{0,2},{1,3},{2,0},{3,1},{4,6},{5,7},{6,4},{7,5},{8,10},{9,11},{10,... | collective-permute-start | bytes 196616 | tf_op jit(solution)/shard_map/ppermute | solution.py:302
  40.7 5.8 %collective-permute-start.8 = (bf16[2,8,512]{2,1,0:T(8,128)(2,1)S(1)}, bf16[2,8,512]{2,1,0:T(8,128)(2,1)S(1)}, u32[]{:S(2)}, u32[]{:S(2)}) collective-permute-start(bf16[2,8,512]{2,1,0:T(8,128)(2,1)S(1)} %get-tuple-element.56), channel_id=1, source_target_pairs={{0,4},{1,5},{2,6},{3,7},{4,0},{5,1},{6,2},{7,3},{8,12},{9,13},{10,... | collective-permute-start | bytes 49160 | tf_op jit(solution)/shard_map/ppermute | solution.py:302
  42.0 4.6 %collective-permute-start.10 = (bf16[2,8,512]{2,1,0:T(8,128)(2,1)S(1)}, bf16[2,8,512]{2,1,0:T(8,128)(2,1)S(1)}, u32[]{:S(2)}, u32[]{:S(2)}) collective-permute-start(bf16[2,8,512]{2,1,0:T(8,128)(2,1)S(1)} %get-tuple-element.57), channel_id=1, source_target_pairs={{0,12},{1,13},{2,14},{3,15},{4,8},{5,9},{6,10},{7,11},{8,4},{9,5},... | collective-permute-start | bytes 49160 | tf_op jit(solution)/shard_map/ppermute | solution.py:302
  43.8 4.1 %collective-permute-start.9 = (bf16[2,8,512]{2,1,0:T(8,128)(2,1)S(1)}, bf16[2,8,512]{2,1,0:T(8,128)(2,1)S(1)}, u32[]{:S(2)}, u32[]{:S(2)}) collective-permute-start(bf16[2,8,512]{2,1,0:T(8,128)(2,1)S(1)} %get-tuple-element.58), channel_id=1, source_target_pairs={{0,8},{1,9},{2,10},{3,11},{4,12},{5,13},{6,14},{7,15},{8,0},{9,1},... | collective-permute-start | bytes 49160 | tf_op jit(solution)/shard_map/ppermute | solution.py:302
  65.2 6.8 %collective-permute-start.13 = (bf16[2,8,512]{2,1,0:T(8,128)(2,1)S(1)}, bf16[2,8,512]{2,1,0:T(8,128)(2,1)S(1)}, u32[]{:S(2)}, u32[]{:S(2)}) collective-permute-start(bf16[2,8,512]{2,1,0:T(8,128)(2,1)S(1)} %get-tuple-element.35), channel_id=1, source_target_pairs={{0,12},{1,13},{2,14},{3,15},{4,8},{5,9},{6,10},{7,11},{8,4},{9,5},... | collective-permute-start | bytes 49160 | tf_op jit(solution)/shard_map/ppermute | solution.py:302
  66.2 5.8 %collective-permute-start.12 = (bf16[2,8,512]{2,1,0:T(8,128)(2,1)S(1)}, bf16[2,8,512]{2,1,0:T(8,128)(2,1)S(1)}, u32[]{:S(2)}, u32[]{:S(2)}) collective-permute-start(bf16[2,8,512]{2,1,0:T(8,128)(2,1)S(1)} %get-tuple-element.35), channel_id=1, source_target_pairs={{0,8},{1,9},{2,10},{3,11},{4,12},{5,13},{6,14},{7,15},{8,0},{9,1},... | collective-permute-start | bytes 49160 | tf_op jit(solution)/shard_map/ppermute | solution.py:302
  67.4 4.7 %collective-permute-start.11 = (bf16[2,8,512]{2,1,0:T(8,128)(2,1)S(1)}, bf16[2,8,512]{2,1,0:T(8,128)(2,1)S(1)}, u32[]{:S(2)}, u32[]{:S(2)}) collective-permute-start(bf16[2,8,512]{2,1,0:T(8,128)(2,1)S(1)} %get-tuple-element.35), channel_id=1, source_target_pairs={{0,4},{1,5},{2,6},{3,7},{4,0},{5,1},{6,2},{7,3},{8,12},{9,13},{10,... | collective-permute-start | bytes 49160 | tf_op jit(solution)/shard_map/ppermute | solution.py:302
  68.5 14.9 %all-to-all-start.2 = ((bf16[16,8,512]{2,1,0:T(8,128)(2,1)}), bf16[16,8,512]{2,1,0:T(8,128)(2,1)S(1)}, u32[]{:S(2)}, u32[]{:S(2)}) async-start(bf16[16,8,512]{2,1,0:T(8,128)(2,1)} %get-tuple-element.34), calls=%async_computation.2 | async-start | bytes 262144 | tf_op jit(solution)/shard_map/all_to_all | solution.py:289
  72.1 8.0 %collective-permute-start.14 = (bf16[4,8,512]{2,1,0:T(8,128)(2,1)S(1)}, bf16[4,8,512]{2,1,0:T(8,128)(2,1)S(1)}, u32[]{:S(2)}, u32[]{:S(2)}) collective-permute-start(bf16[4,8,512]{2,1,0:T(8,128)(2,1)S(1)} %get-tuple-element.55.near_ref), channel_id=1, source_target_pairs={{0,2},{1,3},{2,0},{3,1},{4,6},{5,7},{6,4},{7,5},{8,10},{9,11},{10,... | collective-permute-start | bytes 98312 | tf_op jit(solution)/shard_map/ppermute | solution.py:302
  74.8 7.8 %collective-permute-start.15 = (bf16[4,8,512]{2,1,0:T(8,128)(2,1)S(1)}, bf16[4,8,512]{2,1,0:T(8,128)(2,1)S(1)}, u32[]{:S(2)}, u32[]{:S(2)}) collective-permute-start(bf16[4,8,512]{2,1,0:T(8,128)(2,1)S(1)} %get-tuple-element.55.near_ref), channel_id=1, source_target_pairs={{0,1},{1,0},{2,3},{3,2},{4,5},{5,4},{6,7},{7,6},{8,9},{9,8},{10,11... | collective-permute-start | bytes 98312 | tf_op jit(solution)/shard_map/ppermute | solution.py:302
  88.7 4.2 %collective-permute-start.18 = (bf16[12,8,512]{2,1,0:T(8,128)(2,1)S(1)}, bf16[12,8,512]{2,1,0:T(8,128)(2,1)S(1)}, u32[]{:S(2)}, u32[]{:S(2)}) collective-permute-start(bf16[12,8,512]{2,1,0:T(8,128)(2,1)S(1)} %get-tuple-element.37), channel_id=1, source_target_pairs={{0,1},{1,0},{2,3},{3,2},{4,5},{5,4},{6,7},{7,6},{8,9},{9,8},{10,11... | collective-permute-start | bytes 294920 | tf_op jit(solution)/shard_map/ppermute | solution.py:302
  92.9 4.7 %collective-permute-start.19 = (bf16[8,8,512]{2,1,0:T(8,128)(2,1)S(1)}, bf16[8,8,512]{2,1,0:T(8,128)(2,1)S(1)}, u32[]{:S(2)}, u32[]{:S(2)}) collective-permute-start(bf16[8,8,512]{2,1,0:T(8,128)(2,1)S(1)} %slice.82), channel_id=1, source_target_pairs={{0,2},{1,3},{2,0},{3,1},{4,6},{5,7},{6,4},{7,5},{8,10},{9,11},{10,... | collective-permute-start | bytes 196616 | tf_op jit(solution)/shard_map/ppermute | solution.py:302
  97.7 5.4 %collective-permute-start.20 = (bf16[2,8,512]{2,1,0:T(8,128)(2,1)S(1)}, bf16[2,8,512]{2,1,0:T(8,128)(2,1)S(1)}, u32[]{:S(2)}, u32[]{:S(2)}) collective-permute-start(bf16[2,8,512]{2,1,0:T(8,128)(2,1)S(1)} %get-tuple-element.51), channel_id=1, source_target_pairs={{0,4},{1,5},{2,6},{3,7},{4,0},{5,1},{6,2},{7,3},{8,12},{9,13},{10,... | collective-permute-start | bytes 49160 | tf_op jit(solution)/shard_map/ppermute | solution.py:302
  98.0 5.0 %collective-permute-start.22 = (bf16[2,8,512]{2,1,0:T(8,128)(2,1)S(1)}, bf16[2,8,512]{2,1,0:T(8,128)(2,1)S(1)}, u32[]{:S(2)}, u32[]{:S(2)}) collective-permute-start(bf16[2,8,512]{2,1,0:T(8,128)(2,1)S(1)} %get-tuple-element.52), channel_id=1, source_target_pairs={{0,12},{1,13},{2,14},{3,15},{4,8},{5,9},{6,10},{7,11},{8,4},{9,5},... | collective-permute-start | bytes 49160 | tf_op jit(solution)/shard_map/ppermute | solution.py:302
  98.9 4.2 %collective-permute-start.21 = (bf16[2,8,512]{2,1,0:T(8,128)(2,1)S(1)}, bf16[2,8,512]{2,1,0:T(8,128)(2,1)S(1)}, u32[]{:S(2)}, u32[]{:S(2)}) collective-permute-start(bf16[2,8,512]{2,1,0:T(8,128)(2,1)S(1)} %get-tuple-element.53), channel_id=1, source_target_pairs={{0,8},{1,9},{2,10},{3,11},{4,12},{5,13},{6,14},{7,15},{8,0},{9,1},... | collective-permute-start | bytes 49160 | tf_op jit(solution)/shard_map/ppermute | solution.py:302
  119.7 4.1 %collective-permute-start.24 = (f32[8,512]{1,0:T(8,128)S(1)}, f32[8,512]{1,0:T(8,128)S(1)}, u32[]{:S(2)}, u32[]{:S(2)}) collective-permute-start(f32[8,512]{1,0:T(8,128)S(1)} %get-tuple-element.60), channel_id=1, source_target_pairs={{0,8},{1,9},{2,10},{3,11},{4,12},{5,13},{6,14},{7,15},{8,0},{9,1},... | collective-permute-start | bytes 49160 | tf_op jit(solution)/shard_map/ppermute | solution.py:302
  123.8 6.9 %collective-permute-start.26 = (f32[4,8,512]{2,1,0:T(8,128)S(1)}, f32[4,8,512]{2,1,0:T(8,128)S(1)}, u32[]{:S(2)}, u32[]{:S(2)}) collective-permute-start(f32[4,8,512]{2,1,0:T(8,128)S(1)} %pad_maximum_fusion.3.near_ref), channel_id=1, source_target_pairs={{0,1},{1,0},{2,3},{3,2},{4,5},{5,4},{6,7},{7,6},{8,9},{9,8},{10,11... | collective-permute-start | bytes 196616 | tf_op jit(solution)/shard_map/ppermute | solution.py:302
  (16 other events, 234.1 us)
